TPU v7x, 32 devices: a whole 2x2x4 slice. The times are simulated.
32 devices in a mesh: dp: 16 (over z, y, x), col: 2 (over core).
Axes of the slice: x: 2, y: 2, z: 4, core: 2. Of those that a mesh axis runs over, the one named last changes fastest.
Arguments:
- gradients: bfloat16 [16, 6, 512, 2048], P('dp', None, None, 'col')
- momentum: float32 [6, 512, 2048], P(None, 'dp', 'col'), may hold values from -48 to 48
- master: float32 [6, 512, 2048], P(None, 'dp', 'col'), may hold values from -0.125 to 0.125
- owners: int32 [6], replicated, may hold values from 0 to 15, as said below
Outputs:
- new_weights: bfloat16 [6, 512, 2048], P(None, None, 'col')
- new_master: float32 [6, 512, 2048], P(None, 'dp', 'col')
- new_momentum: float32 [6, 512, 2048], P(None, 'dp', 'col')
- owned_updates: bfloat16 [16, 2, 512, 2048], P('dp', None, None, 'col')
- owned_rms: float32 [16, 2], P('dp')
Inputs may be any that keep to these rules, and one draw needn't show every extreme that they name: `owners`: no owner index appears more than 2 times, and exactly one appears 2 times.
All inputs are finite; a program needn't handle non-finite values.
Results may differ from a plain program's by a relative error of at most 0.04.
Values may be sent and summed in bfloat16 or wider, within the bound.
No kernel may reach another device: no remote copies, remote signals or barrier semaphores. Data moves between devices by JAX's collectives and lax.ppermute only.
A program may use at most 64 MiB of HBM per device.

v0:
```python
import functools
import math

import jax
import jax.numpy as jnp
from jax import lax
from jax.experimental import pallas as pl
from jax.experimental.pallas import tpu as pltpu
from jax.sharding import PartitionSpec as P

KV = 512
D = 2048
MOST = 2

quintic_first = 3.4445
quintic_second = -4.775
quintic_third = 2.0315
momentum_decay = 0.95
learn_rate = 0.3
weight_decay = 0.1
epsilon = 1e-07
factor = 0.2 * math.sqrt(max(KV, D))

VMEM_LIMIT = 56 * 1024 * 1024
LINE = 4


def dot(left, right):
    return jnp.dot(left, right, preferred_element_type=jnp.float32)


def half(value):
    return value.astype(jnp.bfloat16)


def gram_kernel(order_ref, *refs):
    piece_refs, (update_ref, gram_ref) = refs[:-2], refs[-2:]
    start = 0
    for ref in piece_refs:
        rows = ref.shape[1]
        update_ref[0, start : start + rows] = ref[0]
        start += rows
    block = update_ref[0]
    gram = lax.dot_general(
        block, block, (((1,), (1,)), ((), ())), preferred_element_type=jnp.float32
    )
    gram_ref[0] = half(gram)


def grams(pieces, order):
    width = pieces[0].shape[2]
    count = order.shape[0]
    rows = sum(piece.shape[1] for piece in pieces)

    def spec(minor):
        return pl.BlockSpec((1, rows, minor), lambda i, order: (i, 0, 0))

    return pl.pallas_call(
        gram_kernel,
        grid_spec=pltpu.PrefetchScalarGridSpec(
            num_scalar_prefetch=1,
            grid=(count,),
            in_specs=[
                pl.BlockSpec((1, *piece.shape[1:]), lambda i, order: (order[i], 0, 0))
                for piece in pieces
            ],
            out_specs=[spec(width), spec(rows)],
        ),
        out_shape=[
            jax.ShapeDtypeStruct((count, rows, width), jnp.bfloat16),
            jax.ShapeDtypeStruct((count, rows, rows), jnp.bfloat16),
        ],
        compiler_params=pltpu.CompilerParams(vmem_limit_bytes=VMEM_LIMIT),
        cost_estimate=pl.CostEstimate(
            flops=2 * count * rows * rows * width,
            bytes_accessed=2 * count * rows * (2 * width + rows),
            transcendentals=0,
        ),
    )(order, *pieces)


def mixers(grams_now):
    return [
        quintic_second * gram + quintic_third * dot(half(gram), half(gram)) for gram in grams_now
    ]


def next_grams(grams_now, mixes):
    lefts = [
        quintic_first * gram + dot(half(mix), half(gram)) for gram, mix in zip(grams_now, mixes)
    ]
    return [quintic_first * left + dot(half(left), half(mix)) for left, mix in zip(lefts, mixes)]


def chain_kernel(parts, *refs):
    gram_refs = refs[:parts]
    chain_ref, squares_ref = refs[parts:]
    count, rows, _ = chain_ref.shape
    on_diagonal = lax.broadcasted_iota(jnp.int32, (rows, rows), 0) == lax.broadcasted_iota(
        jnp.int32, (rows, rows), 1
    )
    grams_now = []
    inverses = []
    for index in range(count):
        gram = gram_refs[0][index].astype(jnp.float32)
        for ref in gram_refs[1:]:
            gram = gram + ref[index].astype(jnp.float32)
        diagonal = jnp.where(on_diagonal, gram, 0.0)
        squares = jnp.sum(jnp.sum(diagonal, axis=0, keepdims=True), axis=1, keepdims=True)
        squares_ref[index] = jnp.broadcast_to(squares, squares_ref.shape[1:])
        inverse = 1.0 / (jnp.sqrt(squares) + epsilon)
        grams_now.append(gram * inverse * inverse)
        inverses.append(inverse)
    first = mixers(grams_now)
    grams_now = next_grams(grams_now, first)
    second = mixers(grams_now)
    grams_now = next_grams(grams_now, second)
    third = mixers(grams_now)
    pairs = [
        quintic_first * (m0 + m1) + dot(half(m1), half(m0)) for m0, m1 in zip(first, second)
    ]
    cubed = jnp.where(on_diagonal, quintic_first**3, 0.0)
    for index, (pair, m2) in enumerate(zip(pairs, third)):
        whole = quintic_first * pair + quintic_first**2 * m2 + dot(half(m2), half(pair))
        chain_ref[index] = half((cubed + whole) * (factor * inverses[index]))


def chains(gram_parts):
    count, rows, _ = gram_parts[0].shape
    step = 3 if count % 3 == 0 else 1
    parts = len(gram_parts)
    spec = pl.BlockSpec((step, rows, rows), lambda i: (i, 0, 0))
    return pl.pallas_call(
        functools.partial(chain_kernel, parts),
        grid=(count // step,),
        in_specs=[spec] * parts,
        out_specs=[spec, pl.BlockSpec((step, 8, 128), lambda i: (i, 0, 0))],
        out_shape=[
            jax.ShapeDtypeStruct((count, rows, rows), jnp.bfloat16),
            jax.ShapeDtypeStruct((count, 8, 128), jnp.float32),
        ],
        compiler_params=pltpu.CompilerParams(vmem_limit_bytes=VMEM_LIMIT),
        cost_estimate=pl.CostEstimate(
            flops=18 * count * rows * rows * rows,
            bytes_accessed=2 * count * rows * rows * (parts + 1),
            transcendentals=0,
        ),
    )(*gram_parts)


def apply_kernel(sets, first_count, masters, places_ref, spans_ref, slots_ref, order_ref, *refs):
    set_refs = [refs[3 * at : 3 * at + 3] for at in range(sets)]
    master_refs = refs[3 * sets : -6]
    rows_ref, weights_ref, new_rows_ref, owned_ref, rms_ref, scaled_ref = refs[-6:]
    blocks = spans_ref.shape[0]
    height = scaled_ref.shape[0] // blocks
    at = pl.program_id(0)
    matrix = order_ref[at]
    slot = slots_ref[matrix]

    @pl.when(at == 0)
    def _():
        owned_ref[...] = jnp.zeros_like(owned_ref)
        rms_ref[...] = jnp.zeros_like(rms_ref)

    def target(block_at):
        return pl.ds(pl.multiple_of(places_ref[block_at] * height, height), height)

    def span(block_at):
        return pl.ds(pl.multiple_of(spans_ref[block_at] * height, height), height)

    lane = lax.broadcasted_iota(jnp.int32, rms_ref.shape, 1)

    def make(chain_ref, squares_ref, update_ref):
        rms = jnp.sqrt(squares_ref[0, :1, :1] / float(KV * D))
        rms_ref[...] = jnp.where(lane == slot, rms, rms_ref[...])
        scaled_ref[...] = half(dot(chain_ref[0], update_ref[0]))

    for index, chosen in enumerate(set_refs):
        pl.when((at >= first_count) == (index == 1))(functools.partial(make, *chosen))

    decayed = rows_ref[0] * (1.0 - learn_rate * weight_decay)
    new_rows_ref[0] = decayed - learn_rate * scaled_ref[:height].astype(jnp.float32)
    def write(lies):
        for block_at, (piece, where) in enumerate(lies):
            decayed = master_refs[piece][where, 0].astype(jnp.float32) * (
                1.0 - learn_rate * weight_decay
            )
            weights_ref[0, target(block_at)] = half(
                decayed - learn_rate * scaled_ref[span(block_at)].astype(jnp.float32)
            )

    for start, stop, lies in masters:
        pl.when((matrix >= start) & (matrix < stop))(functools.partial(write, lies))

    @pl.when(slot >= 0)
    def _():
        for block_at in range(blocks):
            owned_ref[jnp.maximum(slot, 0), target(block_at)] = scaled_ref[span(block_at)]


def applied(places, spans, slots, order, sets, master_pieces, masters, master):
    _, rows, width = sets[0][2].shape
    count, row_count, _ = master.shape
    first_count = sets[0][0].shape[0]

    def by_matrix(height, minor):
        def index(i, places, spans, slots, order):
            return (order[i], 0, 0)

        return pl.BlockSpec((1, height, minor), index)

    def by_piece(piece, start, depth):
        def index(i, places, spans, slots, order):
            return (0, jnp.clip(order[i] - start, 0, piece.shape[1] - 1), 0, 0)

        return pl.BlockSpec((depth, 1, *piece.shape[2:]), index)

    def by_step(array, start):
        last = array.shape[0] - 1

        def index(i, *_):
            return (jnp.clip(i - start, 0, last), 0, 0)

        return pl.BlockSpec((1, *array.shape[1:]), index)

    owned = (MOST, rows, width)
    return pl.pallas_call(
        functools.partial(apply_kernel, len(sets), first_count, masters),
        grid_spec=pltpu.PrefetchScalarGridSpec(
            num_scalar_prefetch=4,
            grid=(count,),
            in_specs=[
                by_step(array, at * first_count) for at, arrays in enumerate(sets) for array in arrays
            ]
            + [by_piece(*piece) for piece in master_pieces]
            + [by_matrix(row_count, width)],
            out_specs=[
                by_matrix(rows, width),
                by_matrix(row_count, width),
                pl.BlockSpec(owned, lambda i, *_: (0, 0, 0)),
                pl.BlockSpec((1, MOST), lambda i, *_: (0, 0)),
            ],
            scratch_shapes=[pltpu.VMEM((rows, width), jnp.bfloat16)],
        ),
        out_shape=[
            jax.ShapeDtypeStruct((count, rows, width), jnp.bfloat16),
            jax.ShapeDtypeStruct(master.shape, jnp.float32),
            jax.ShapeDtypeStruct(owned, jnp.bfloat16),
            jax.ShapeDtypeStruct((1, MOST), jnp.float32),
        ],
        compiler_params=pltpu.CompilerParams(vmem_limit_bytes=VMEM_LIMIT),
        cost_estimate=pl.CostEstimate(
            flops=2 * count * rows * rows * width,
            bytes_accessed=2 * count * rows * (4 * width + rows),
            transcendentals=0,
        ),
    )(
        places,
        spans,
        slots,
        order,
        *[array for arrays in sets for array in arrays],
        *[piece[0] for piece in master_pieces],
        master,
    )


class Grid:
    def __init__(self, count):
        self.count = count
        self.me = lax.axis_index("dp")
        self.x_pairs = [(d, d ^ 1) for d in range(count)]
        self.y_pairs = [(d, d ^ 2) for d in range(count)]

    def over_x(self, value):
        return lax.ppermute(value, "dp", self.x_pairs)

    def over_y(self, value):
        return lax.ppermute(value, "dp", self.y_pairs)

    def over_z(self, value, shift):
        pairs = [(d, (d // 4 + shift) % LINE * 4 + d % 4) for d in range(self.count)]
        return lax.ppermute(value, "dp", pairs)


def place(me, dx, dy, dz):
    z = ((me >> 2) + dz) & (LINE - 1)
    return z * 4 + ((me & 3) ^ (2 * dy + dx))


def after(value, *others):
    return lax.optimization_barrier((value, *others))[0]


def added(*values):
    return sum(value.astype(jnp.float32) for value in values)


class MasterGather:
    def __init__(self, grid, master):
        self.grid = grid
        self.lines = [[z * 4 + corner for z in range(LINE)] for corner in range(4)]
        self.split = master.shape[0] // 2
        self.own = half(master)
        self.line = lax.all_gather(self.own, "dp", axis_index_groups=self.lines)

    def near(self, *ties):
        line = after(self.line, *ties)
        self.high = line[:, self.split :]
        sent = jnp.concatenate([self.high, self.own[None, : self.split]])
        self.near_x = self.grid.over_x(sent)
        self.near_y = self.grid.over_y(sent)

    def low_plane(self):
        low_x, low_y = self.near_x[LINE], self.near_y[LINE]
        self.plane = jnp.stack([self.own[: self.split], low_y, low_x, self.grid.over_x(low_y)])

    def low_lines(self, *ties):
        low = lax.all_gather(after(self.plane, *ties), "dp", axis_index_groups=self.lines)
        self.low = low.reshape(4 * LINE, *low.shape[2:])

    def high_corners(self, *ties):
        near_y = after(self.near_y, *ties)
        near_x = after(self.near_x, *ties)
        self.far_x = self.grid.over_x(near_y[: LINE // 2])
        self.far_y = self.grid.over_y(near_x[LINE // 2 : LINE])

    def pieces(self):
        high = [self.high, self.near_y, self.near_x, self.far_x, self.far_y]
        depths = [LINE, LINE, LINE, LINE // 2, LINE // 2]
        return [(self.low, 0, 4 * LINE)] + [
            (piece, self.split, depth) for piece, depth in zip(high, depths)
        ]

    def masters(self, matrices):
        low = [(0, z * 4 + at) for at in range(4) for z in range(LINE)]
        high = [(piece, z) for piece in (1, 2, 3) for z in range(LINE)]
        high += [(4 + z // 2, z % 2) for z in range(LINE)]
        return [(0, self.split, low), (self.split, matrices, high)]

    def places(self):
        corner, z_mine = self.grid.me & 3, self.grid.me >> 2
        places = [
            z * 4 + (corner ^ (2 * dy + dx)) for dx in range(2) for dy in range(2) for z in range(LINE)
        ]
        spans = [at * 4 + ((z - z_mine) & (LINE - 1)) for at in range(4) for z in range(LINE)]
        return jnp.stack(places).astype(jnp.int32), jnp.stack(spans).astype(jnp.int32)


def reduce_scatter(grid, terms, row_count, master_gather):
    def term(me, dx, dy, dz):
        start = place(me, dx, dy, dz) * row_count
        return lax.dynamic_slice_in_dim(terms, start, row_count, axis=1)

    me = grid.me
    raw_far1, raw_far2 = term(me, 1, 1, 1), term(me, 1, 1, 2)
    me = after(grid.me, raw_far1, raw_far2, master_gather.own)
    raw_x1, raw_far3, raw_y2 = term(me, 1, 0, 1), term(me, 1, 1, 3), term(me, 0, 1, 2)
    raw_y3, raw_far0, raw_x0 = term(me, 0, 1, 3), term(me, 1, 1, 0), term(me, 1, 0, 0)
    far1 = grid.over_x(raw_far1)
    far2 = grid.over_y(raw_far2)
    along_x1 = grid.over_x(raw_x1)
    far3 = grid.over_y(raw_far3)
    along_y2 = grid.over_y(raw_y2)

    me = after(grid.me, far1, far2, raw_y3)
    sent_x2 = half(added(term(me, 1, 0, 2), far2))
    sent_y1 = half(added(term(me, 0, 1, 1), far1))
    along_x2 = grid.over_x(sent_x2)
    along_y1 = grid.over_y(sent_y1)

    me = after(grid.me, far3, along_x1, sent_x2, sent_y1)
    sent_x3 = half(added(term(me, 1, 0, 3), far3))
    along_x3 = grid.over_x(sent_x3)
    along_y3 = grid.over_y(after(raw_y3, far3, along_x1))

    me = after(grid.me, along_y2, along_x2, sent_x3)
    near2 = half(added(term(me, 0, 0, 2), along_x2, along_y2))
    line2 = grid.over_z(near2, 2)
    far0 = grid.over_x(after(raw_far0, along_x2))

    me = after(grid.me, along_x1, along_y1, along_x3, near2)
    near1 = half(added(term(me, 0, 0, 1), along_x1, along_y1))
    line1 = grid.over_z(near1, 1)
    along_x0 = grid.over_x(after(raw_x0, along_x3))

    me = after(grid.me, along_x3, along_y3, far0, near1)
    near3 = half(added(term(me, 0, 0, 3), along_x3, along_y3))
    sent_y0 = half(added(term(me, 0, 1, 0), far0))
    line3 = grid.over_z(near3, 3)
    master_gather.near(near3, sent_y0)
    along_y0 = grid.over_y(sent_y0)
    me = after(grid.me, near3, sent_y0, line2)
    return added(term(me, 0, 0, 0), along_x0, along_y0, line1, line2, line3)


def all_gather(grid, own, before_z2, before_x2):
    x0, y0 = grid.over_x(own), grid.over_y(own)
    z1, z3 = grid.over_z(own, LINE - 1), grid.over_z(own, 1)
    far0 = grid.over_x(y0)
    x1, y1 = grid.over_x(z1), grid.over_y(z1)
    x3, y3 = grid.over_x(z3), grid.over_y(z3)
    z2 = grid.over_z(after(own, z1, z3, *before_z2), 2)
    far3 = grid.over_y(x3)
    sent = after(z2, before_x2)
    x2, y2 = grid.over_x(sent), grid.over_y(sent)
    far1 = grid.over_x(y1)
    far2 = grid.over_y(x2)
    return [own, z1, z2, z3, y0, y1, y2, y3, x0, x1, x2, x3, far0, far1, far2, far3]


def updated(summed, momentum):
    new_momentum = momentum_decay * momentum + summed
    return new_momentum, half(summed + momentum_decay * new_momentum)


def per_device(gradients, momentum, master, owners):
    me = lax.axis_index("dp")
    dp_count = lax.axis_size("dp")
    matrices, row_count, width = momentum.shape
    terms = gradients[0]
    held = owners == me
    index = jnp.arange(matrices)
    rank = jnp.sum(held[None, :] & (index[None, :] < index[:, None]), axis=1)
    slots = jnp.where(held, rank, -1).astype(jnp.int32)

    in_pieces = dp_count == 4 * LINE and row_count % 32 == 0
    if in_pieces:
        grid = Grid(dp_count)
        rows = master
        master_gather = MasterGather(grid, master)
        places, spans = master_gather.places()
        summed = reduce_scatter(grid, terms, row_count, master_gather)
        new_momentum, own = updated(summed, momentum)
        master_gather.low_plane()
        pieces = all_gather(
            grid, own, (master_gather.near_x, master_gather.near_y), master_gather.plane
        )
        master_gather.low_lines(*pieces[1:4])
        master_gather.high_corners(*pieces[1:])
        master_pieces, masters = master_gather.pieces(), master_gather.masters(matrices)
    else:
        places = spans = jnp.zeros((1,), jnp.int32)
        rows = jnp.zeros((matrices, terms.shape[1], width), jnp.float32)
        rows = lax.dynamic_update_slice_in_dim(rows, master, me * row_count, axis=1)
        summed = lax.psum_scatter(terms, "dp", scatter_dimension=1, tiled=True)
        new_momentum, own = updated(summed.astype(jnp.float32), momentum)
        master_pieces = [(lax.all_gather(half(master), "dp", axis=1, tiled=True)[None], 0, 1)]
        masters = [(0, matrices, [(0, 0)])]
        pieces = [lax.all_gather(own, "dp", axis=1, tiled=True)]

    order = jnp.arange(matrices, dtype=jnp.int32)
    if lax.axis_size("col") == 2 and matrices % 2 == 0:
        size = matrices // 2
        order = (order + lax.axis_index("col") * size) % matrices
        mine, theirs = order[:size], order[size:]
        their_update, their_gram = grams(pieces, theirs)
        swap = [(0, 1), (1, 0)]
        other_part = lax.ppermute(their_gram, "col", swap)
        my_update, my_gram = grams(pieces, mine)
        chain, squares = chains([my_gram, other_part])
        sent = chain
        if in_pieces:
            sent = after(chain, master_gather.far_x, master_gather.far_y)
        other = [lax.ppermute(sent, "col", swap), lax.ppermute(squares, "col", swap)]
        sets = [[chain, squares, my_update], [*other, their_update]]
    else:
        update, gram = grams(pieces, order)
        sets = [[*chains([lax.psum(gram, "col")]), update]]
    new_weights, new_master, owned_updates, rms = applied(
        places, spans, slots, order, sets, master_pieces, masters, rows
    )
    if not in_pieces:
        new_master = lax.dynamic_slice_in_dim(new_master, me * row_count, row_count, axis=1)
    return (new_weights, new_master, new_momentum, owned_updates[None], rms)


def solution(mesh):
    return jax.shard_map(
        per_device,
        mesh=mesh,
        in_specs=(P("dp", None, None, "col"), P(None, "dp", "col"), P(None, "dp", "col"), P()),
        out_specs=(
            P(None, None, "col"),
            P(None, "dp", "col"),
            P(None, "dp", "col"),
            P("dp", None, None, "col"),
            P("dp", None),
        ),
        check_vma=False,
    )
```

profile of v0, /device:TPU:0, one launch (start us, length us, event | category | flops | bytes accessed | tf_op | source)
XLA Modules:
  0.0 216.9 jit_solution(6730817314637197697)
XLA Ops:
  11.3 3.0 %collective-permute-start.3 = (bf16[6,32,1024]{2,1,0:T(8,128)(2,1)}, bf16[6,32,1024]{2,1,0:T(8,128)(2,1)}, u32[]{:S(2)}, u32[]{:S(2)}) collective-permute-start(bf16[6,32,1024]{2,1,0:T(8,128)(2,1)} %get-tuple-element.71), channel_id=1, source_target_pairs={{0,4},{2,6},{4,0},{6,2},{8,12},{10,14},{12,8},{14,10},{16,20},{18,... | collective-permute-start | bytes 1179656 | tf_op jit(solution)/shard_map/ppermute | solution.py:280
  15.8 2.6 %dynamic-slice_bitcast_fusion = (bf16[6,32,1024]{2,1,0:T(8,128)(2,1)}, bf16[6,32,1024]{2,1,0:T(8,128)(2,1)S(1)}, bf16[6,32,1024]{2,1,0:T(8,128)(2,1)S(1)}, bf16[...) fusion(bf16[1,6,512,1024]{3,2,1,0:T(8,128)(2,1)} %param.4, ...), kind=kLoop, calls=%fused_computation.26 | loop fusion | bytes 4718616 | tf_op jit(solution)/shard_map/dynamic_slice | solution.py:354
  21.0 3.6 %collective-permute-done.3 = bf16[6,32,1024]{2,1,0:T(8,128)(2,1)} collective-permute-done((bf16[6,32,1024]{2,1,0:T(8,128)(2,1)}, bf16[6,32,1024]{2,1,0:T(8,128)(2,1)}, u32[]{:S(2)}, u32[]{:S(2)}) %collective-permute-start.3) | collective-permute-done | bytes 393248 | tf_op jit(solution)/shard_map/ppermute | solution.py:280
  24.6 2.1 collective-permute-done.2
  26.7 2.6 %fusion.12 = (bf16[6,32,1024]{2,1,0:T(8,128)(2,1)}, bf16[6,32,1024]{2,1,0:T(8,128)(2,1)}) fusion(bf16[6,32,1024]{2,1,0:T(8,128)(2,1)} %collective-permute-done.2, bf16[1,6,512,1024]{3,2,1,0:T(8,128)(2,1)} %param.4, s32[]{:T(128)S(6)} %select_n.67, bf16[6,32,1024]{2,1,0:T(8,128)(2,1)} %collective-permute-done.3, s32[]{:T(128)S(6)} %select_n.66), kind=kLoop, calls=%fused_computation.21 | loop fusion | flops 1572864 | bytes 2359304 | tf_op jit(solution)/shard_map/convert_element_type | solution.py:33
  31.2 3.8 %collective-permute-done.1 = bf16[6,32,1024]{2,1,0:T(8,128)(2,1)S(1)} collective-permute-done((bf16[6,32,1024]{2,1,0:T(8,128)(2,1)S(1)}, bf16[6,32,1024]{2,1,0:T(8,128)(2,1)S(1)}, u32[]{:S(2)}, u32[]{:S(2)}) %collective-permute-start.1) | collective-permute-done | bytes 393248 | tf_op jit(solution)/shard_map/ppermute | solution.py:277
  39.1 2.2 %collective-permute-done.9 = bf16[6,32,1024]{2,1,0:T(8,128)(2,1)S(1)} collective-permute-done((bf16[6,32,1024]{2,1,0:T(8,128)(2,1)S(1)}, bf16[6,32,1024]{2,1,0:T(8,128)(2,1)S(1)}, u32[]{:S(2)}, u32[]{:S(2)}) %collective-permute-start.9) | collective-permute-done | bytes 393248 | tf_op jit(solution)/shard_map/ppermute | solution.py:280
  41.3 2.2 %collective-permute-done.6 = bf16[6,32,1024]{2,1,0:T(8,128)(2,1)} collective-permute-done((bf16[6,32,1024]{2,1,0:T(8,128)(2,1)}, bf16[6,32,1024]{2,1,0:T(8,128)(2,1)}, u32[]{:S(2)}, u32[]{:S(2)}) %collective-permute-start.6) | collective-permute-done | bytes 393248 | tf_op jit(solution)/shard_map/ppermute | solution.py:277
  47.1 2.6 %collective-permute-start.10 = (bf16[6,32,1024]{2,1,0:T(8,128)(2,1)}, bf16[6,32,1024]{2,1,0:T(8,128)(2,1)S(1)}, u32[]{:S(2)}, u32[]{:S(2)}) collective-permute-start(bf16[6,32,1024]{2,1,0:T(8,128)(2,1)} %fusion.10), channel_id=1, source_target_pairs={{0,16},{2,18},{4,20},{6,22},{8,24},{10,26},{12,28},{14,30},{16,0},... | collective-permute-start | bytes 1179656 | tf_op jit(solution)/shard_map/ppermute | solution.py:284
  51.8 2.1 fusion.8
  57.3 2.9 %collective-permute-done.7 = bf16[6,32,1024]{2,1,0:T(8,128)(2,1)S(1)} collective-permute-done((bf16[6,32,1024]{2,1,0:T(8,128)(2,1)S(1)}, bf16[6,32,1024]{2,1,0:T(8,128)(2,1)S(1)}, u32[]{:S(2)}, u32[]{:S(2)}) %collective-permute-start.7) | collective-permute-done | bytes 393248 | tf_op jit(solution)/shard_map/ppermute | solution.py:277
  60.3 2.3 %fusion.4 = (bf16[6,32,1024]{2,1,0:T(8,128)(2,1)}, bf16[6,32,1024]{2,1,0:T(8,128)(2,1)}) fusion(bf16[6,32,1024]{2,1,0:T(8,128)(2,1)S(1)} %collective-permute-done.7, bf16[1,6,512,1024]{3,2,1,0:T(8,128)(2,1)} %param.4, s32[]{:T(128)S(6)} %select_n.74, bf16[6,32,1024]{2,1,0:T(8,128)(2,1)S(1)} %collective-permute-done.5, ...), kind=kLoop, calls=%fused_computation.8 | loop fusion | flops 1966080 | bytes 2752520 | tf_op jit(solution)/shard_map/convert_element_type | solution.py:33
  62.7 4.0 %collective-permute-start.14 = (bf16[6,32,1024]{2,1,0:T(8,128)(2,1)}, bf16[6,32,1024]{2,1,0:T(8,128)(2,1)}, u32[]{:S(2)}, u32[]{:S(2)}) collective-permute-start(bf16[6,32,1024]{2,1,0:T(8,128)(2,1)} %get-tuple-element.68), channel_id=1, source_target_pairs={{0,24},{2,26},{4,28},{6,30},{8,0},{10,2},{12,4},{14,6},{16,8},{18,... | collective-permute-start | bytes 1179656 | tf_op jit(solution)/shard_map/ppermute | solution.py:284
  69.1 6.0 %collective-permute-done.10 = bf16[6,32,1024]{2,1,0:T(8,128)(2,1)S(1)} collective-permute-done((bf16[6,32,1024]{2,1,0:T(8,128)(2,1)}, bf16[6,32,1024]{2,1,0:T(8,128)(2,1)S(1)}, u32[]{:S(2)}, u32[]{:S(2)}) %collective-permute-start.10) | collective-permute-done | bytes 393248 | tf_op jit(solution)/shard_map/ppermute | solution.py:284
  77.6 5.2 %collective-permute-done.14 = bf16[6,32,1024]{2,1,0:T(8,128)(2,1)} collective-permute-done((bf16[6,32,1024]{2,1,0:T(8,128)(2,1)}, bf16[6,32,1024]{2,1,0:T(8,128)(2,1)}, u32[]{:S(2)}, u32[]{:S(2)}) %collective-permute-start.14) | collective-permute-done | bytes 393248 | tf_op jit(solution)/shard_map/ppermute | solution.py:284
  82.8 3.2 %add_convert_fusion = (bf16[6,32,1024]{2,1,0:T(8,128)(2,1)S(1)}, f32[6,32,1024]{2,1,0:T(8,128)}) fusion(f32[6,32,1024]{2,1,0:T(8,128)} %param.5, bf16[6,32,1024]{2,1,0:T(8,128)(2,1)} %collective-permute-done.14, bf16[6,32,1024]{2,1,0:T(8,128)(2,1)} %copy-done.7, bf16[6,32,1024]{2,1,0:T(8,128)(2,1)} %collective-permute-done.13, ...), kind=kLoop, calls=%fused_computation.24 | loop fusion | flops 3145728 | bytes 4325380 | tf_op jit(solution)/shard_map/convert_element_type | solution.py:33
  86.7 3.2 %collective-permute-start.15 = (bf16[6,32,1024]{2,1,0:T(8,128)(2,1)S(1)}, bf16[6,32,1024]{2,1,0:T(8,128)(2,1)S(1)}, u32[]{:S(2)}, u32[]{:S(2)}) collective-permute-start(bf16[6,32,1024]{2,1,0:T(8,128)(2,1)S(1)} %get-tuple-element.43.refs_0_), channel_id=1, source_target_pairs={{0,24},{2,26},{4,28},{6,30},{8,0},{10,2},{12,4},{14,6},{16,8},{18,... | collective-permute-start | bytes 1179656 | tf_op jit(solution)/shard_map/ppermute | solution.py:284
  91.3 8.6 %collective-permute-done.16.refs_3_ = bf16[6,32,1024]{2,1,0:T(8,128)(2,1)} collective-permute-done((bf16[6,32,1024]{2,1,0:T(8,128)(2,1)S(1)}, bf16[6,32,1024]{2,1,0:T(8,128)(2,1)}, u32[]{:S(2)}, u32[]{:S(2)}) %collective-permute-start.16) | collective-permute-done | bytes 393248 | tf_op jit(solution)/shard_map/ppermute | solution.py:284
  101.5 4.2 %collective-permute-done.15.refs_1_ = bf16[6,32,1024]{2,1,0:T(8,128)(2,1)S(1)} collective-permute-done((bf16[6,32,1024]{2,1,0:T(8,128)(2,1)S(1)}, bf16[6,32,1024]{2,1,0:T(8,128)(2,1)S(1)}, u32[]{:S(2)}, u32[]{:S(2)}) %collective-permute-start.15) | collective-permute-done | bytes 393248 | tf_op jit(solution)/shard_map/ppermute | solution.py:284
  106.4 2.9 %collective-permute-start.19 = (bf16[6,32,1024]{2,1,0:T(8,128)(2,1)S(1)}, bf16[6,32,1024]{2,1,0:T(8,128)(2,1)}, u32[]{:S(2)}, u32[]{:S(2)}) collective-permute-start(bf16[6,32,1024]{2,1,0:T(8,128)(2,1)S(1)} %get-tuple-element.43.refs_0_), channel_id=1, source_target_pairs={{0,16},{2,18},{4,20},{6,22},{8,24},{10,26},{12,28},{14,30},{16,0},... | collective-permute-start | bytes 1179656 | tf_op jit(solution)/shard_map/ppermute | solution.py:284
  112.4 4.8 %collective-permute-done.22 = bf16[3,32,1024]{2,1,0:T(8,128)(2,1)S(1)} collective-permute-done((bf16[3,32,1024]{2,1,0:T(8,128)(2,1)S(1)}, bf16[3,32,1024]{2,1,0:T(8,128)(2,1)S(1)}, u32[]{:S(2)}, u32[]{:S(2)}) %collective-permute-start.22) | collective-permute-done | bytes 196640 | tf_op jit(solution)/shard_map/ppermute | solution.py:277
  119.1 6.7 %collective-permute-done.19.refs_2_ = bf16[6,32,1024]{2,1,0:T(8,128)(2,1)} collective-permute-done((bf16[6,32,1024]{2,1,0:T(8,128)(2,1)S(1)}, bf16[6,32,1024]{2,1,0:T(8,128)(2,1)}, u32[]{:S(2)}, u32[]{:S(2)}) %collective-permute-start.19) | collective-permute-done | bytes 393248 | tf_op jit(solution)/shard_map/ppermute | solution.py:284
  128.6 5.0 %collective-permute-done.29.refs_12_ = bf16[6,32,1024]{2,1,0:T(8,128)(2,1)} collective-permute-done((bf16[6,32,1024]{2,1,0:T(8,128)(2,1)}, bf16[6,32,1024]{2,1,0:T(8,128)(2,1)}, u32[]{:S(2)}, u32[]{:S(2)}) %collective-permute-start.29) | collective-permute-done | bytes 393248 | tf_op jit(solution)/shard_map/ppermute | solution.py:277
  136.9 2.7 %collective-permute-start.30 = (bf16[6,32,1024]{2,1,0:T(8,128)(2,1)}, bf16[6,32,1024]{2,1,0:T(8,128)(2,1)}, u32[]{:S(2)}, u32[]{:S(2)}) collective-permute-start(bf16[6,32,1024]{2,1,0:T(8,128)(2,1)} %collective-permute-done.21.refs_5_), channel_id=1, source_target_pairs={{0,2},{2,0},{4,6},{6,4},{8,10},{10,8},{12,14},{14,12},{16,18},{18,... | collective-permute-start | bytes 1179656 | tf_op jit(solution)/shard_map/ppermute | solution.py:277
  144.1 6.4 %collective-permute-done.26.refs_9_ = bf16[6,32,1024]{2,1,0:T(8,128)(2,1)} collective-permute-done((bf16[6,32,1024]{2,1,0:T(8,128)(2,1)}, bf16[6,32,1024]{2,1,0:T(8,128)(2,1)}, u32[]{:S(2)}, u32[]{:S(2)}) %collective-permute-start.26) | collective-permute-done | bytes 393248 | tf_op jit(solution)/shard_map/ppermute | solution.py:277
  150.5 6.3 %collective-permute-done.30.refs_13_ = bf16[6,32,1024]{2,1,0:T(8,128)(2,1)} collective-permute-done((bf16[6,32,1024]{2,1,0:T(8,128)(2,1)}, bf16[6,32,1024]{2,1,0:T(8,128)(2,1)}, u32[]{:S(2)}, u32[]{:S(2)}) %collective-permute-start.30) | collective-permute-done | bytes 393248 | tf_op jit(solution)/shard_map/ppermute | solution.py:277
  156.8 3.8 %collective-permute-done.31.refs_14_ = bf16[6,32,1024]{2,1,0:T(8,128)(2,1)} collective-permute-done((bf16[6,32,1024]{2,1,0:T(8,128)(2,1)}, bf16[6,32,1024]{2,1,0:T(8,128)(2,1)}, u32[]{:S(2)}, u32[]{:S(2)}) %collective-permute-start.31) | collective-permute-done | bytes 393248 | tf_op jit(solution)/shard_map/ppermute | solution.py:280
  160.6 6.1 %shard_map.84 = (bf16[3,512,1024]{2,1,0:T(8,128)(2,1)}, bf16[3,512,512]{2,1,0:T(8,128)(2,1)}) custom-call(s32[3]{0:T(128)} %get-tuple-element.75.order_ref, bf16[6,32,1024]{2,1,0:T(8,128)(2,1)} %copy-done.1, bf16[6,32,1024]{2,1,0:T(8,128)(2,1)} %copy-done.6, bf16[6,32,1024]{2,1,0:T(8,128)(2,1)} %collective-permute-done.19.refs_2_, ...), custom_call_target="tpu_custom_call" | custom-call | flops 1610612736 | bytes 7864320 | tf_op jit(solution)/shard_map/pallas_call | solution.py:58
  168.5 2.9 %collective-permute-start.34 = (bf16[2,3,32,1024]{3,2,1,0:T(8,128)(2,1)S(1)}, bf16[2,3,32,1024]{3,2,1,0:T(8,128)(2,1)S(1)}, u32[]{:S(2)}, u32[]{:S(2)}) collective-permute-start(bf16[2,3,32,1024]{3,2,1,0:T(8,128)(2,1)S(1)} %slice.31), channel_id=1, source_target_pairs={{0,2},{2,0},{4,6},{6,4},{8,10},{10,8},{12,14},{14,12},{16,18},{18,... | collective-permute-start | bytes 1179656 | tf_op jit(solution)/shard_map/ppermute | solution.py:277
  171.4 5.9 %shard_map.83 = (bf16[3,512,1024]{2,1,0:T(8,128)(2,1)}, bf16[3,512,512]{2,1,0:T(8,128)(2,1)}) custom-call(s32[3]{0:T(128)} %get-tuple-element.76.order_ref, bf16[6,32,1024]{2,1,0:T(8,128)(2,1)} %copy-done.1, bf16[6,32,1024]{2,1,0:T(8,128)(2,1)} %copy-done.6, bf16[6,32,1024]{2,1,0:T(8,128)(2,1)} %collective-permute-done.19.refs_2_, ...), custom_call_target="tpu_custom_call" | custom-call | flops 1610612736 | bytes 7864320 | tf_op jit(solution)/shard_map/pallas_call | solution.py:58
  178.5 12.3 %shard_map.85 = (bf16[3,512,512]{2,1,0:T(8,128)(2,1)}, f32[3,8,128]{2,1,0:T(8,128)}) custom-call(bf16[3,512,512]{2,1,0:T(8,128)(2,1)} %get-tuple-element.45.refs_0_, bf16[3,512,512]{2,1,0:T(8,128)(2,1)} %copy-done.13), custom_call_target="tpu_custom_call" | custom-call | flops 7247757312 | bytes 4718592 | tf_op jit(solution)/shard_map/pallas_call | solution.py:133
  195.7 14.3 %shard_map.86 = (bf16[6,512,1024]{2,1,0:T(8,128)(2,1)}, f32[6,32,1024]{2,1,0:T(8,128)}, bf16[2,512,1024]{2,1,0:T(8,128)(2,1)}, f32[1,2]{1,0:T(1,128)}) custom-call(s32[16]{0:T(128)} %stack.125.places_ref, s32[16]{0:T(128)} %stack.142.spans_ref, s32[6]{0:T(128)} %broadcast_select_fusion.slots_ref, s32[6]{0:T(128)} %copy-done.11, ...), custom_call_target="tpu_custom_call" | custom-call | flops 3221225472 | bytes 28311552 | tf_op jit(solution)/shard_map/pallas_call | solution.py:228
  (106 shorter events, 56.1 us)
Async XLA Ops:
  7.2 59.5 %all-gather.5.cloned.1.call-start = ((), (), s32[]{:S(2)}) async-start(), calls=%async_computation | async-start | bytes 1966080 | tf_op jit(solution)/shard_map/all_gather | solution.py:306
  9.2 185.3 %all-gather.7.cloned.1.call-start = ((), (), s32[]{:S(2)}) async-start(), calls=%async_computation.1 | async-start | bytes 3932160 | tf_op jit(solution)/shard_map/all_gather | solution.py:320
  18.4 16.5 %collective-permute-start.1 = (bf16[6,32,1024]{2,1,0:T(8,128)(2,1)S(1)}, bf16[6,32,1024]{2,1,0:T(8,128)(2,1)S(1)}, u32[]{:S(2)}, u32[]{:S(2)}) collective-permute-start(bf16[6,32,1024]{2,1,0:T(8,128)(2,1)S(1)} %get-tuple-element.65), channel_id=1, source_target_pairs={{0,2},{2,0},{4,6},{6,4},{8,10},{10,8},{12,14},{14,12},{16,18},{18,... | collective-permute-start | bytes 1179656 | tf_op jit(solution)/shard_map/ppermute | solution.py:277
  19.0 16.0 %collective-permute-start = (bf16[6,32,1024]{2,1,0:T(8,128)(2,1)S(1)}, bf16[6,32,1024]{2,1,0:T(8,128)(2,1)}, u32[]{:S(2)}, u32[]{:S(2)}) collective-permute-start(bf16[6,32,1024]{2,1,0:T(8,128)(2,1)S(1)} %get-tuple-element.66), channel_id=1, source_target_pairs={{0,4},{2,6},{4,0},{6,2},{8,12},{10,14},{12,8},{14,10},{16,20},{18,... | collective-permute-start | bytes 1179656 | tf_op jit(solution)/shard_map/ppermute | solution.py:280
  19.0 22.3 %collective-permute-start.9 = (bf16[6,32,1024]{2,1,0:T(8,128)(2,1)S(1)}, bf16[6,32,1024]{2,1,0:T(8,128)(2,1)S(1)}, u32[]{:S(2)}, u32[]{:S(2)}) collective-permute-start(bf16[6,32,1024]{2,1,0:T(8,128)(2,1)S(1)} %get-tuple-element.62), channel_id=1, source_target_pairs={{0,4},{2,6},{4,0},{6,2},{8,12},{10,14},{12,8},{14,10},{16,20},{18,... | collective-permute-start | bytes 1179656 | tf_op jit(solution)/shard_map/ppermute | solution.py:280
  29.2 20.6 %collective-permute-start.8 = (bf16[6,32,1024]{2,1,0:T(8,128)(2,1)}, bf16[6,32,1024]{2,1,0:T(8,128)(2,1)}, u32[]{:S(2)}, u32[]{:S(2)}) collective-permute-start(bf16[6,32,1024]{2,1,0:T(8,128)(2,1)} %get-tuple-element.69), channel_id=1, source_target_pairs={{0,4},{2,6},{4,0},{6,2},{8,12},{10,14},{12,8},{14,10},{16,20},{18,... | collective-permute-start | bytes 1179656 | tf_op jit(solution)/shard_map/ppermute | solution.py:280
  29.2 14.3 %collective-permute-start.6 = (bf16[6,32,1024]{2,1,0:T(8,128)(2,1)}, bf16[6,32,1024]{2,1,0:T(8,128)(2,1)}, u32[]{:S(2)}, u32[]{:S(2)}) collective-permute-start(bf16[6,32,1024]{2,1,0:T(8,128)(2,1)} %get-tuple-element.70), channel_id=1, source_target_pairs={{0,2},{2,0},{4,6},{6,4},{8,10},{10,8},{12,14},{14,12},{16,18},{18,... | collective-permute-start | bytes 1179656 | tf_op jit(solution)/shard_map/ppermute | solution.py:277
  37.0 14.8 %collective-permute-start.4 = (bf16[6,32,1024]{2,1,0:T(8,128)(2,1)}, bf16[6,32,1024]{2,1,0:T(8,128)(2,1)S(1)}, u32[]{:S(2)}, u32[]{:S(2)}) collective-permute-start(bf16[6,32,1024]{2,1,0:T(8,128)(2,1)} %fusion.11), channel_id=1, source_target_pairs={{0,2},{2,0},{4,6},{6,4},{8,10},{10,8},{12,14},{14,12},{16,18},{18,... | collective-permute-start | bytes 1179656 | tf_op jit(solution)/shard_map/ppermute | solution.py:277
  38.5 18.8 %collective-permute-start.5 = (bf16[6,32,1024]{2,1,0:T(8,128)(2,1)S(1)}, bf16[6,32,1024]{2,1,0:T(8,128)(2,1)S(1)}, u32[]{:S(2)}, u32[]{:S(2)}) collective-permute-start(bf16[6,32,1024]{2,1,0:T(8,128)(2,1)S(1)} %get-tuple-element.35), channel_id=1, source_target_pairs={{0,4},{2,6},{4,0},{6,2},{8,12},{10,14},{12,8},{14,10},{16,20},{18,... | collective-permute-start | bytes 1179656 | tf_op jit(solution)/shard_map/ppermute | solution.py:280
  43.5 16.7 %collective-permute-start.7 = (bf16[6,32,1024]{2,1,0:T(8,128)(2,1)S(1)}, bf16[6,32,1024]{2,1,0:T(8,128)(2,1)S(1)}, u32[]{:S(2)}, u32[]{:S(2)}) collective-permute-start(bf16[6,32,1024]{2,1,0:T(8,128)(2,1)S(1)} %get-tuple-element.36), channel_id=1, source_target_pairs={{0,2},{2,0},{4,6},{6,4},{8,10},{10,8},{12,14},{14,12},{16,18},{18,... | collective-permute-start | bytes 1179656 | tf_op jit(solution)/shard_map/ppermute | solution.py:277
  47.1 28.0 %collective-permute-start.10 = (bf16[6,32,1024]{2,1,0:T(8,128)(2,1)}, bf16[6,32,1024]{2,1,0:T(8,128)(2,1)S(1)}, u32[]{:S(2)}, u32[]{:S(2)}) collective-permute-start(bf16[6,32,1024]{2,1,0:T(8,128)(2,1)} %fusion.10), channel_id=1, source_target_pairs={{0,16},{2,18},{4,20},{6,22},{8,24},{10,26},{12,28},{14,30},{16,0},... | collective-permute-start | bytes 1179656 | tf_op jit(solution)/shard_map/ppermute | solution.py:284
  53.9 22.7 %collective-permute-start.13 = (bf16[6,32,1024]{2,1,0:T(8,128)(2,1)}, bf16[6,32,1024]{2,1,0:T(8,128)(2,1)}, u32[]{:S(2)}, u32[]{:S(2)}) collective-permute-start(bf16[6,32,1024]{2,1,0:T(8,128)(2,1)} %fusion.8), channel_id=1, source_target_pairs={{0,8},{2,10},{4,12},{6,14},{8,16},{10,18},{12,20},{14,22},{16,24},... | collective-permute-start | bytes 1179656 | tf_op jit(solution)/shard_map/ppermute | solution.py:284
  55.5 22.1 %collective-permute-start.11 = (bf16[6,32,1024]{2,1,0:T(8,128)(2,1)}, bf16[6,32,1024]{2,1,0:T(8,128)(2,1)}, u32[]{:S(2)}, u32[]{:S(2)}) collective-permute-start(bf16[6,32,1024]{2,1,0:T(8,128)(2,1)} %get-tuple-element.41), channel_id=1, source_target_pairs={{0,2},{2,0},{4,6},{6,4},{8,10},{10,8},{12,14},{14,12},{16,18},{18,... | collective-permute-start | bytes 1179656 | tf_op jit(solution)/shard_map/ppermute | solution.py:277
  62.6 15.0 %collective-permute-start.12 = (bf16[6,32,1024]{2,1,0:T(8,128)(2,1)}, bf16[6,32,1024]{2,1,0:T(8,128)(2,1)}, u32[]{:S(2)}, u32[]{:S(2)}) collective-permute-start(bf16[6,32,1024]{2,1,0:T(8,128)(2,1)} %get-tuple-element.67), channel_id=1, source_target_pairs={{0,4},{2,6},{4,0},{6,2},{8,12},{10,14},{12,8},{14,10},{16,20},{18,... | collective-permute-start | bytes 1179656 | tf_op jit(solution)/shard_map/ppermute | solution.py:280
  62.7 20.1 %collective-permute-start.14 = (bf16[6,32,1024]{2,1,0:T(8,128)(2,1)}, bf16[6,32,1024]{2,1,0:T(8,128)(2,1)}, u32[]{:S(2)}, u32[]{:S(2)}) collective-permute-start(bf16[6,32,1024]{2,1,0:T(8,128)(2,1)} %get-tuple-element.68), channel_id=1, source_target_pairs={{0,24},{2,26},{4,28},{6,30},{8,0},{10,2},{12,4},{14,6},{16,8},{18,... | collective-permute-start | bytes 1179656 | tf_op jit(solution)/shard_map/ppermute | solution.py:284
  75.1 30.5 %collective-permute-start.18 = (bf16[5,3,32,1024]{3,2,1,0:T(8,128)(2,1)}, bf16[5,3,32,1024]{3,2,1,0:T(8,128)(2,1)S(1)}, u32[]{:S(2)}, u32[]{:S(2)}) collective-permute-start(bf16[5,3,32,1024]{3,2,1,0:T(8,128)(2,1)} %pad_maximum_fusion), channel_id=1, source_target_pairs={{0,4},{2,6},{4,0},{6,2},{8,12},{10,14},{12,8},{14,10},{16,20},{18,... | collective-permute-start | bytes 2949128 | tf_op jit(solution)/shard_map/ppermute | solution.py:280
  76.6 29.0 %collective-permute-start.17 = (bf16[5,3,32,1024]{3,2,1,0:T(8,128)(2,1)}, bf16[5,3,32,1024]{3,2,1,0:T(8,128)(2,1)S(1)}, u32[]{:S(2)}, u32[]{:S(2)}) collective-permute-start(bf16[5,3,32,1024]{3,2,1,0:T(8,128)(2,1)} %pad_maximum_fusion), channel_id=1, source_target_pairs={{0,2},{2,0},{4,6},{6,4},{8,10},{10,8},{12,14},{14,12},{16,18},{18,... | collective-permute-start | bytes 2949128 | tf_op jit(solution)/shard_map/ppermute | solution.py:277
  86.0 13.9 %collective-permute-start.16 = (bf16[6,32,1024]{2,1,0:T(8,128)(2,1)S(1)}, bf16[6,32,1024]{2,1,0:T(8,128)(2,1)}, u32[]{:S(2)}, u32[]{:S(2)}) collective-permute-start(bf16[6,32,1024]{2,1,0:T(8,128)(2,1)S(1)} %get-tuple-element.43.refs_0_), channel_id=1, source_target_pairs={{0,8},{2,10},{4,12},{6,14},{8,16},{10,18},{12,20},{14,22},{16,24},... | collective-permute-start | bytes 1179656 | tf_op jit(solution)/shard_map/ppermute | solution.py:284
  86.7 19.0 %collective-permute-start.15 = (bf16[6,32,1024]{2,1,0:T(8,128)(2,1)S(1)}, bf16[6,32,1024]{2,1,0:T(8,128)(2,1)S(1)}, u32[]{:S(2)}, u32[]{:S(2)}) collective-permute-start(bf16[6,32,1024]{2,1,0:T(8,128)(2,1)S(1)} %get-tuple-element.43.refs_0_), channel_id=1, source_target_pairs={{0,24},{2,26},{4,28},{6,30},{8,0},{10,2},{12,4},{14,6},{16,8},{18,... | collective-permute-start | bytes 1179656 | tf_op jit(solution)/shard_map/ppermute | solution.py:284
  89.9 37.3 %collective-permute-start.25 = (bf16[6,32,1024]{2,1,0:T(8,128)(2,1)S(1)}, bf16[6,32,1024]{2,1,0:T(8,128)(2,1)}, u32[]{:S(2)}, u32[]{:S(2)}) collective-permute-start(bf16[6,32,1024]{2,1,0:T(8,128)(2,1)S(1)} %get-tuple-element.43.refs_0_), channel_id=1, source_target_pairs={{0,2},{2,0},{4,6},{6,4},{8,10},{10,8},{12,14},{14,12},{16,18},{18,... | collective-permute-start | bytes 1179656 | tf_op jit(solution)/shard_map/ppermute | solution.py:277
  106.4 19.4 %collective-permute-start.19 = (bf16[6,32,1024]{2,1,0:T(8,128)(2,1)S(1)}, bf16[6,32,1024]{2,1,0:T(8,128)(2,1)}, u32[]{:S(2)}, u32[]{:S(2)}) collective-permute-start(bf16[6,32,1024]{2,1,0:T(8,128)(2,1)S(1)} %get-tuple-element.43.refs_0_), channel_id=1, source_target_pairs={{0,16},{2,18},{4,20},{6,22},{8,24},{10,26},{12,28},{14,30},{16,0},... | collective-permute-start | bytes 1179656 | tf_op jit(solution)/shard_map/ppermute | solution.py:284
  110.2 24.6 %collective-permute-start.28 = (bf16[6,32,1024]{2,1,0:T(8,128)(2,1)}, bf16[6,32,1024]{2,1,0:T(8,128)(2,1)}, u32[]{:S(2)}, u32[]{:S(2)}) collective-permute-start(bf16[6,32,1024]{2,1,0:T(8,128)(2,1)} %collective-permute-done.16.refs_3_), channel_id=1, source_target_pairs={{0,2},{2,0},{4,6},{6,4},{8,10},{10,8},{12,14},{14,12},{16,18},{18,... | collective-permute-start | bytes 1179656 | tf_op jit(solution)/shard_map/ppermute | solution.py:277
  111.4 28.2 %collective-permute-start.24 = (bf16[6,32,1024]{2,1,0:T(8,128)(2,1)}, bf16[6,32,1024]{2,1,0:T(8,128)(2,1)}, u32[]{:S(2)}, u32[]{:S(2)}) collective-permute-start(bf16[6,32,1024]{2,1,0:T(8,128)(2,1)} %collective-permute-done.16.refs_3_), channel_id=1, source_target_pairs={{0,4},{2,6},{4,0},{6,2},{8,12},{10,14},{12,8},{14,10},{16,20},{18,... | collective-permute-start | bytes 1179656 | tf_op jit(solution)/shard_map/ppermute | solution.py:280
  117.2 16.4 %collective-permute-start.29 = (bf16[6,32,1024]{2,1,0:T(8,128)(2,1)}, bf16[6,32,1024]{2,1,0:T(8,128)(2,1)}, u32[]{:S(2)}, u32[]{:S(2)}) collective-permute-start(bf16[6,32,1024]{2,1,0:T(8,128)(2,1)} %collective-permute-done.20.refs_4_), channel_id=1, source_target_pairs={{0,2},{2,0},{4,6},{6,4},{8,10},{10,8},{12,14},{14,12},{16,18},{18,... | collective-permute-start | bytes 1179656 | tf_op jit(solution)/shard_map/ppermute | solution.py:277
  127.2 14.9 %collective-permute-start.27 = (bf16[6,32,1024]{2,1,0:T(8,128)(2,1)}, bf16[6,32,1024]{2,1,0:T(8,128)(2,1)}, u32[]{:S(2)}, u32[]{:S(2)}) collective-permute-start(bf16[6,32,1024]{2,1,0:T(8,128)(2,1)} %collective-permute-done.19.refs_2_), channel_id=1, source_target_pairs={{0,2},{2,0},{4,6},{6,4},{8,10},{10,8},{12,14},{14,12},{16,18},{18,... | collective-permute-start | bytes 1179656 | tf_op jit(solution)/shard_map/ppermute | solution.py:277
  133.6 16.9 %collective-permute-start.26 = (bf16[6,32,1024]{2,1,0:T(8,128)(2,1)}, bf16[6,32,1024]{2,1,0:T(8,128)(2,1)}, u32[]{:S(2)}, u32[]{:S(2)}) collective-permute-start(bf16[6,32,1024]{2,1,0:T(8,128)(2,1)} %copy-done.6), channel_id=1, source_target_pairs={{0,2},{2,0},{4,6},{6,4},{8,10},{10,8},{12,14},{14,12},{16,18},{18,... | collective-permute-start | bytes 1179656 | tf_op jit(solution)/shard_map/ppermute | solution.py:277
  134.8 15.7 %collective-permute-start.32 = (bf16[6,32,1024]{2,1,0:T(8,128)(2,1)}, bf16[6,32,1024]{2,1,0:T(8,128)(2,1)}, u32[]{:S(2)}, u32[]{:S(2)}) collective-permute-start(bf16[6,32,1024]{2,1,0:T(8,128)(2,1)} %collective-permute-done.28.refs_11_), channel_id=1, source_target_pairs={{0,4},{2,6},{4,0},{6,2},{8,12},{10,14},{12,8},{14,10},{16,20},{18,... | collective-permute-start | bytes 1179656 | tf_op jit(solution)/shard_map/ppermute | solution.py:280
  136.9 19.9 %collective-permute-start.30 = (bf16[6,32,1024]{2,1,0:T(8,128)(2,1)}, bf16[6,32,1024]{2,1,0:T(8,128)(2,1)}, u32[]{:S(2)}, u32[]{:S(2)}) collective-permute-start(bf16[6,32,1024]{2,1,0:T(8,128)(2,1)} %collective-permute-done.21.refs_5_), channel_id=1, source_target_pairs={{0,2},{2,0},{4,6},{6,4},{8,10},{10,8},{12,14},{14,12},{16,18},{18,... | collective-permute-start | bytes 1179656 | tf_op jit(solution)/shard_map/ppermute | solution.py:277
  139.6 17.2 %collective-permute-start.23 = (bf16[6,32,1024]{2,1,0:T(8,128)(2,1)}, bf16[6,32,1024]{2,1,0:T(8,128)(2,1)}, u32[]{:S(2)}, u32[]{:S(2)}) collective-permute-start(bf16[6,32,1024]{2,1,0:T(8,128)(2,1)} %collective-permute-done.19.refs_2_), channel_id=1, source_target_pairs={{0,4},{2,6},{4,0},{6,2},{8,12},{10,14},{12,8},{14,10},{16,20},{18,... | collective-permute-start | bytes 1179656 | tf_op jit(solution)/shard_map/ppermute | solution.py:280
  142.0 18.6 %collective-permute-start.31 = (bf16[6,32,1024]{2,1,0:T(8,128)(2,1)}, bf16[6,32,1024]{2,1,0:T(8,128)(2,1)}, u32[]{:S(2)}, u32[]{:S(2)}) collective-permute-start(bf16[6,32,1024]{2,1,0:T(8,128)(2,1)} %collective-permute-done.27.refs_10_), channel_id=1, source_target_pairs={{0,4},{2,6},{4,0},{6,2},{8,12},{10,14},{12,8},{14,10},{16,20},{18,... | collective-permute-start | bytes 1179656 | tf_op jit(solution)/shard_map/ppermute | solution.py:280
  166.8 23.9 %collective-permute-start.35 = (bf16[2,3,32,1024]{3,2,1,0:T(8,128)(2,1)S(1)}, bf16[2,3,32,1024]{3,2,1,0:T(8,128)(2,1)S(1)}, u32[]{:S(2)}, u32[]{:S(2)}) collective-permute-start(bf16[2,3,32,1024]{3,2,1,0:T(8,128)(2,1)S(1)} %slice.32), channel_id=1, source_target_pairs={{0,4},{2,6},{4,0},{6,2},{8,12},{10,14},{12,8},{14,10},{16,20},{18,... | collective-permute-start | bytes 1179656 | tf_op jit(solution)/shard_map/ppermute | solution.py:280
  168.5 22.2 %collective-permute-start.34 = (bf16[2,3,32,1024]{3,2,1,0:T(8,128)(2,1)S(1)}, bf16[2,3,32,1024]{3,2,1,0:T(8,128)(2,1)S(1)}, u32[]{:S(2)}, u32[]{:S(2)}) collective-permute-start(bf16[2,3,32,1024]{3,2,1,0:T(8,128)(2,1)S(1)} %slice.31), channel_id=1, source_target_pairs={{0,2},{2,0},{4,6},{6,4},{8,10},{10,8},{12,14},{14,12},{16,18},{18,... | collective-permute-start | bytes 1179656 | tf_op jit(solution)/shard_map/ppermute | solution.py:277
  (22 other events, 479.0 us)
Sparse Core Ops, SparseCore 0:
  9.6 40.4 all-gather.4
  128.7 61.5 all-gather.6
where the time goes:
time: 218 us; the launch traced here: 217 us
  waiting for transfers between devices  79.1 us (36%)
  starting transfers between devices  54.9 us (25%)
  Pallas kernels  38.5 us (18%)
  other arithmetic  19 us (9%)
  between operations  14.3 us (7%)
  local copies, waits for them, and re-layouts  11 us (5%)
    ppermute x15, waiting for transfers between devices, over_x(): return lax.ppermute(value, 'dp', self.x_pairs)  36.7 us
    ppermute x6, waiting for transfers between devices, over_z(): return lax.ppermute(value, 'dp', pairs)  30.7 us
    ppermute x15, starting transfers between devices, over_x(): return lax.ppermute(value, 'dp', self.x_pairs)  22.2 us
    ppermute x14, starting transfers between devices, over_y(): return lax.ppermute(value, 'dp', self.y_pairs)  17.1 us
    convert_element_type x7, other arithmetic, half(): return value.astype(jnp.bfloat16)  16.2 us
    ppermute x6, starting transfers between devices, over_z(): return lax.ppermute(value, 'dp', pairs)  14.9 us
    pallas_call x1, Pallas kernels, applied(): pl.pallas_call(functools.partial(apply_kernel, len(sets), first_count, ma...  14.3 us
    pallas_call x1, Pallas kernels, chains(): pl.pallas_call(functools.partial(chain_kernel, parts), grid=(count // ste...  12.3 us
  transfers between devices with their start and end apart: 40, of which 22 were waited for; matrix products, arithmetic and copies ran while one was open for 12% of the time, Pallas kernels for 11%

commit v1 on v0

--- a/solution.py
+++ b/solution.py
@@ -353,46 +353,48 @@
         start = place(me, dx, dy, dz) * row_count
         return lax.dynamic_slice_in_dim(terms, start, row_count, axis=1)
 
-    me = grid.me
-    raw_far1, raw_far2 = term(me, 1, 1, 1), term(me, 1, 1, 2)
+    raw_far1, raw_far2 = term(grid.me, 1, 1, 1), term(grid.me, 1, 1, 2)
     me = after(grid.me, raw_far1, raw_far2, master_gather.own)
-    raw_x1, raw_far3, raw_y2 = term(me, 1, 0, 1), term(me, 1, 1, 3), term(me, 0, 1, 2)
-    raw_y3, raw_far0, raw_x0 = term(me, 0, 1, 3), term(me, 1, 1, 0), term(me, 1, 0, 0)
+    raw = {
+        where: term(me, *where)
+        for where in [(1, 0, 1), (1, 1, 3), (0, 1, 2), (0, 1, 3), (1, 1, 0), (1, 0, 0)]
+    }
     far1 = grid.over_x(raw_far1)
     far2 = grid.over_y(raw_far2)
-    along_x1 = grid.over_x(raw_x1)
-    far3 = grid.over_y(raw_far3)
-    along_y2 = grid.over_y(raw_y2)
-
-    me = after(grid.me, far1, far2, raw_y3)
-    sent_x2 = half(added(term(me, 1, 0, 2), far2))
-    sent_y1 = half(added(term(me, 0, 1, 1), far1))
+    along_x1 = grid.over_x(raw[1, 0, 1])
+    far3 = grid.over_y(raw[1, 1, 3])
+    along_y2 = grid.over_y(raw[0, 1, 2])
+    me = after(grid.me, *raw.values())
+    rest = [(1, 0, 2), (0, 1, 1), (1, 0, 3), (0, 1, 0)] + [(0, 0, dz) for dz in range(LINE)]
+    raw.update(zip(rest, lax.optimization_barrier([term(me, *where) for where in rest])))
+
+    far1, far2, here = lax.optimization_barrier((far1, far2, [raw[where] for where in rest]))
+    raw.update(zip(rest, here))
+    sent_x2 = half(added(raw[1, 0, 2], far2))
+    sent_y1 = half(added(raw[0, 1, 1], far1))
     along_x2 = grid.over_x(sent_x2)
     along_y1 = grid.over_y(sent_y1)
 
-    me = after(grid.me, far3, along_x1, sent_x2, sent_y1)
-    sent_x3 = half(added(term(me, 1, 0, 3), far3))
+    far0 = grid.over_x(after(raw[1, 1, 0], along_x1, sent_x2, sent_y1))
+
+    mine2, mine3 = after((raw[0, 0, 2], raw[1, 0, 3]), along_x2, along_y2)
+    near2 = half(added(mine2, along_x2, along_y2))
+    sent_x3 = half(added(mine3, far3))
+    line2 = grid.over_z(near2, 2)
     along_x3 = grid.over_x(sent_x3)
-    along_y3 = grid.over_y(after(raw_y3, far3, along_x1))
-
-    me = after(grid.me, along_y2, along_x2, sent_x3)
-    near2 = half(added(term(me, 0, 0, 2), along_x2, along_y2))
-    line2 = grid.over_z(near2, 2)
-    far0 = grid.over_x(after(raw_far0, along_x2))
-
-    me = after(grid.me, along_x1, along_y1, along_x3, near2)
-    near1 = half(added(term(me, 0, 0, 1), along_x1, along_y1))
+    along_y3 = grid.over_y(after(raw[0, 1, 3], along_y2, far3))
+
+    near1 = half(added(after(raw[0, 0, 1], near2, sent_x3), along_x1, along_y1))
     line1 = grid.over_z(near1, 1)
-    along_x0 = grid.over_x(after(raw_x0, along_x3))
-
-    me = after(grid.me, along_x3, along_y3, far0, near1)
-    near3 = half(added(term(me, 0, 0, 3), along_x3, along_y3))
-    sent_y0 = half(added(term(me, 0, 1, 0), far0))
+    along_x0 = grid.over_x(after(raw[1, 0, 0], near1))
+
+    sent_y0 = half(added(after(raw[0, 1, 0], near1), far0))
+    near3 = half(added(after(raw[0, 0, 3], sent_y0, line2), along_x3, along_y3))
     line3 = grid.over_z(near3, 3)
     master_gather.near(near3, sent_y0)
     along_y0 = grid.over_y(sent_y0)
-    me = after(grid.me, near3, sent_y0, line2)
-    return added(term(me, 0, 0, 0), along_x0, along_y0, line1, line2, line3)
+    mine = after(raw[0, 0, 0], near3, sent_y0, line2)
+    return added(mine, along_x0, along_y0, line1, line2, line3)
 
 
 def all_gather(grid, own, before_z2, before_x2):

time: 218 us -> 222 us (1.018)
  waiting for transfers between devices: 79.1 us -> 96 us
  starting transfers between devices: 54.9 us -> 46 us
  other arithmetic: 19 us -> 14.1 us
    ppermute x14, waiting for transfers between devices: 10.5 us -> 23.8 us  [over_y(): return lax.ppermute(value, 'dp', self.y_pairs)]
    ppermute x15, starting transfers between devices: 22.2 us -> 15 us  [over_x(): return lax.ppermute(value, 'dp', self.x_pairs)]
    ppermute x6, starting transfers between devices: 14.9 us -> 10.6 us  [over_z(): return lax.ppermute(value, 'dp', pairs)]
    convert_element_type x7 -> x9, other arithmetic: 16.2 us -> 12.4 us  [half(): return value.astype(jnp.bfloat16)]
    ppermute x14, starting transfers between devices: 17.1 us -> 19.7 us  [over_y(): return lax.ppermute(value, 'dp', self.y_pairs)]
    dynamic_slice x2 -> x3, local copies, waits for them, and re-layouts: 4.72 us -> 6.08 us  [term(): return lax.dynamic_slice_in_dim(terms, start, row_count, axis=1)]
  transfers between devices with their start and end apart: 40 -> 40, of which waited for: 22 -> 17; matrix products, arithmetic and copies ran while one was open for 12% -> 10% of each run, Pallas kernels for 11% -> 11%
where the time goes in v1:
time: 222 us; the launch traced here: 221 us
  waiting for transfers between devices  96 us (43%)
  starting transfers between devices  46 us (21%)
  Pallas kernels  38.6 us (17%)
  between operations  14.4 us (6%)
  other arithmetic  14.1 us (6%)
  local copies, waits for them, and re-layouts  11.6 us (5%)
    ppermute x15, waiting for transfers between devices, over_x(): return lax.ppermute(value, 'dp', self.x_pairs)  38.4 us
    ppermute x6, waiting for transfers between devices, over_z(): return lax.ppermute(value, 'dp', pairs)  32.6 us
    ppermute x14, waiting for transfers between devices, over_y(): return lax.ppermute(value, 'dp', self.y_pairs)  23.8 us
    ppermute x14, starting transfers between devices, over_y(): return lax.ppermute(value, 'dp', self.y_pairs)  19.7 us
    ppermute x15, starting transfers between devices, over_x(): return lax.ppermute(value, 'dp', self.x_pairs)  15 us
    pallas_call x1, Pallas kernels, applied(): pl.pallas_call(functools.partial(apply_kernel, len(sets), first_count, ma...  14.4 us
    convert_element_type x9, other arithmetic, half(): return value.astype(jnp.bfloat16)  12.4 us
    pallas_call x1, Pallas kernels, chains(): pl.pallas_call(functools.partial(chain_kernel, parts), grid=(count // ste...  12.3 us
  transfers between devices with their start and end apart: 40, of which 17 were waited for; matrix products, arithmetic and copies ran while one was open for 10% of the time, Pallas kernels for 11%

profile of v1, /device:TPU:0, one launch (start us, length us, event | category | flops | bytes accessed | tf_op | source)
XLA Modules:
  0.0 220.8 jit_solution(13257057841192985517)
XLA Ops:
  7.2 1.9 dynamic-slice_bitcast_fusion.14
  9.2 3.0 %collective-permute-start.1 = (bf16[6,32,1024]{2,1,0:T(8,128)(2,1)}, bf16[6,32,1024]{2,1,0:T(8,128)(2,1)}, u32[]{:S(2)}, u32[]{:S(2)}) collective-permute-start(bf16[6,32,1024]{2,1,0:T(8,128)(2,1)} %get-tuple-element.113), channel_id=1, source_target_pairs={{0,4},{2,6},{4,0},{6,2},{8,12},{10,14},{12,8},{14,10},{16,20},{18,... | collective-permute-start | bytes 1179656 | tf_op jit(solution)/shard_map/ppermute | solution.py:280
  13.6 1.9 convert_element_type.100
  15.7 1.9 dynamic-slice_bitcast_fusion.8
  20.2 2.3 %dynamic-slice_bitcast_fusion = (bf16[6,32,1024]{2,1,0:T(8,128)(2,1)S(1)}, bf16[6,32,1024]{2,1,0:T(8,128)(2,1)S(1)}, bf16[6,32,1024]{2,1,0:T(8,128)(2,1)S(1)}, b...) fusion(bf16[1,6,512,1024]{3,2,1,0:T(8,128)(2,1)} %param.4, ...), kind=kLoop, calls=%fused_computation.12 | loop fusion | bytes 6291488 | tf_op jit(solution)/shard_map/dynamic_slice | solution.py:354
  22.5 1.7 collective-permute-done
  25.3 1.6 collective-permute-start.2
  26.9 4.0 %collective-permute-done.3 = bf16[6,32,1024]{2,1,0:T(8,128)(2,1)} collective-permute-done((bf16[6,32,1024]{2,1,0:T(8,128)(2,1)S(1)}, bf16[6,32,1024]{2,1,0:T(8,128)(2,1)}, u32[]{:S(2)}, u32[]{:S(2)}) %collective-permute-start.3) | collective-permute-done | bytes 393248 | tf_op jit(solution)/shard_map/ppermute | solution.py:280
  30.8 7.6 %collective-permute-done.4 = bf16[6,32,1024]{2,1,0:T(8,128)(2,1)} collective-permute-done((bf16[6,32,1024]{2,1,0:T(8,128)(2,1)S(1)}, bf16[6,32,1024]{2,1,0:T(8,128)(2,1)}, u32[]{:S(2)}, u32[]{:S(2)}) %collective-permute-start.4) | collective-permute-done | bytes 393248 | tf_op jit(solution)/shard_map/ppermute | solution.py:280
  38.4 1.7 collective-permute-start.10
  40.7 1.7 collective-permute-start.7
  45.1 2.9 %collective-permute-start.8 = (bf16[6,32,1024]{2,1,0:T(8,128)(2,1)S(1)}, bf16[6,32,1024]{2,1,0:T(8,128)(2,1)S(1)}, u32[]{:S(2)}, u32[]{:S(2)}) collective-permute-start(bf16[6,32,1024]{2,1,0:T(8,128)(2,1)S(1)} %add_convert_fusion.6), channel_id=1, source_target_pairs={{0,16},{2,18},{4,20},{6,22},{8,24},{10,26},{12,28},{14,30},{16,0},... | collective-permute-start | bytes 1179656 | tf_op jit(solution)/shard_map/ppermute | solution.py:284
  48.0 9.2 %collective-permute-done.6 = bf16[6,32,1024]{2,1,0:T(8,128)(2,1)S(1)} collective-permute-done((bf16[6,32,1024]{2,1,0:T(8,128)(2,1)S(1)}, bf16[6,32,1024]{2,1,0:T(8,128)(2,1)S(1)}, u32[]{:S(2)}, u32[]{:S(2)}) %collective-permute-start.6) | collective-permute-done | bytes 393248 | tf_op jit(solution)/shard_map/ppermute | solution.py:280
  57.2 1.9 add_convert_fusion.3
  63.0 14.1 %collective-permute-done.8 = bf16[6,32,1024]{2,1,0:T(8,128)(2,1)S(1)} collective-permute-done((bf16[6,32,1024]{2,1,0:T(8,128)(2,1)S(1)}, bf16[6,32,1024]{2,1,0:T(8,128)(2,1)S(1)}, u32[]{:S(2)}, u32[]{:S(2)}) %collective-permute-start.8) | collective-permute-done | bytes 393248 | tf_op jit(solution)/shard_map/ppermute | solution.py:284
  83.0 6.2 %collective-permute-done.11 = bf16[6,32,1024]{2,1,0:T(8,128)(2,1)} collective-permute-done((bf16[6,32,1024]{2,1,0:T(8,128)(2,1)S(1)}, bf16[6,32,1024]{2,1,0:T(8,128)(2,1)}, u32[]{:S(2)}, u32[]{:S(2)}) %collective-permute-start.11) | collective-permute-done | bytes 393248 | tf_op jit(solution)/shard_map/ppermute | solution.py:277
  90.4 3.1 %add_convert_fusion = (bf16[6,32,1024]{2,1,0:T(8,128)(2,1)S(1)}, f32[6,32,1024]{2,1,0:T(8,128)}) fusion(bf16[6,32,1024]{2,1,0:T(8,128)(2,1)} %collective-permute-done.14, bf16[6,32,1024]{2,1,0:T(8,128)(2,1)} %copy-done.8, bf16[6,32,1024]{2,1,0:T(8,128)(2,1)} %collective-permute-done.13, bf16[6,32,1024]{2,1,0:T(8,128)(2,1)} %collective-permute-done.12, ...), kind=kLoop, calls=%fused_computation.2 | loop fusion | flops 3145728 | bytes 4325376 | tf_op jit(solution)/shard_map/convert_element_type | solution.py:33
  93.5 3.8 %collective-permute-start.15 = (bf16[6,32,1024]{2,1,0:T(8,128)(2,1)S(1)}, bf16[6,32,1024]{2,1,0:T(8,128)(2,1)S(1)}, u32[]{:S(2)}, u32[]{:S(2)}) collective-permute-start(bf16[6,32,1024]{2,1,0:T(8,128)(2,1)S(1)} %get-tuple-element.81.refs_0_), channel_id=1, source_target_pairs={{0,24},{2,26},{4,28},{6,30},{8,0},{10,2},{12,4},{14,6},{16,8},{18,... | collective-permute-start | bytes 1179656 | tf_op jit(solution)/shard_map/ppermute | solution.py:284
  97.9 9.5 %collective-permute-done.16.refs_3_ = bf16[6,32,1024]{2,1,0:T(8,128)(2,1)S(1)} collective-permute-done((bf16[6,32,1024]{2,1,0:T(8,128)(2,1)S(1)}, bf16[6,32,1024]{2,1,0:T(8,128)(2,1)S(1)}, u32[]{:S(2)}, u32[]{:S(2)}) %collective-permute-start.16) | collective-permute-done | bytes 393248 | tf_op jit(solution)/shard_map/ppermute | solution.py:284
  108.8 2.8 %collective-permute-done.15.refs_1_ = bf16[6,32,1024]{2,1,0:T(8,128)(2,1)S(1)} collective-permute-done((bf16[6,32,1024]{2,1,0:T(8,128)(2,1)S(1)}, bf16[6,32,1024]{2,1,0:T(8,128)(2,1)S(1)}, u32[]{:S(2)}, u32[]{:S(2)}) %collective-permute-start.15) | collective-permute-done | bytes 393248 | tf_op jit(solution)/shard_map/ppermute | solution.py:284
  111.6 2.4 %collective-permute-start.19 = (bf16[6,32,1024]{2,1,0:T(8,128)(2,1)S(1)}, bf16[6,32,1024]{2,1,0:T(8,128)(2,1)}, u32[]{:S(2)}, u32[]{:S(2)}) collective-permute-start(bf16[6,32,1024]{2,1,0:T(8,128)(2,1)S(1)} %get-tuple-element.81.refs_0_), channel_id=1, source_target_pairs={{0,16},{2,18},{4,20},{6,22},{8,24},{10,26},{12,28},{14,30},{16,0},... | collective-permute-start | bytes 1179656 | tf_op jit(solution)/shard_map/ppermute | solution.py:284
  117.7 5.1 %collective-permute-done.22 = bf16[3,32,1024]{2,1,0:T(8,128)(2,1)S(1)} collective-permute-done((bf16[3,32,1024]{2,1,0:T(8,128)(2,1)S(1)}, bf16[3,32,1024]{2,1,0:T(8,128)(2,1)S(1)}, u32[]{:S(2)}, u32[]{:S(2)}) %collective-permute-start.22) | collective-permute-done | bytes 196640 | tf_op jit(solution)/shard_map/ppermute | solution.py:277
  125.3 5.0 %collective-permute-done.19.refs_2_ = bf16[6,32,1024]{2,1,0:T(8,128)(2,1)} collective-permute-done((bf16[6,32,1024]{2,1,0:T(8,128)(2,1)S(1)}, bf16[6,32,1024]{2,1,0:T(8,128)(2,1)}, u32[]{:S(2)}, u32[]{:S(2)}) %collective-permute-start.19) | collective-permute-done | bytes 393248 | tf_op jit(solution)/shard_map/ppermute | solution.py:284
  132.4 7.4 %collective-permute-done.29.refs_12_ = bf16[6,32,1024]{2,1,0:T(8,128)(2,1)} collective-permute-done((bf16[6,32,1024]{2,1,0:T(8,128)(2,1)}, bf16[6,32,1024]{2,1,0:T(8,128)(2,1)}, u32[]{:S(2)}, u32[]{:S(2)}) %collective-permute-start.29) | collective-permute-done | bytes 393248 | tf_op jit(solution)/shard_map/ppermute | solution.py:277
  143.9 4.4 %collective-permute-done.27.refs_10_ = bf16[6,32,1024]{2,1,0:T(8,128)(2,1)} collective-permute-done((bf16[6,32,1024]{2,1,0:T(8,128)(2,1)}, bf16[6,32,1024]{2,1,0:T(8,128)(2,1)}, u32[]{:S(2)}, u32[]{:S(2)}) %collective-permute-start.27) | collective-permute-done | bytes 393248 | tf_op jit(solution)/shard_map/ppermute | solution.py:277
  150.3 6.3 %collective-permute-done.26.refs_9_ = bf16[6,32,1024]{2,1,0:T(8,128)(2,1)} collective-permute-done((bf16[6,32,1024]{2,1,0:T(8,128)(2,1)S(1)}, bf16[6,32,1024]{2,1,0:T(8,128)(2,1)}, u32[]{:S(2)}, u32[]{:S(2)}) %collective-permute-start.26) | collective-permute-done | bytes 393248 | tf_op jit(solution)/shard_map/ppermute | solution.py:277
  156.6 7.2 %collective-permute-done.30.refs_13_ = bf16[6,32,1024]{2,1,0:T(8,128)(2,1)} collective-permute-done((bf16[6,32,1024]{2,1,0:T(8,128)(2,1)}, bf16[6,32,1024]{2,1,0:T(8,128)(2,1)}, u32[]{:S(2)}, u32[]{:S(2)}) %collective-permute-start.30) | collective-permute-done | bytes 393248 | tf_op jit(solution)/shard_map/ppermute | solution.py:277
  163.9 3.0 %collective-permute-done.31.refs_14_ = bf16[6,32,1024]{2,1,0:T(8,128)(2,1)} collective-permute-done((bf16[6,32,1024]{2,1,0:T(8,128)(2,1)}, bf16[6,32,1024]{2,1,0:T(8,128)(2,1)}, u32[]{:S(2)}, u32[]{:S(2)}) %collective-permute-start.31) | collective-permute-done | bytes 393248 | tf_op jit(solution)/shard_map/ppermute | solution.py:280
  166.9 6.1 %shard_map.84 = (bf16[3,512,1024]{2,1,0:T(8,128)(2,1)}, bf16[3,512,512]{2,1,0:T(8,128)(2,1)}) custom-call(s32[3]{0:T(128)} %get-tuple-element.117.order_ref, bf16[6,32,1024]{2,1,0:T(8,128)(2,1)} %copy-done.1, bf16[6,32,1024]{2,1,0:T(8,128)(2,1)} %copy-done.7, bf16[6,32,1024]{2,1,0:T(8,128)(2,1)} %collective-permute-done.19.refs_2_, ...), custom_call_target="tpu_custom_call" | custom-call | flops 1610612736 | bytes 7864320 | tf_op jit(solution)/shard_map/pallas_call | solution.py:58
  175.3 5.9 %shard_map.83 = (bf16[3,512,1024]{2,1,0:T(8,128)(2,1)}, bf16[3,512,512]{2,1,0:T(8,128)(2,1)}) custom-call(s32[3]{0:T(128)} %get-tuple-element.118.order_ref, bf16[6,32,1024]{2,1,0:T(8,128)(2,1)} %copy-done.1, bf16[6,32,1024]{2,1,0:T(8,128)(2,1)} %copy-done.7, bf16[6,32,1024]{2,1,0:T(8,128)(2,1)} %collective-permute-done.19.refs_2_, ...), custom_call_target="tpu_custom_call" | custom-call | flops 1610612736 | bytes 7864320 | tf_op jit(solution)/shard_map/pallas_call | solution.py:58
  182.3 12.3 %shard_map.85 = (bf16[3,512,512]{2,1,0:T(8,128)(2,1)}, f32[3,8,128]{2,1,0:T(8,128)}) custom-call(bf16[3,512,512]{2,1,0:T(8,128)(2,1)} %get-tuple-element.83.refs_0_, bf16[3,512,512]{2,1,0:T(8,128)(2,1)} %copy-done.14), custom_call_target="tpu_custom_call" | custom-call | flops 7247757312 | bytes 4718592 | tf_op jit(solution)/shard_map/pallas_call | solution.py:133
  199.5 14.4 %shard_map.86 = (bf16[6,512,1024]{2,1,0:T(8,128)(2,1)}, f32[6,32,1024]{2,1,0:T(8,128)}, bf16[2,512,1024]{2,1,0:T(8,128)(2,1)}, f32[1,2]{1,0:T(1,128)}) custom-call(s32[16]{0:T(128)} %stack.125.places_ref, s32[16]{0:T(128)} %stack.142.spans_ref, s32[6]{0:T(128)} %broadcast_select_fusion.slots_ref, s32[6]{0:T(128)} %copy-done.12, ...), custom_call_target="tpu_custom_call" | custom-call | flops 3221225472 | bytes 28311552 | tf_op jit(solution)/shard_map/pallas_call | solution.py:228
  (111 shorter events, 44.0 us)
Async XLA Ops:
  7.2 72.4 %all-gather.5.cloned.1.call-start = ((), (), s32[]{:S(2)}) async-start(), calls=%async_computation | async-start | bytes 1966080 | tf_op jit(solution)/shard_map/all_gather | solution.py:306
  9.2 13.3 %collective-permute-start.1 = (bf16[6,32,1024]{2,1,0:T(8,128)(2,1)}, bf16[6,32,1024]{2,1,0:T(8,128)(2,1)}, u32[]{:S(2)}, u32[]{:S(2)}) collective-permute-start(bf16[6,32,1024]{2,1,0:T(8,128)(2,1)} %get-tuple-element.113), channel_id=1, source_target_pairs={{0,4},{2,6},{4,0},{6,2},{8,12},{10,14},{12,8},{14,10},{16,20},{18,... | collective-permute-start | bytes 1179656 | tf_op jit(solution)/shard_map/ppermute | solution.py:280
  15.6 182.7 %all-gather.7.cloned.1.call-start = ((), (), s32[]{:S(2)}) async-start(), calls=%async_computation.1 | async-start | bytes 3932160 | tf_op jit(solution)/shard_map/all_gather | solution.py:320
  17.6 13.3 %collective-permute-start.3 = (bf16[6,32,1024]{2,1,0:T(8,128)(2,1)S(1)}, bf16[6,32,1024]{2,1,0:T(8,128)(2,1)}, u32[]{:S(2)}, u32[]{:S(2)}) collective-permute-start(bf16[6,32,1024]{2,1,0:T(8,128)(2,1)S(1)} %get-tuple-element.110), channel_id=1, source_target_pairs={{0,4},{2,6},{4,0},{6,2},{8,12},{10,14},{12,8},{14,10},{16,20},{18,... | collective-permute-start | bytes 1179656 | tf_op jit(solution)/shard_map/ppermute | solution.py:280
  18.1 20.3 %collective-permute-start.4 = (bf16[6,32,1024]{2,1,0:T(8,128)(2,1)S(1)}, bf16[6,32,1024]{2,1,0:T(8,128)(2,1)}, u32[]{:S(2)}, u32[]{:S(2)}) collective-permute-start(bf16[6,32,1024]{2,1,0:T(8,128)(2,1)S(1)} %get-tuple-element.111), channel_id=1, source_target_pairs={{0,4},{2,6},{4,0},{6,2},{8,12},{10,14},{12,8},{14,10},{16,20},{18,... | collective-permute-start | bytes 1179656 | tf_op jit(solution)/shard_map/ppermute | solution.py:280
  19.7 21.0 %collective-permute-start.5 = (bf16[6,32,1024]{2,1,0:T(8,128)(2,1)S(1)}, bf16[6,32,1024]{2,1,0:T(8,128)(2,1)}, u32[]{:S(2)}, u32[]{:S(2)}) collective-permute-start(bf16[6,32,1024]{2,1,0:T(8,128)(2,1)S(1)} %get-tuple-element.112), channel_id=1, source_target_pairs={{0,2},{2,0},{4,6},{6,4},{8,10},{10,8},{12,14},{14,12},{16,18},{18,... | collective-permute-start | bytes 1179656 | tf_op jit(solution)/shard_map/ppermute | solution.py:277
  25.3 17.1 %collective-permute-start.2 = (bf16[6,32,1024]{2,1,0:T(8,128)(2,1)S(1)}, bf16[6,32,1024]{2,1,0:T(8,128)(2,1)S(1)}, u32[]{:S(2)}, u32[]{:S(2)}) collective-permute-start(bf16[6,32,1024]{2,1,0:T(8,128)(2,1)S(1)} %add_convert_fusion.7), channel_id=1, source_target_pairs={{0,2},{2,0},{4,6},{6,4},{8,10},{10,8},{12,14},{14,12},{16,18},{18,... | collective-permute-start | bytes 1179656 | tf_op jit(solution)/shard_map/ppermute | solution.py:277
  38.4 40.2 %collective-permute-start.10 = (bf16[6,32,1024]{2,1,0:T(8,128)(2,1)S(1)}, bf16[6,32,1024]{2,1,0:T(8,128)(2,1)S(1)}, u32[]{:S(2)}, u32[]{:S(2)}) collective-permute-start(bf16[6,32,1024]{2,1,0:T(8,128)(2,1)S(1)} %get-tuple-element.77), channel_id=1, source_target_pairs={{0,4},{2,6},{4,0},{6,2},{8,12},{10,14},{12,8},{14,10},{16,20},{18,... | collective-permute-start | bytes 1179656 | tf_op jit(solution)/shard_map/ppermute | solution.py:280
  40.3 16.8 %collective-permute-start.6 = (bf16[6,32,1024]{2,1,0:T(8,128)(2,1)S(1)}, bf16[6,32,1024]{2,1,0:T(8,128)(2,1)S(1)}, u32[]{:S(2)}, u32[]{:S(2)}) collective-permute-start(bf16[6,32,1024]{2,1,0:T(8,128)(2,1)S(1)} %add_convert_fusion.4), channel_id=1, source_target_pairs={{0,4},{2,6},{4,0},{6,2},{8,12},{10,14},{12,8},{14,10},{16,20},{18,... | collective-permute-start | bytes 1179656 | tf_op jit(solution)/shard_map/ppermute | solution.py:280
  40.7 19.9 %collective-permute-start.7 = (bf16[6,32,1024]{2,1,0:T(8,128)(2,1)S(1)}, bf16[6,32,1024]{2,1,0:T(8,128)(2,1)S(1)}, u32[]{:S(2)}, u32[]{:S(2)}) collective-permute-start(bf16[6,32,1024]{2,1,0:T(8,128)(2,1)S(1)} %get-tuple-element.75), channel_id=1, source_target_pairs={{0,2},{2,0},{4,6},{6,4},{8,10},{10,8},{12,14},{14,12},{16,18},{18,... | collective-permute-start | bytes 1179656 | tf_op jit(solution)/shard_map/ppermute | solution.py:277
  43.5 35.1 %collective-permute-start.9 = (bf16[6,32,1024]{2,1,0:T(8,128)(2,1)S(1)}, bf16[6,32,1024]{2,1,0:T(8,128)(2,1)S(1)}, u32[]{:S(2)}, u32[]{:S(2)}) collective-permute-start(bf16[6,32,1024]{2,1,0:T(8,128)(2,1)S(1)} %add_convert_fusion.5), channel_id=1, source_target_pairs={{0,2},{2,0},{4,6},{6,4},{8,10},{10,8},{12,14},{14,12},{16,18},{18,... | collective-permute-start | bytes 1179656 | tf_op jit(solution)/shard_map/ppermute | solution.py:277
  45.1 32.0 %collective-permute-start.8 = (bf16[6,32,1024]{2,1,0:T(8,128)(2,1)S(1)}, bf16[6,32,1024]{2,1,0:T(8,128)(2,1)S(1)}, u32[]{:S(2)}, u32[]{:S(2)}) collective-permute-start(bf16[6,32,1024]{2,1,0:T(8,128)(2,1)S(1)} %add_convert_fusion.6), channel_id=1, source_target_pairs={{0,16},{2,18},{4,20},{6,22},{8,24},{10,26},{12,28},{14,30},{16,0},... | collective-permute-start | bytes 1179656 | tf_op jit(solution)/shard_map/ppermute | solution.py:284
  59.1 30.1 %collective-permute-start.13 = (bf16[6,32,1024]{2,1,0:T(8,128)(2,1)}, bf16[6,32,1024]{2,1,0:T(8,128)(2,1)}, u32[]{:S(2)}, u32[]{:S(2)}) collective-permute-start(bf16[6,32,1024]{2,1,0:T(8,128)(2,1)} %add_convert_fusion.3), channel_id=1, source_target_pairs={{0,8},{2,10},{4,12},{6,14},{8,16},{10,18},{12,20},{14,22},{16,24},... | collective-permute-start | bytes 1179656 | tf_op jit(solution)/shard_map/ppermute | solution.py:284
  61.5 21.0 %collective-permute-start.12 = (bf16[6,32,1024]{2,1,0:T(8,128)(2,1)}, bf16[6,32,1024]{2,1,0:T(8,128)(2,1)}, u32[]{:S(2)}, u32[]{:S(2)}) collective-permute-start(bf16[6,32,1024]{2,1,0:T(8,128)(2,1)} %add_convert_fusion.2), channel_id=1, source_target_pairs={{0,4},{2,6},{4,0},{6,2},{8,12},{10,14},{12,8},{14,10},{16,20},{18,... | collective-permute-start | bytes 1179656 | tf_op jit(solution)/shard_map/ppermute | solution.py:280
  80.9 30.7 %collective-permute-start.18 = (bf16[5,3,32,1024]{3,2,1,0:T(8,128)(2,1)S(1)}, bf16[5,3,32,1024]{3,2,1,0:T(8,128)(2,1)S(1)}, u32[]{:S(2)}, u32[]{:S(2)}) collective-permute-start(bf16[5,3,32,1024]{3,2,1,0:T(8,128)(2,1)S(1)} %pad_maximum_fusion), channel_id=1, source_target_pairs={{0,4},{2,6},{4,0},{6,2},{8,12},{10,14},{12,8},{14,10},{16,20},{18,... | collective-permute-start | bytes 2949128 | tf_op jit(solution)/shard_map/ppermute | solution.py:280
  82.5 29.2 %collective-permute-start.17 = (bf16[5,3,32,1024]{3,2,1,0:T(8,128)(2,1)S(1)}, bf16[5,3,32,1024]{3,2,1,0:T(8,128)(2,1)S(1)}, u32[]{:S(2)}, u32[]{:S(2)}) collective-permute-start(bf16[5,3,32,1024]{3,2,1,0:T(8,128)(2,1)S(1)} %pad_maximum_fusion), channel_id=1, source_target_pairs={{0,2},{2,0},{4,6},{6,4},{8,10},{10,8},{12,14},{14,12},{16,18},{18,... | collective-permute-start | bytes 2949128 | tf_op jit(solution)/shard_map/ppermute | solution.py:277
  93.5 13.9 %collective-permute-start.16 = (bf16[6,32,1024]{2,1,0:T(8,128)(2,1)S(1)}, bf16[6,32,1024]{2,1,0:T(8,128)(2,1)S(1)}, u32[]{:S(2)}, u32[]{:S(2)}) collective-permute-start(bf16[6,32,1024]{2,1,0:T(8,128)(2,1)S(1)} %get-tuple-element.81.refs_0_), channel_id=1, source_target_pairs={{0,8},{2,10},{4,12},{6,14},{8,16},{10,18},{12,20},{14,22},{16,24},... | collective-permute-start | bytes 1179656 | tf_op jit(solution)/shard_map/ppermute | solution.py:284
  93.5 18.1 %collective-permute-start.15 = (bf16[6,32,1024]{2,1,0:T(8,128)(2,1)S(1)}, bf16[6,32,1024]{2,1,0:T(8,128)(2,1)S(1)}, u32[]{:S(2)}, u32[]{:S(2)}) collective-permute-start(bf16[6,32,1024]{2,1,0:T(8,128)(2,1)S(1)} %get-tuple-element.81.refs_0_), channel_id=1, source_target_pairs={{0,24},{2,26},{4,28},{6,30},{8,0},{10,2},{12,4},{14,6},{16,8},{18,... | collective-permute-start | bytes 1179656 | tf_op jit(solution)/shard_map/ppermute | solution.py:284
  97.3 34.4 %collective-permute-start.25 = (bf16[6,32,1024]{2,1,0:T(8,128)(2,1)S(1)}, bf16[6,32,1024]{2,1,0:T(8,128)(2,1)}, u32[]{:S(2)}, u32[]{:S(2)}) collective-permute-start(bf16[6,32,1024]{2,1,0:T(8,128)(2,1)S(1)} %get-tuple-element.81.refs_0_), channel_id=1, source_target_pairs={{0,2},{2,0},{4,6},{6,4},{8,10},{10,8},{12,14},{14,12},{16,18},{18,... | collective-permute-start | bytes 1179656 | tf_op jit(solution)/shard_map/ppermute | solution.py:277
  111.6 18.7 %collective-permute-start.19 = (bf16[6,32,1024]{2,1,0:T(8,128)(2,1)S(1)}, bf16[6,32,1024]{2,1,0:T(8,128)(2,1)}, u32[]{:S(2)}, u32[]{:S(2)}) collective-permute-start(bf16[6,32,1024]{2,1,0:T(8,128)(2,1)S(1)} %get-tuple-element.81.refs_0_), channel_id=1, source_target_pairs={{0,16},{2,18},{4,20},{6,22},{8,24},{10,26},{12,28},{14,30},{16,0},... | collective-permute-start | bytes 1179656 | tf_op jit(solution)/shard_map/ppermute | solution.py:284
  114.7 26.6 %collective-permute-start.28 = (bf16[6,32,1024]{2,1,0:T(8,128)(2,1)S(1)}, bf16[6,32,1024]{2,1,0:T(8,128)(2,1)}, u32[]{:S(2)}, u32[]{:S(2)}) collective-permute-start(bf16[6,32,1024]{2,1,0:T(8,128)(2,1)S(1)} %collective-permute-done.16.refs_3_), channel_id=1, source_target_pairs={{0,2},{2,0},{4,6},{6,4},{8,10},{10,8},{12,14},{14,12},{16,18},{18,... | collective-permute-start | bytes 1179656 | tf_op jit(solution)/shard_map/ppermute | solution.py:277
  116.2 27.1 %collective-permute-start.24 = (bf16[6,32,1024]{2,1,0:T(8,128)(2,1)S(1)}, bf16[6,32,1024]{2,1,0:T(8,128)(2,1)}, u32[]{:S(2)}, u32[]{:S(2)}) collective-permute-start(bf16[6,32,1024]{2,1,0:T(8,128)(2,1)S(1)} %collective-permute-done.16.refs_3_), channel_id=1, source_target_pairs={{0,4},{2,6},{4,0},{6,2},{8,12},{10,14},{12,8},{14,10},{16,20},{18,... | collective-permute-start | bytes 1179656 | tf_op jit(solution)/shard_map/ppermute | solution.py:280
  122.8 17.0 %collective-permute-start.29 = (bf16[6,32,1024]{2,1,0:T(8,128)(2,1)}, bf16[6,32,1024]{2,1,0:T(8,128)(2,1)}, u32[]{:S(2)}, u32[]{:S(2)}) collective-permute-start(bf16[6,32,1024]{2,1,0:T(8,128)(2,1)} %collective-permute-done.20.refs_4_), channel_id=1, source_target_pairs={{0,2},{2,0},{4,6},{6,4},{8,10},{10,8},{12,14},{14,12},{16,18},{18,... | collective-permute-start | bytes 1179656 | tf_op jit(solution)/shard_map/ppermute | solution.py:277
  130.3 12.4 %collective-permute-start.21 = (bf16[6,32,1024]{2,1,0:T(8,128)(2,1)S(1)}, bf16[6,32,1024]{2,1,0:T(8,128)(2,1)}, u32[]{:S(2)}, u32[]{:S(2)}) collective-permute-start(bf16[6,32,1024]{2,1,0:T(8,128)(2,1)S(1)} %collective-permute-done.15.refs_1_), channel_id=1, source_target_pairs={{0,4},{2,6},{4,0},{6,2},{8,12},{10,14},{12,8},{14,10},{16,20},{18,... | collective-permute-start | bytes 1179656 | tf_op jit(solution)/shard_map/ppermute | solution.py:280
  131.8 16.4 %collective-permute-start.27 = (bf16[6,32,1024]{2,1,0:T(8,128)(2,1)}, bf16[6,32,1024]{2,1,0:T(8,128)(2,1)}, u32[]{:S(2)}, u32[]{:S(2)}) collective-permute-start(bf16[6,32,1024]{2,1,0:T(8,128)(2,1)} %collective-permute-done.19.refs_2_), channel_id=1, source_target_pairs={{0,2},{2,0},{4,6},{6,4},{8,10},{10,8},{12,14},{14,12},{16,18},{18,... | collective-permute-start | bytes 1179656 | tf_op jit(solution)/shard_map/ppermute | solution.py:277
  139.8 16.9 %collective-permute-start.26 = (bf16[6,32,1024]{2,1,0:T(8,128)(2,1)S(1)}, bf16[6,32,1024]{2,1,0:T(8,128)(2,1)}, u32[]{:S(2)}, u32[]{:S(2)}) collective-permute-start(bf16[6,32,1024]{2,1,0:T(8,128)(2,1)S(1)} %collective-permute-done.15.refs_1_), channel_id=1, source_target_pairs={{0,2},{2,0},{4,6},{6,4},{8,10},{10,8},{12,14},{14,12},{16,18},{18,... | collective-permute-start | bytes 1179656 | tf_op jit(solution)/shard_map/ppermute | solution.py:277
  141.3 15.4 %collective-permute-start.32 = (bf16[6,32,1024]{2,1,0:T(8,128)(2,1)}, bf16[6,32,1024]{2,1,0:T(8,128)(2,1)}, u32[]{:S(2)}, u32[]{:S(2)}) collective-permute-start(bf16[6,32,1024]{2,1,0:T(8,128)(2,1)} %collective-permute-done.28.refs_11_), channel_id=1, source_target_pairs={{0,4},{2,6},{4,0},{6,2},{8,12},{10,14},{12,8},{14,10},{16,20},{18,... | collective-permute-start | bytes 1179656 | tf_op jit(solution)/shard_map/ppermute | solution.py:280
  142.7 21.1 %collective-permute-start.30 = (bf16[6,32,1024]{2,1,0:T(8,128)(2,1)}, bf16[6,32,1024]{2,1,0:T(8,128)(2,1)}, u32[]{:S(2)}, u32[]{:S(2)}) collective-permute-start(bf16[6,32,1024]{2,1,0:T(8,128)(2,1)} %collective-permute-done.21.refs_5_), channel_id=1, source_target_pairs={{0,2},{2,0},{4,6},{6,4},{8,10},{10,8},{12,14},{14,12},{16,18},{18,... | collective-permute-start | bytes 1179656 | tf_op jit(solution)/shard_map/ppermute | solution.py:277
  143.3 20.6 %collective-permute-start.23 = (bf16[6,32,1024]{2,1,0:T(8,128)(2,1)}, bf16[6,32,1024]{2,1,0:T(8,128)(2,1)}, u32[]{:S(2)}, u32[]{:S(2)}) collective-permute-start(bf16[6,32,1024]{2,1,0:T(8,128)(2,1)} %collective-permute-done.19.refs_2_), channel_id=1, source_target_pairs={{0,4},{2,6},{4,0},{6,2},{8,12},{10,14},{12,8},{14,10},{16,20},{18,... | collective-permute-start | bytes 1179656 | tf_op jit(solution)/shard_map/ppermute | solution.py:280
  148.2 18.7 %collective-permute-start.31 = (bf16[6,32,1024]{2,1,0:T(8,128)(2,1)}, bf16[6,32,1024]{2,1,0:T(8,128)(2,1)}, u32[]{:S(2)}, u32[]{:S(2)}) collective-permute-start(bf16[6,32,1024]{2,1,0:T(8,128)(2,1)} %collective-permute-done.27.refs_10_), channel_id=1, source_target_pairs={{0,4},{2,6},{4,0},{6,2},{8,12},{10,14},{12,8},{14,10},{16,20},{18,... | collective-permute-start | bytes 1179656 | tf_op jit(solution)/shard_map/ppermute | solution.py:280
  173.2 21.4 %collective-permute-start.35 = (bf16[2,3,32,1024]{3,2,1,0:T(8,128)(2,1)S(1)}, bf16[2,3,32,1024]{3,2,1,0:T(8,128)(2,1)S(1)}, u32[]{:S(2)}, u32[]{:S(2)}) collective-permute-start(bf16[2,3,32,1024]{3,2,1,0:T(8,128)(2,1)S(1)} %slice.32), channel_id=1, source_target_pairs={{0,4},{2,6},{4,0},{6,2},{8,12},{10,14},{12,8},{14,10},{16,20},{18,... | collective-permute-start | bytes 1179656 | tf_op jit(solution)/shard_map/ppermute | solution.py:280
  174.7 19.9 %collective-permute-start.34 = (bf16[2,3,32,1024]{3,2,1,0:T(8,128)(2,1)S(1)}, bf16[2,3,32,1024]{3,2,1,0:T(8,128)(2,1)S(1)}, u32[]{:S(2)}, u32[]{:S(2)}) collective-permute-start(bf16[2,3,32,1024]{3,2,1,0:T(8,128)(2,1)S(1)} %slice.31), channel_id=1, source_target_pairs={{0,2},{2,0},{4,6},{6,4},{8,10},{10,8},{12,14},{14,12},{16,18},{18,... | collective-permute-start | bytes 1179656 | tf_op jit(solution)/shard_map/ppermute | solution.py:277
  (23 other events, 477.7 us)
Sparse Core Ops, SparseCore 0:
  15.7 55.5 all-gather.4
  132.5 62.3 all-gather.6

commit v2 on v0

--- a/solution.py
+++ b/solution.py
@@ -21,7 +21,7 @@
 epsilon = 1e-07
 factor = 0.2 * math.sqrt(max(KV, D))
 
-VMEM_LIMIT = 56 * 1024 * 1024
+MIB = 1024 * 1024
 LINE = 4
 
 
@@ -70,7 +70,7 @@
             jax.ShapeDtypeStruct((count, rows, width), jnp.bfloat16),
             jax.ShapeDtypeStruct((count, rows, rows), jnp.bfloat16),
         ],
-        compiler_params=pltpu.CompilerParams(vmem_limit_bytes=VMEM_LIMIT),
+        compiler_params=pltpu.CompilerParams(vmem_limit_bytes=9 * MIB),
         cost_estimate=pl.CostEstimate(
             flops=2 * count * rows * rows * width,
             bytes_accessed=2 * count * rows * (2 * width + rows),
@@ -139,7 +139,7 @@
             jax.ShapeDtypeStruct((count, rows, rows), jnp.bfloat16),
             jax.ShapeDtypeStruct((count, 8, 128), jnp.float32),
         ],
-        compiler_params=pltpu.CompilerParams(vmem_limit_bytes=VMEM_LIMIT),
+        compiler_params=pltpu.CompilerParams(vmem_limit_bytes=20 * MIB),
         cost_estimate=pl.CostEstimate(
             flops=18 * count * rows * rows * rows,
             bytes_accessed=2 * count * rows * rows * (parts + 1),
@@ -249,7 +249,7 @@
             jax.ShapeDtypeStruct(owned, jnp.bfloat16),
             jax.ShapeDtypeStruct((1, MOST), jnp.float32),
         ],
-        compiler_params=pltpu.CompilerParams(vmem_limit_bytes=VMEM_LIMIT),
+        compiler_params=pltpu.CompilerParams(vmem_limit_bytes=20 * MIB),
         cost_estimate=pl.CostEstimate(
             flops=2 * count * rows * rows * width,
             bytes_accessed=2 * count * rows * (4 * width + rows),

time: 218 us -> 224 us (1.028)
  local copies, waits for them, and re-layouts: 11 us -> 22.7 us
  Pallas kernels: 38.5 us -> 32.1 us
    unnamed x28 -> x38, local copies, waits for them, and re-layouts: 3.11 us -> 16.1 us
    pallas_call x1, Pallas kernels: 14.3 us -> 11.7 us  [applied(): pl.pallas_call(functools.partial(apply_kernel, len(sets), first_count, ma...]
  transfers between devices with their start and end apart: 40 -> 40, of which waited for: 22 -> 23; matrix products, arithmetic and copies ran while one was open for 12% -> 11% of each run, Pallas kernels for 11% -> 9%
where the time goes in v2:
time: 224 us; the launch traced here: 223 us
  waiting for transfers between devices  79.4 us (35%)
  starting transfers between devices  55.5 us (25%)
  Pallas kernels  32.1 us (14%)
  local copies, waits for them, and re-layouts  22.7 us (10%)
  other arithmetic  19.3 us (9%)
  between operations  14.2 us (6%)
    ppermute x15, waiting for transfers between devices, over_x(): return lax.ppermute(value, 'dp', self.x_pairs)  36.8 us
    ppermute x6, waiting for transfers between devices, over_z(): return lax.ppermute(value, 'dp', pairs)  29.6 us
    ppermute x15, starting transfers between devices, over_x(): return lax.ppermute(value, 'dp', self.x_pairs)  23 us
    ppermute x14, starting transfers between devices, over_y(): return lax.ppermute(value, 'dp', self.y_pairs)  17 us
    unnamed x38, local copies, waits for them, and re-layouts  16.1 us
    convert_element_type x7, other arithmetic, half(): return value.astype(jnp.bfloat16)  15.7 us
    ppermute x6, starting transfers between devices, over_z(): return lax.ppermute(value, 'dp', pairs)  14.9 us
    ppermute x14, waiting for transfers between devices, over_y(): return lax.ppermute(value, 'dp', self.y_pairs)  11.7 us
  transfers between devices with their start and end apart: 40, of which 23 were waited for; matrix products, arithmetic and copies ran while one was open for 11% of the time, Pallas kernels for 9%

profile of v2, /device:TPU:0, one launch (start us, length us, event | category | flops | bytes accessed | tf_op | source)
XLA Modules:
  0.0 223.2 jit_solution(10200616502767764589)
XLA Ops:
  11.3 3.0 %collective-permute-start.3 = (bf16[6,32,1024]{2,1,0:T(8,128)(2,1)}, bf16[6,32,1024]{2,1,0:T(8,128)(2,1)}, u32[]{:S(2)}, u32[]{:S(2)}) collective-permute-start(bf16[6,32,1024]{2,1,0:T(8,128)(2,1)} %get-tuple-element.71), channel_id=1, source_target_pairs={{0,4},{2,6},{4,0},{6,2},{8,12},{10,14},{12,8},{14,10},{16,20},{18,... | collective-permute-start | bytes 1179656 | tf_op jit(solution)/shard_map/ppermute | solution.py:280
  20.3 4.3 %collective-permute-done.3 = bf16[6,32,1024]{2,1,0:T(8,128)(2,1)} collective-permute-done((bf16[6,32,1024]{2,1,0:T(8,128)(2,1)}, bf16[6,32,1024]{2,1,0:T(8,128)(2,1)}, u32[]{:S(2)}, u32[]{:S(2)}) %collective-permute-start.3) | collective-permute-done | bytes 393248 | tf_op jit(solution)/shard_map/ppermute | solution.py:280
  24.6 2.1 collective-permute-done.2
  26.7 2.6 %fusion.12 = (bf16[6,32,1024]{2,1,0:T(8,128)(2,1)}, bf16[6,32,1024]{2,1,0:T(8,128)(2,1)}) fusion(bf16[6,32,1024]{2,1,0:T(8,128)(2,1)} %collective-permute-done.2, bf16[1,6,512,1024]{3,2,1,0:T(8,128)(2,1)} %param.4, s32[]{:T(128)S(6)} %select_n.67, bf16[6,32,1024]{2,1,0:T(8,128)(2,1)} %collective-permute-done.3, s32[]{:T(128)S(6)} %select_n.66), kind=kLoop, calls=%fused_computation.21 | loop fusion | flops 1572864 | bytes 2359304 | tf_op jit(solution)/shard_map/convert_element_type | solution.py:33
  31.2 3.8 %collective-permute-done.1 = bf16[6,32,1024]{2,1,0:T(8,128)(2,1)S(1)} collective-permute-done((bf16[6,32,1024]{2,1,0:T(8,128)(2,1)S(1)}, bf16[6,32,1024]{2,1,0:T(8,128)(2,1)S(1)}, u32[]{:S(2)}, u32[]{:S(2)}) %collective-permute-start.1) | collective-permute-done | bytes 393248 | tf_op jit(solution)/shard_map/ppermute | solution.py:277
  35.0 2.1 fusion.11
  39.2 2.2 collective-permute-done.9
  41.4 2.1 collective-permute-done.6
  46.4 2.7 %collective-permute-start.10 = (bf16[6,32,1024]{2,1,0:T(8,128)(2,1)S(1)}, bf16[6,32,1024]{2,1,0:T(8,128)(2,1)S(1)}, u32[]{:S(2)}, u32[]{:S(2)}) collective-permute-start(bf16[6,32,1024]{2,1,0:T(8,128)(2,1)S(1)} %fusion.10), channel_id=1, source_target_pairs={{0,16},{2,18},{4,20},{6,22},{8,24},{10,26},{12,28},{14,30},{16,0},... | collective-permute-start | bytes 1179656 | tf_op jit(solution)/shard_map/ppermute | solution.py:284
  51.8 2.2 fusion.8
  57.3 2.9 %collective-permute-done.7 = bf16[6,32,1024]{2,1,0:T(8,128)(2,1)S(1)} collective-permute-done((bf16[6,32,1024]{2,1,0:T(8,128)(2,1)S(1)}, bf16[6,32,1024]{2,1,0:T(8,128)(2,1)S(1)}, u32[]{:S(2)}, u32[]{:S(2)}) %collective-permute-start.7) | collective-permute-done | bytes 393248 | tf_op jit(solution)/shard_map/ppermute | solution.py:277
  60.3 2.3 %fusion.4 = (bf16[6,32,1024]{2,1,0:T(8,128)(2,1)}, bf16[6,32,1024]{2,1,0:T(8,128)(2,1)}) fusion(bf16[6,32,1024]{2,1,0:T(8,128)(2,1)S(1)} %collective-permute-done.7, bf16[1,6,512,1024]{3,2,1,0:T(8,128)(2,1)} %param.4, s32[]{:T(128)S(6)} %select_n.74, bf16[6,32,1024]{2,1,0:T(8,128)(2,1)S(1)} %collective-permute-done.5, ...), kind=kLoop, calls=%fused_computation.8 | loop fusion | flops 1966080 | bytes 2752520 | tf_op jit(solution)/shard_map/convert_element_type | solution.py:33
  62.7 4.0 %collective-permute-start.14 = (bf16[6,32,1024]{2,1,0:T(8,128)(2,1)}, bf16[6,32,1024]{2,1,0:T(8,128)(2,1)}, u32[]{:S(2)}, u32[]{:S(2)}) collective-permute-start(bf16[6,32,1024]{2,1,0:T(8,128)(2,1)} %get-tuple-element.68), channel_id=1, source_target_pairs={{0,24},{2,26},{4,28},{6,30},{8,0},{10,2},{12,4},{14,6},{16,8},{18,... | collective-permute-start | bytes 1179656 | tf_op jit(solution)/shard_map/ppermute | solution.py:284
  69.0 6.2 %collective-permute-done.10 = bf16[6,32,1024]{2,1,0:T(8,128)(2,1)S(1)} collective-permute-done((bf16[6,32,1024]{2,1,0:T(8,128)(2,1)S(1)}, bf16[6,32,1024]{2,1,0:T(8,128)(2,1)S(1)}, u32[]{:S(2)}, u32[]{:S(2)}) %collective-permute-start.10) | collective-permute-done | bytes 393248 | tf_op jit(solution)/shard_map/ppermute | solution.py:284
  77.8 5.0 %collective-permute-done.14 = bf16[6,32,1024]{2,1,0:T(8,128)(2,1)} collective-permute-done((bf16[6,32,1024]{2,1,0:T(8,128)(2,1)}, bf16[6,32,1024]{2,1,0:T(8,128)(2,1)}, u32[]{:S(2)}, u32[]{:S(2)}) %collective-permute-start.14) | collective-permute-done | bytes 393248 | tf_op jit(solution)/shard_map/ppermute | solution.py:284
  82.8 3.1 %add_convert_fusion = (bf16[6,32,1024]{2,1,0:T(8,128)(2,1)S(1)}, f32[6,32,1024]{2,1,0:T(8,128)}) fusion(f32[6,32,1024]{2,1,0:T(8,128)} %param.5, bf16[6,32,1024]{2,1,0:T(8,128)(2,1)} %collective-permute-done.14, bf16[6,32,1024]{2,1,0:T(8,128)(2,1)S(1)} %collective-permute-done.10, bf16[6,32,1024]{2,1,0:T(8,128)(2,1)} %collective-permute-done.13, ...), kind=kLoop, calls=%fused_computation.24 | loop fusion | flops 3145728 | bytes 4325380 | tf_op jit(solution)/shard_map/convert_element_type | solution.py:33
  86.5 3.2 %collective-permute-start.15 = (bf16[6,32,1024]{2,1,0:T(8,128)(2,1)S(1)}, bf16[6,32,1024]{2,1,0:T(8,128)(2,1)S(1)}, u32[]{:S(2)}, u32[]{:S(2)}) collective-permute-start(bf16[6,32,1024]{2,1,0:T(8,128)(2,1)S(1)} %get-tuple-element.43.refs_0_), channel_id=1, source_target_pairs={{0,24},{2,26},{4,28},{6,30},{8,0},{10,2},{12,4},{14,6},{16,8},{18,... | collective-permute-start | bytes 1179656 | tf_op jit(solution)/shard_map/ppermute | solution.py:284
  91.2 8.5 %collective-permute-done.16.refs_3_ = bf16[6,32,1024]{2,1,0:T(8,128)(2,1)S(1)} collective-permute-done((bf16[6,32,1024]{2,1,0:T(8,128)(2,1)S(1)}, bf16[6,32,1024]{2,1,0:T(8,128)(2,1)S(1)}, u32[]{:S(2)}, u32[]{:S(2)}) %collective-permute-start.16) | collective-permute-done | bytes 393248 | tf_op jit(solution)/shard_map/ppermute | solution.py:284
  101.2 4.2 %collective-permute-done.15.refs_1_ = bf16[6,32,1024]{2,1,0:T(8,128)(2,1)S(1)} collective-permute-done((bf16[6,32,1024]{2,1,0:T(8,128)(2,1)S(1)}, bf16[6,32,1024]{2,1,0:T(8,128)(2,1)S(1)}, u32[]{:S(2)}, u32[]{:S(2)}) %collective-permute-start.15) | collective-permute-done | bytes 393248 | tf_op jit(solution)/shard_map/ppermute | solution.py:284
  106.1 2.8 %collective-permute-start.19 = (bf16[6,32,1024]{2,1,0:T(8,128)(2,1)S(1)}, bf16[6,32,1024]{2,1,0:T(8,128)(2,1)}, u32[]{:S(2)}, u32[]{:S(2)}) collective-permute-start(bf16[6,32,1024]{2,1,0:T(8,128)(2,1)S(1)} %get-tuple-element.43.refs_0_), channel_id=1, source_target_pairs={{0,16},{2,18},{4,20},{6,22},{8,24},{10,26},{12,28},{14,30},{16,0},... | collective-permute-start | bytes 1179656 | tf_op jit(solution)/shard_map/ppermute | solution.py:284
  112.2 4.7 %collective-permute-done.22 = bf16[3,32,1024]{2,1,0:T(8,128)(2,1)S(1)} collective-permute-done((bf16[3,32,1024]{2,1,0:T(8,128)(2,1)S(1)}, bf16[3,32,1024]{2,1,0:T(8,128)(2,1)S(1)}, u32[]{:S(2)}, u32[]{:S(2)}) %collective-permute-start.22) | collective-permute-done | bytes 196640 | tf_op jit(solution)/shard_map/ppermute | solution.py:277
  119.8 5.7 %collective-permute-done.19.refs_2_ = bf16[6,32,1024]{2,1,0:T(8,128)(2,1)} collective-permute-done((bf16[6,32,1024]{2,1,0:T(8,128)(2,1)S(1)}, bf16[6,32,1024]{2,1,0:T(8,128)(2,1)}, u32[]{:S(2)}, u32[]{:S(2)}) %collective-permute-start.19) | collective-permute-done | bytes 393248 | tf_op jit(solution)/shard_map/ppermute | solution.py:284
  128.3 4.9 %collective-permute-done.29.refs_12_ = bf16[6,32,1024]{2,1,0:T(8,128)(2,1)} collective-permute-done((bf16[6,32,1024]{2,1,0:T(8,128)(2,1)}, bf16[6,32,1024]{2,1,0:T(8,128)(2,1)}, u32[]{:S(2)}, u32[]{:S(2)}) %collective-permute-start.29) | collective-permute-done | bytes 393248 | tf_op jit(solution)/shard_map/ppermute | solution.py:277
  136.7 2.7 %collective-permute-start.30 = (bf16[6,32,1024]{2,1,0:T(8,128)(2,1)}, bf16[6,32,1024]{2,1,0:T(8,128)(2,1)}, u32[]{:S(2)}, u32[]{:S(2)}) collective-permute-start(bf16[6,32,1024]{2,1,0:T(8,128)(2,1)} %collective-permute-done.21.refs_5_), channel_id=1, source_target_pairs={{0,2},{2,0},{4,6},{6,4},{8,10},{10,8},{12,14},{14,12},{16,18},{18,... | collective-permute-start | bytes 1179656 | tf_op jit(solution)/shard_map/ppermute | solution.py:277
  143.4 6.7 %collective-permute-done.26.refs_9_ = bf16[6,32,1024]{2,1,0:T(8,128)(2,1)} collective-permute-done((bf16[6,32,1024]{2,1,0:T(8,128)(2,1)}, bf16[6,32,1024]{2,1,0:T(8,128)(2,1)}, u32[]{:S(2)}, u32[]{:S(2)}) %collective-permute-start.26) | collective-permute-done | bytes 393248 | tf_op jit(solution)/shard_map/ppermute | solution.py:277
  150.1 6.4 %collective-permute-done.30.refs_13_ = bf16[6,32,1024]{2,1,0:T(8,128)(2,1)} collective-permute-done((bf16[6,32,1024]{2,1,0:T(8,128)(2,1)}, bf16[6,32,1024]{2,1,0:T(8,128)(2,1)}, u32[]{:S(2)}, u32[]{:S(2)}) %collective-permute-start.30) | collective-permute-done | bytes 393248 | tf_op jit(solution)/shard_map/ppermute | solution.py:277
  156.6 3.9 %collective-permute-done.31.refs_14_ = bf16[6,32,1024]{2,1,0:T(8,128)(2,1)} collective-permute-done((bf16[6,32,1024]{2,1,0:T(8,128)(2,1)}, bf16[6,32,1024]{2,1,0:T(8,128)(2,1)}, u32[]{:S(2)}, u32[]{:S(2)}) %collective-permute-start.31) | collective-permute-done | bytes 393248 | tf_op jit(solution)/shard_map/ppermute | solution.py:280
  161.5 5.0 %shard_map.84 = (bf16[3,512,1024]{2,1,0:T(8,128)(2,1)S(1)}, bf16[3,512,512]{2,1,0:T(8,128)(2,1)S(1)}) custom-call(s32[3]{0:T(128)S(1)} %get-tuple-element.75.order_ref, bf16[6,32,1024]{2,1,0:T(8,128)(2,1)S(1)} %get-tuple-element.43.refs_0_, bf16[6,32,1024]{2,1,0:T(8,128)(2,1)S(1)} %copy-done.7, bf16[6,32,1024]{2,1,0:T(8,128)(2,1)} %collective-permute-done.19.refs_2_, ...), custom_call_target="tpu_custom_call" | custom-call | flops 1610612736 | bytes 7864320 | tf_op jit(solution)/shard_map/pallas_call | solution.py:58
  169.9 2.8 %collective-permute-start.34 = (bf16[2,3,32,1024]{3,2,1,0:T(8,128)(2,1)S(1)}, bf16[2,3,32,1024]{3,2,1,0:T(8,128)(2,1)S(1)}, u32[]{:S(2)}, u32[]{:S(2)}) collective-permute-start(bf16[2,3,32,1024]{3,2,1,0:T(8,128)(2,1)S(1)} %slice.31), channel_id=1, source_target_pairs={{0,2},{2,0},{4,6},{6,4},{8,10},{10,8},{12,14},{14,12},{16,18},{18,... | collective-permute-start | bytes 1179656 | tf_op jit(solution)/shard_map/ppermute | solution.py:277
  172.8 4.8 %shard_map.83 = (bf16[3,512,1024]{2,1,0:T(8,128)(2,1)S(1)}, bf16[3,512,512]{2,1,0:T(8,128)(2,1)S(1)}) custom-call(s32[3]{0:T(128)S(1)} %get-tuple-element.76.order_ref, bf16[6,32,1024]{2,1,0:T(8,128)(2,1)S(1)} %get-tuple-element.43.refs_0_, bf16[6,32,1024]{2,1,0:T(8,128)(2,1)S(1)} %copy-done.7, bf16[6,32,1024]{2,1,0:T(8,128)(2,1)} %collective-permute-done.19.refs_2_, ...), custom_call_target="tpu_custom_call" | custom-call | flops 1610612736 | bytes 7864320 | tf_op jit(solution)/shard_map/pallas_call | solution.py:58
  179.3 10.5 %shard_map.85 = (bf16[3,512,512]{2,1,0:T(8,128)(2,1)}, f32[3,8,128]{2,1,0:T(8,128)S(1)}) custom-call(bf16[3,512,512]{2,1,0:T(8,128)(2,1)S(1)} %get-tuple-element.45.refs_0_, bf16[3,512,512]{2,1,0:T(8,128)(2,1)S(1)} %collective-permute-done.33.refs_1_), custom_call_target="tpu_custom_call" | custom-call | flops 7247757312 | bytes 4718592 | tf_op jit(solution)/shard_map/pallas_call | solution.py:133
  204.6 11.7 %shard_map.86 = (bf16[6,512,1024]{2,1,0:T(8,128)(2,1)}, f32[6,32,1024]{2,1,0:T(8,128)}, bf16[2,512,1024]{2,1,0:T(8,128)(2,1)}, f32[1,2]{1,0:T(1,128)}) custom-call(s32[16]{0:T(128)S(1)} %copy-done.12, s32[16]{0:T(128)S(1)} %copy-done.13, s32[6]{0:T(128)S(1)} %copy-done.14, s32[6]{0:T(128)S(1)} %and_select_fusion.order_ref, ...), custom_call_target="tpu_custom_call" | custom-call | flops 3221225472 | bytes 28311552 | tf_op jit(solution)/shard_map/pallas_call | solution.py:228
  (116 shorter events, 69.8 us)
Async XLA Ops:
  7.2 59.5 %all-gather.5.cloned.1.call-start = ((), (), s32[]{:S(2)}) async-start(), calls=%async_computation | async-start | bytes 1966080 | tf_op jit(solution)/shard_map/all_gather | solution.py:306
  9.2 185.9 %all-gather.7.cloned.1.call-start = ((), (), s32[]{:S(2)}) async-start(), calls=%async_computation.1 | async-start | bytes 3932160 | tf_op jit(solution)/shard_map/all_gather | solution.py:320
  17.6 17.3 %collective-permute-start.1 = (bf16[6,32,1024]{2,1,0:T(8,128)(2,1)S(1)}, bf16[6,32,1024]{2,1,0:T(8,128)(2,1)S(1)}, u32[]{:S(2)}, u32[]{:S(2)}) collective-permute-start(bf16[6,32,1024]{2,1,0:T(8,128)(2,1)S(1)} %get-tuple-element.65), channel_id=1, source_target_pairs={{0,2},{2,0},{4,6},{6,4},{8,10},{10,8},{12,14},{14,12},{16,18},{18,... | collective-permute-start | bytes 1179656 | tf_op jit(solution)/shard_map/ppermute | solution.py:277
  18.2 16.7 %collective-permute-start = (bf16[6,32,1024]{2,1,0:T(8,128)(2,1)S(1)}, bf16[6,32,1024]{2,1,0:T(8,128)(2,1)}, u32[]{:S(2)}, u32[]{:S(2)}) collective-permute-start(bf16[6,32,1024]{2,1,0:T(8,128)(2,1)S(1)} %get-tuple-element.66), channel_id=1, source_target_pairs={{0,4},{2,6},{4,0},{6,2},{8,12},{10,14},{12,8},{14,10},{16,20},{18,... | collective-permute-start | bytes 1179656 | tf_op jit(solution)/shard_map/ppermute | solution.py:280
  18.3 23.1 %collective-permute-start.9 = (bf16[6,32,1024]{2,1,0:T(8,128)(2,1)S(1)}, bf16[6,32,1024]{2,1,0:T(8,128)(2,1)}, u32[]{:S(2)}, u32[]{:S(2)}) collective-permute-start(bf16[6,32,1024]{2,1,0:T(8,128)(2,1)S(1)} %get-tuple-element.62), channel_id=1, source_target_pairs={{0,4},{2,6},{4,0},{6,2},{8,12},{10,14},{12,8},{14,10},{16,20},{18,... | collective-permute-start | bytes 1179656 | tf_op jit(solution)/shard_map/ppermute | solution.py:280
  29.2 20.6 %collective-permute-start.8 = (bf16[6,32,1024]{2,1,0:T(8,128)(2,1)}, bf16[6,32,1024]{2,1,0:T(8,128)(2,1)}, u32[]{:S(2)}, u32[]{:S(2)}) collective-permute-start(bf16[6,32,1024]{2,1,0:T(8,128)(2,1)} %get-tuple-element.69), channel_id=1, source_target_pairs={{0,4},{2,6},{4,0},{6,2},{8,12},{10,14},{12,8},{14,10},{16,20},{18,... | collective-permute-start | bytes 1179656 | tf_op jit(solution)/shard_map/ppermute | solution.py:280
  29.2 14.3 %collective-permute-start.6 = (bf16[6,32,1024]{2,1,0:T(8,128)(2,1)}, bf16[6,32,1024]{2,1,0:T(8,128)(2,1)}, u32[]{:S(2)}, u32[]{:S(2)}) collective-permute-start(bf16[6,32,1024]{2,1,0:T(8,128)(2,1)} %get-tuple-element.70), channel_id=1, source_target_pairs={{0,2},{2,0},{4,6},{6,4},{8,10},{10,8},{12,14},{14,12},{16,18},{18,... | collective-permute-start | bytes 1179656 | tf_op jit(solution)/shard_map/ppermute | solution.py:277
  37.1 14.7 %collective-permute-start.4 = (bf16[6,32,1024]{2,1,0:T(8,128)(2,1)}, bf16[6,32,1024]{2,1,0:T(8,128)(2,1)S(1)}, u32[]{:S(2)}, u32[]{:S(2)}) collective-permute-start(bf16[6,32,1024]{2,1,0:T(8,128)(2,1)} %fusion.11), channel_id=1, source_target_pairs={{0,2},{2,0},{4,6},{6,4},{8,10},{10,8},{12,14},{14,12},{16,18},{18,... | collective-permute-start | bytes 1179656 | tf_op jit(solution)/shard_map/ppermute | solution.py:277
  38.7 18.7 %collective-permute-start.5 = (bf16[6,32,1024]{2,1,0:T(8,128)(2,1)S(1)}, bf16[6,32,1024]{2,1,0:T(8,128)(2,1)S(1)}, u32[]{:S(2)}, u32[]{:S(2)}) collective-permute-start(bf16[6,32,1024]{2,1,0:T(8,128)(2,1)S(1)} %get-tuple-element.35), channel_id=1, source_target_pairs={{0,4},{2,6},{4,0},{6,2},{8,12},{10,14},{12,8},{14,10},{16,20},{18,... | collective-permute-start | bytes 1179656 | tf_op jit(solution)/shard_map/ppermute | solution.py:280
  43.5 16.7 %collective-permute-start.7 = (bf16[6,32,1024]{2,1,0:T(8,128)(2,1)S(1)}, bf16[6,32,1024]{2,1,0:T(8,128)(2,1)S(1)}, u32[]{:S(2)}, u32[]{:S(2)}) collective-permute-start(bf16[6,32,1024]{2,1,0:T(8,128)(2,1)S(1)} %get-tuple-element.36), channel_id=1, source_target_pairs={{0,2},{2,0},{4,6},{6,4},{8,10},{10,8},{12,14},{14,12},{16,18},{18,... | collective-permute-start | bytes 1179656 | tf_op jit(solution)/shard_map/ppermute | solution.py:277
  46.4 28.7 %collective-permute-start.10 = (bf16[6,32,1024]{2,1,0:T(8,128)(2,1)S(1)}, bf16[6,32,1024]{2,1,0:T(8,128)(2,1)S(1)}, u32[]{:S(2)}, u32[]{:S(2)}) collective-permute-start(bf16[6,32,1024]{2,1,0:T(8,128)(2,1)S(1)} %fusion.10), channel_id=1, source_target_pairs={{0,16},{2,18},{4,20},{6,22},{8,24},{10,26},{12,28},{14,30},{16,0},... | collective-permute-start | bytes 1179656 | tf_op jit(solution)/shard_map/ppermute | solution.py:284
  54.0 22.2 %collective-permute-start.13 = (bf16[6,32,1024]{2,1,0:T(8,128)(2,1)}, bf16[6,32,1024]{2,1,0:T(8,128)(2,1)}, u32[]{:S(2)}, u32[]{:S(2)}) collective-permute-start(bf16[6,32,1024]{2,1,0:T(8,128)(2,1)} %fusion.8), channel_id=1, source_target_pairs={{0,8},{2,10},{4,12},{6,14},{8,16},{10,18},{12,20},{14,22},{16,24},... | collective-permute-start | bytes 1179656 | tf_op jit(solution)/shard_map/ppermute | solution.py:284
  55.6 22.2 %collective-permute-start.11 = (bf16[6,32,1024]{2,1,0:T(8,128)(2,1)S(1)}, bf16[6,32,1024]{2,1,0:T(8,128)(2,1)}, u32[]{:S(2)}, u32[]{:S(2)}) collective-permute-start(bf16[6,32,1024]{2,1,0:T(8,128)(2,1)S(1)} %get-tuple-element.41), channel_id=1, source_target_pairs={{0,2},{2,0},{4,6},{6,4},{8,10},{10,8},{12,14},{14,12},{16,18},{18,... | collective-permute-start | bytes 1179656 | tf_op jit(solution)/shard_map/ppermute | solution.py:277
  62.6 15.2 %collective-permute-start.12 = (bf16[6,32,1024]{2,1,0:T(8,128)(2,1)}, bf16[6,32,1024]{2,1,0:T(8,128)(2,1)}, u32[]{:S(2)}, u32[]{:S(2)}) collective-permute-start(bf16[6,32,1024]{2,1,0:T(8,128)(2,1)} %get-tuple-element.67), channel_id=1, source_target_pairs={{0,4},{2,6},{4,0},{6,2},{8,12},{10,14},{12,8},{14,10},{16,20},{18,... | collective-permute-start | bytes 1179656 | tf_op jit(solution)/shard_map/ppermute | solution.py:280
  62.7 20.1 %collective-permute-start.14 = (bf16[6,32,1024]{2,1,0:T(8,128)(2,1)}, bf16[6,32,1024]{2,1,0:T(8,128)(2,1)}, u32[]{:S(2)}, u32[]{:S(2)}) collective-permute-start(bf16[6,32,1024]{2,1,0:T(8,128)(2,1)} %get-tuple-element.68), channel_id=1, source_target_pairs={{0,24},{2,26},{4,28},{6,30},{8,0},{10,2},{12,4},{14,6},{16,8},{18,... | collective-permute-start | bytes 1179656 | tf_op jit(solution)/shard_map/ppermute | solution.py:284
  75.1 30.3 %collective-permute-start.18 = (bf16[5,3,32,1024]{3,2,1,0:T(8,128)(2,1)}, bf16[5,3,32,1024]{3,2,1,0:T(8,128)(2,1)S(1)}, u32[]{:S(2)}, u32[]{:S(2)}) collective-permute-start(bf16[5,3,32,1024]{3,2,1,0:T(8,128)(2,1)} %pad_maximum_fusion), channel_id=1, source_target_pairs={{0,4},{2,6},{4,0},{6,2},{8,12},{10,14},{12,8},{14,10},{16,20},{18,... | collective-permute-start | bytes 2949128 | tf_op jit(solution)/shard_map/ppermute | solution.py:280
  76.2 29.2 %collective-permute-start.17 = (bf16[5,3,32,1024]{3,2,1,0:T(8,128)(2,1)}, bf16[5,3,32,1024]{3,2,1,0:T(8,128)(2,1)S(1)}, u32[]{:S(2)}, u32[]{:S(2)}) collective-permute-start(bf16[5,3,32,1024]{3,2,1,0:T(8,128)(2,1)} %pad_maximum_fusion), channel_id=1, source_target_pairs={{0,2},{2,0},{4,6},{6,4},{8,10},{10,8},{12,14},{14,12},{16,18},{18,... | collective-permute-start | bytes 2949128 | tf_op jit(solution)/shard_map/ppermute | solution.py:277
  85.9 13.8 %collective-permute-start.16 = (bf16[6,32,1024]{2,1,0:T(8,128)(2,1)S(1)}, bf16[6,32,1024]{2,1,0:T(8,128)(2,1)S(1)}, u32[]{:S(2)}, u32[]{:S(2)}) collective-permute-start(bf16[6,32,1024]{2,1,0:T(8,128)(2,1)S(1)} %get-tuple-element.43.refs_0_), channel_id=1, source_target_pairs={{0,8},{2,10},{4,12},{6,14},{8,16},{10,18},{12,20},{14,22},{16,24},... | collective-permute-start | bytes 1179656 | tf_op jit(solution)/shard_map/ppermute | solution.py:284
  86.5 18.9 %collective-permute-start.15 = (bf16[6,32,1024]{2,1,0:T(8,128)(2,1)S(1)}, bf16[6,32,1024]{2,1,0:T(8,128)(2,1)S(1)}, u32[]{:S(2)}, u32[]{:S(2)}) collective-permute-start(bf16[6,32,1024]{2,1,0:T(8,128)(2,1)S(1)} %get-tuple-element.43.refs_0_), channel_id=1, source_target_pairs={{0,24},{2,26},{4,28},{6,30},{8,0},{10,2},{12,4},{14,6},{16,8},{18,... | collective-permute-start | bytes 1179656 | tf_op jit(solution)/shard_map/ppermute | solution.py:284
  89.7 37.3 %collective-permute-start.25 = (bf16[6,32,1024]{2,1,0:T(8,128)(2,1)S(1)}, bf16[6,32,1024]{2,1,0:T(8,128)(2,1)}, u32[]{:S(2)}, u32[]{:S(2)}) collective-permute-start(bf16[6,32,1024]{2,1,0:T(8,128)(2,1)S(1)} %get-tuple-element.43.refs_0_), channel_id=1, source_target_pairs={{0,2},{2,0},{4,6},{6,4},{8,10},{10,8},{12,14},{14,12},{16,18},{18,... | collective-permute-start | bytes 1179656 | tf_op jit(solution)/shard_map/ppermute | solution.py:277
  106.1 19.4 %collective-permute-start.19 = (bf16[6,32,1024]{2,1,0:T(8,128)(2,1)S(1)}, bf16[6,32,1024]{2,1,0:T(8,128)(2,1)}, u32[]{:S(2)}, u32[]{:S(2)}) collective-permute-start(bf16[6,32,1024]{2,1,0:T(8,128)(2,1)S(1)} %get-tuple-element.43.refs_0_), channel_id=1, source_target_pairs={{0,16},{2,18},{4,20},{6,22},{8,24},{10,26},{12,28},{14,30},{16,0},... | collective-permute-start | bytes 1179656 | tf_op jit(solution)/shard_map/ppermute | solution.py:284
  110.1 24.6 %collective-permute-start.28 = (bf16[6,32,1024]{2,1,0:T(8,128)(2,1)S(1)}, bf16[6,32,1024]{2,1,0:T(8,128)(2,1)}, u32[]{:S(2)}, u32[]{:S(2)}) collective-permute-start(bf16[6,32,1024]{2,1,0:T(8,128)(2,1)S(1)} %collective-permute-done.16.refs_3_), channel_id=1, source_target_pairs={{0,2},{2,0},{4,6},{6,4},{8,10},{10,8},{12,14},{14,12},{16,18},{18,... | collective-permute-start | bytes 1179656 | tf_op jit(solution)/shard_map/ppermute | solution.py:277
  111.1 28.3 %collective-permute-start.24 = (bf16[6,32,1024]{2,1,0:T(8,128)(2,1)S(1)}, bf16[6,32,1024]{2,1,0:T(8,128)(2,1)}, u32[]{:S(2)}, u32[]{:S(2)}) collective-permute-start(bf16[6,32,1024]{2,1,0:T(8,128)(2,1)S(1)} %collective-permute-done.16.refs_3_), channel_id=1, source_target_pairs={{0,4},{2,6},{4,0},{6,2},{8,12},{10,14},{12,8},{14,10},{16,20},{18,... | collective-permute-start | bytes 1179656 | tf_op jit(solution)/shard_map/ppermute | solution.py:280
  116.9 16.4 %collective-permute-start.29 = (bf16[6,32,1024]{2,1,0:T(8,128)(2,1)}, bf16[6,32,1024]{2,1,0:T(8,128)(2,1)}, u32[]{:S(2)}, u32[]{:S(2)}) collective-permute-start(bf16[6,32,1024]{2,1,0:T(8,128)(2,1)} %collective-permute-done.20.refs_4_), channel_id=1, source_target_pairs={{0,2},{2,0},{4,6},{6,4},{8,10},{10,8},{12,14},{14,12},{16,18},{18,... | collective-permute-start | bytes 1179656 | tf_op jit(solution)/shard_map/ppermute | solution.py:277
  127.0 14.7 %collective-permute-start.27 = (bf16[6,32,1024]{2,1,0:T(8,128)(2,1)}, bf16[6,32,1024]{2,1,0:T(8,128)(2,1)}, u32[]{:S(2)}, u32[]{:S(2)}) collective-permute-start(bf16[6,32,1024]{2,1,0:T(8,128)(2,1)} %collective-permute-done.19.refs_2_), channel_id=1, source_target_pairs={{0,2},{2,0},{4,6},{6,4},{8,10},{10,8},{12,14},{14,12},{16,18},{18,... | collective-permute-start | bytes 1179656 | tf_op jit(solution)/shard_map/ppermute | solution.py:277
  133.3 16.9 %collective-permute-start.26 = (bf16[6,32,1024]{2,1,0:T(8,128)(2,1)}, bf16[6,32,1024]{2,1,0:T(8,128)(2,1)}, u32[]{:S(2)}, u32[]{:S(2)}) collective-permute-start(bf16[6,32,1024]{2,1,0:T(8,128)(2,1)} %copy-done.6), channel_id=1, source_target_pairs={{0,2},{2,0},{4,6},{6,4},{8,10},{10,8},{12,14},{14,12},{16,18},{18,... | collective-permute-start | bytes 1179656 | tf_op jit(solution)/shard_map/ppermute | solution.py:277
  134.7 15.4 %collective-permute-start.32 = (bf16[6,32,1024]{2,1,0:T(8,128)(2,1)}, bf16[6,32,1024]{2,1,0:T(8,128)(2,1)}, u32[]{:S(2)}, u32[]{:S(2)}) collective-permute-start(bf16[6,32,1024]{2,1,0:T(8,128)(2,1)} %collective-permute-done.28.refs_11_), channel_id=1, source_target_pairs={{0,4},{2,6},{4,0},{6,2},{8,12},{10,14},{12,8},{14,10},{16,20},{18,... | collective-permute-start | bytes 1179656 | tf_op jit(solution)/shard_map/ppermute | solution.py:280
  136.7 19.8 %collective-permute-start.30 = (bf16[6,32,1024]{2,1,0:T(8,128)(2,1)}, bf16[6,32,1024]{2,1,0:T(8,128)(2,1)}, u32[]{:S(2)}, u32[]{:S(2)}) collective-permute-start(bf16[6,32,1024]{2,1,0:T(8,128)(2,1)} %collective-permute-done.21.refs_5_), channel_id=1, source_target_pairs={{0,2},{2,0},{4,6},{6,4},{8,10},{10,8},{12,14},{14,12},{16,18},{18,... | collective-permute-start | bytes 1179656 | tf_op jit(solution)/shard_map/ppermute | solution.py:277
  139.4 17.1 %collective-permute-start.23 = (bf16[6,32,1024]{2,1,0:T(8,128)(2,1)}, bf16[6,32,1024]{2,1,0:T(8,128)(2,1)}, u32[]{:S(2)}, u32[]{:S(2)}) collective-permute-start(bf16[6,32,1024]{2,1,0:T(8,128)(2,1)} %collective-permute-done.19.refs_2_), channel_id=1, source_target_pairs={{0,4},{2,6},{4,0},{6,2},{8,12},{10,14},{12,8},{14,10},{16,20},{18,... | collective-permute-start | bytes 1179656 | tf_op jit(solution)/shard_map/ppermute | solution.py:280
  141.7 18.8 %collective-permute-start.31 = (bf16[6,32,1024]{2,1,0:T(8,128)(2,1)}, bf16[6,32,1024]{2,1,0:T(8,128)(2,1)}, u32[]{:S(2)}, u32[]{:S(2)}) collective-permute-start(bf16[6,32,1024]{2,1,0:T(8,128)(2,1)} %collective-permute-done.27.refs_10_), channel_id=1, source_target_pairs={{0,4},{2,6},{4,0},{6,2},{8,12},{10,14},{12,8},{14,10},{16,20},{18,... | collective-permute-start | bytes 1179656 | tf_op jit(solution)/shard_map/ppermute | solution.py:280
  168.2 21.6 %collective-permute-start.35 = (bf16[2,3,32,1024]{3,2,1,0:T(8,128)(2,1)S(1)}, bf16[2,3,32,1024]{3,2,1,0:T(8,128)(2,1)S(1)}, u32[]{:S(2)}, u32[]{:S(2)}) collective-permute-start(bf16[2,3,32,1024]{3,2,1,0:T(8,128)(2,1)S(1)} %slice.32), channel_id=1, source_target_pairs={{0,4},{2,6},{4,0},{6,2},{8,12},{10,14},{12,8},{14,10},{16,20},{18,... | collective-permute-start | bytes 1179656 | tf_op jit(solution)/shard_map/ppermute | solution.py:280
  169.9 20.6 %collective-permute-start.34 = (bf16[2,3,32,1024]{3,2,1,0:T(8,128)(2,1)S(1)}, bf16[2,3,32,1024]{3,2,1,0:T(8,128)(2,1)S(1)}, u32[]{:S(2)}, u32[]{:S(2)}) collective-permute-start(bf16[2,3,32,1024]{3,2,1,0:T(8,128)(2,1)S(1)} %slice.31), channel_id=1, source_target_pairs={{0,2},{2,0},{4,6},{6,4},{8,10},{10,8},{12,14},{14,12},{16,18},{18,... | collective-permute-start | bytes 1179656 | tf_op jit(solution)/shard_map/ppermute | solution.py:277
  (27 other events, 187.9 us)
Sparse Core Ops, SparseCore 0:
  9.6 41.3 all-gather.4
  128.5 61.3 all-gather.6

commit v3 on v2

--- a/solution.py
+++ b/solution.py
@@ -70,7 +70,7 @@
             jax.ShapeDtypeStruct((count, rows, width), jnp.bfloat16),
             jax.ShapeDtypeStruct((count, rows, rows), jnp.bfloat16),
         ],
-        compiler_params=pltpu.CompilerParams(vmem_limit_bytes=9 * MIB),
+        compiler_params=pltpu.CompilerParams(vmem_limit_bytes=56 * MIB),
         cost_estimate=pl.CostEstimate(
             flops=2 * count * rows * rows * width,
             bytes_accessed=2 * count * rows * (2 * width + rows),
@@ -249,7 +249,7 @@
             jax.ShapeDtypeStruct(owned, jnp.bfloat16),
             jax.ShapeDtypeStruct((1, MOST), jnp.float32),
         ],
-        compiler_params=pltpu.CompilerParams(vmem_limit_bytes=20 * MIB),
+        compiler_params=pltpu.CompilerParams(vmem_limit_bytes=56 * MIB),
         cost_estimate=pl.CostEstimate(
             flops=2 * count * rows * rows * width,
             bytes_accessed=2 * count * rows * (4 * width + rows),
@@ -321,22 +321,15 @@
         self.low = low.reshape(4 * LINE, *low.shape[2:])
 
     def high_corners(self, *ties):
-        near_y = after(self.near_y, *ties)
-        near_x = after(self.near_x, *ties)
-        self.far_x = self.grid.over_x(near_y[: LINE // 2])
-        self.far_y = self.grid.over_y(near_x[LINE // 2 : LINE])
+        self.far = self.grid.over_x(after(self.near_y, *ties)[:LINE])
 
     def pieces(self):
-        high = [self.high, self.near_y, self.near_x, self.far_x, self.far_y]
-        depths = [LINE, LINE, LINE, LINE // 2, LINE // 2]
-        return [(self.low, 0, 4 * LINE)] + [
-            (piece, self.split, depth) for piece, depth in zip(high, depths)
-        ]
+        high = [self.high, self.near_y, self.near_x, self.far]
+        return [(self.low, 0, 4 * LINE)] + [(piece, self.split, LINE) for piece in high]
 
     def masters(self, matrices):
         low = [(0, z * 4 + at) for at in range(4) for z in range(LINE)]
-        high = [(piece, z) for piece in (1, 2, 3) for z in range(LINE)]
-        high += [(4 + z // 2, z % 2) for z in range(LINE)]
+        high = [(piece, z) for piece in (1, 2, 3, 4) for z in range(LINE)]
         return [(0, self.split, low), (self.split, matrices, high)]
 
     def places(self):
@@ -462,7 +455,7 @@
         chain, squares = chains([my_gram, other_part])
         sent = chain
         if in_pieces:
-            sent = after(chain, master_gather.far_x, master_gather.far_y)
+            sent = after(chain, master_gather.far)
         other = [lax.ppermute(sent, "col", swap), lax.ppermute(squares, "col", swap)]
         sets = [[chain, squares, my_update], [*other, their_update]]
     else:

time: 224 us -> 214 us (0.955)
  local copies, waits for them, and re-layouts: 22.7 us -> 11.3 us
  Pallas kernels: 32.1 us -> 35.6 us
    unnamed x38 -> x32, local copies, waits for them, and re-layouts: 16.1 us -> 3.37 us
    pallas_call x1, Pallas kernels: 11.7 us -> 14.4 us  [applied(): pl.pallas_call(functools.partial(apply_kernel, len(sets), first_count, ma...]
    ppermute x14 -> x13, waiting for transfers between devices: 11.7 us -> 10.1 us  [over_y(): return lax.ppermute(value, 'dp', self.y_pairs)]
    ppermute x14 -> x13, starting transfers between devices: 17 us -> 16.2 us  [over_y(): return lax.ppermute(value, 'dp', self.y_pairs)]
  transfers between devices with their start and end apart: 40 -> 39, of which waited for: 23 -> 23; matrix products, arithmetic and copies ran while one was open for 11% -> 12% of each run, Pallas kernels for 9% -> 10%
where the time goes in v3:
time: 214 us; the launch traced here: 213 us
  waiting for transfers between devices  79.3 us (37%)
  starting transfers between devices  53.5 us (25%)
  Pallas kernels  35.6 us (17%)
  other arithmetic  19.1 us (9%)
  between operations  14.3 us (7%)
  local copies, waits for them, and re-layouts  11.3 us (5%)
    ppermute x15, waiting for transfers between devices, over_x(): return lax.ppermute(value, 'dp', self.x_pairs)  37.3 us
    ppermute x6, waiting for transfers between devices, over_z(): return lax.ppermute(value, 'dp', pairs)  31.1 us
    ppermute x15, starting transfers between devices, over_x(): return lax.ppermute(value, 'dp', self.x_pairs)  22.3 us
    convert_element_type x7, other arithmetic, half(): return value.astype(jnp.bfloat16)  16.3 us
    ppermute x13, starting transfers between devices, over_y(): return lax.ppermute(value, 'dp', self.y_pairs)  16.2 us
    ppermute x6, starting transfers between devices, over_z(): return lax.ppermute(value, 'dp', pairs)  14.8 us
    pallas_call x1, Pallas kernels, applied(): pl.pallas_call(functools.partial(apply_kernel, len(sets), first_count, ma...  14.4 us
    pallas_call x2, Pallas kernels, grams(): pl.pallas_call(gram_kernel, grid_spec=pltpu.PrefetchScalarGridSpec(num_sc...  12 us
  transfers between devices with their start and end apart: 39, of which 23 were waited for; matrix products, arithmetic and copies ran while one was open for 12% of the time, Pallas kernels for 10%

profile of v3, /device:TPU:0, one launch (start us, length us, event | category | flops | bytes accessed | tf_op | source)
XLA Modules:
  0.0 213.1 jit_solution(8757829713622245966)
XLA Ops:
  10.5 3.0 %collective-permute-start.3 = (bf16[6,32,1024]{2,1,0:T(8,128)(2,1)S(1)}, bf16[6,32,1024]{2,1,0:T(8,128)(2,1)}, u32[]{:S(2)}, u32[]{:S(2)}) collective-permute-start(bf16[6,32,1024]{2,1,0:T(8,128)(2,1)S(1)} %get-tuple-element.69), channel_id=1, source_target_pairs={{0,4},{2,6},{4,0},{6,2},{8,12},{10,14},{12,8},{14,10},{16,20},{18,... | collective-permute-start | bytes 1179656 | tf_op jit(solution)/shard_map/ppermute | solution.py:280
  15.0 2.6 %dynamic-slice_bitcast_fusion = (bf16[6,32,1024]{2,1,0:T(8,128)(2,1)S(1)}, bf16[6,32,1024]{2,1,0:T(8,128)(2,1)S(1)}, bf16[6,32,1024]{2,1,0:T(8,128)(2,1)S(1)}, b...) fusion(bf16[1,6,512,1024]{3,2,1,0:T(8,128)(2,1)} %param.4, ...), kind=kLoop, calls=%fused_computation.26 | loop fusion | bytes 4718616 | tf_op jit(solution)/shard_map/dynamic_slice | solution.py:347
  20.2 3.4 %collective-permute-done.3 = bf16[6,32,1024]{2,1,0:T(8,128)(2,1)} collective-permute-done((bf16[6,32,1024]{2,1,0:T(8,128)(2,1)S(1)}, bf16[6,32,1024]{2,1,0:T(8,128)(2,1)}, u32[]{:S(2)}, u32[]{:S(2)}) %collective-permute-start.3) | collective-permute-done | bytes 393248 | tf_op jit(solution)/shard_map/ppermute | solution.py:280
  23.6 2.1 collective-permute-done.2
  25.7 2.6 %fusion.12 = (bf16[6,32,1024]{2,1,0:T(8,128)(2,1)}, bf16[6,32,1024]{2,1,0:T(8,128)(2,1)}) fusion(bf16[6,32,1024]{2,1,0:T(8,128)(2,1)} %collective-permute-done.2, bf16[1,6,512,1024]{3,2,1,0:T(8,128)(2,1)} %param.4, s32[]{:T(128)S(6)} %select_n.67, bf16[6,32,1024]{2,1,0:T(8,128)(2,1)} %collective-permute-done.3, s32[]{:T(128)S(6)} %select_n.66), kind=kLoop, calls=%fused_computation.21 | loop fusion | flops 1572864 | bytes 2359304 | tf_op jit(solution)/shard_map/convert_element_type | solution.py:33
  30.3 3.8 %collective-permute-done.1 = bf16[6,32,1024]{2,1,0:T(8,128)(2,1)} collective-permute-done((bf16[6,32,1024]{2,1,0:T(8,128)(2,1)}, bf16[6,32,1024]{2,1,0:T(8,128)(2,1)}, u32[]{:S(2)}, u32[]{:S(2)}) %collective-permute-start.1) | collective-permute-done | bytes 393248 | tf_op jit(solution)/shard_map/ppermute | solution.py:277
  38.2 2.2 %collective-permute-done.9 = bf16[6,32,1024]{2,1,0:T(8,128)(2,1)} collective-permute-done((bf16[6,32,1024]{2,1,0:T(8,128)(2,1)S(1)}, bf16[6,32,1024]{2,1,0:T(8,128)(2,1)}, u32[]{:S(2)}, u32[]{:S(2)}) %collective-permute-start.9) | collective-permute-done | bytes 393248 | tf_op jit(solution)/shard_map/ppermute | solution.py:280
  40.4 2.1 collective-permute-done.6
  44.0 2.2 %fusion.10 = bf16[6,32,1024]{2,1,0:T(8,128)(2,1)} fusion(bf16[6,32,1024]{2,1,0:T(8,128)(2,1)} %collective-permute-done.9, bf16[6,32,1024]{2,1,0:T(8,128)(2,1)} %collective-permute-done.6, bf16[1,6,512,1024]{3,2,1,0:T(8,128)(2,1)} %param.4, s32[]{:T(128)S(6)} %select_n.71), kind=kLoop, calls=%fused_computation.17 | loop fusion | flops 1179648 | bytes 1572868 | tf_op jit(solution)/shard_map/convert_element_type | solution.py:33
  46.2 2.6 %collective-permute-start.10 = (bf16[6,32,1024]{2,1,0:T(8,128)(2,1)}, bf16[6,32,1024]{2,1,0:T(8,128)(2,1)}, u32[]{:S(2)}, u32[]{:S(2)}) collective-permute-start(bf16[6,32,1024]{2,1,0:T(8,128)(2,1)} %fusion.10), channel_id=1, source_target_pairs={{0,16},{2,18},{4,20},{6,22},{8,24},{10,26},{12,28},{14,30},{16,0},... | collective-permute-start | bytes 1179656 | tf_op jit(solution)/shard_map/ppermute | solution.py:284
  50.9 2.2 %fusion.8 = bf16[6,32,1024]{2,1,0:T(8,128)(2,1)} fusion(bf16[6,32,1024]{2,1,0:T(8,128)(2,1)} %collective-permute-done.8, bf16[6,32,1024]{2,1,0:T(8,128)(2,1)} %collective-permute-done.1, bf16[1,6,512,1024]{3,2,1,0:T(8,128)(2,1)} %param.4, s32[]{:T(128)S(6)} %select_n.72), kind=kLoop, calls=%fused_computation.14 | loop fusion | flops 1179648 | bytes 1572868 | tf_op jit(solution)/shard_map/convert_element_type | solution.py:33
  56.4 2.9 %collective-permute-done.7 = bf16[6,32,1024]{2,1,0:T(8,128)(2,1)S(1)} collective-permute-done((bf16[6,32,1024]{2,1,0:T(8,128)(2,1)S(1)}, bf16[6,32,1024]{2,1,0:T(8,128)(2,1)S(1)}, u32[]{:S(2)}, u32[]{:S(2)}) %collective-permute-start.7) | collective-permute-done | bytes 393248 | tf_op jit(solution)/shard_map/ppermute | solution.py:277
  59.3 2.3 %fusion.4 = (bf16[6,32,1024]{2,1,0:T(8,128)(2,1)}, bf16[6,32,1024]{2,1,0:T(8,128)(2,1)}) fusion(bf16[6,32,1024]{2,1,0:T(8,128)(2,1)S(1)} %collective-permute-done.7, bf16[1,6,512,1024]{3,2,1,0:T(8,128)(2,1)} %param.4, s32[]{:T(128)S(6)} %select_n.74, bf16[6,32,1024]{2,1,0:T(8,128)(2,1)S(1)} %collective-permute-done.5, ...), kind=kLoop, calls=%fused_computation.8 | loop fusion | flops 1966080 | bytes 2752520 | tf_op jit(solution)/shard_map/convert_element_type | solution.py:33
  61.8 3.9 %collective-permute-start.14 = (bf16[6,32,1024]{2,1,0:T(8,128)(2,1)}, bf16[6,32,1024]{2,1,0:T(8,128)(2,1)}, u32[]{:S(2)}, u32[]{:S(2)}) collective-permute-start(bf16[6,32,1024]{2,1,0:T(8,128)(2,1)} %get-tuple-element.66), channel_id=1, source_target_pairs={{0,24},{2,26},{4,28},{6,30},{8,0},{10,2},{12,4},{14,6},{16,8},{18,... | collective-permute-start | bytes 1179656 | tf_op jit(solution)/shard_map/ppermute | solution.py:284
  68.1 7.2 %collective-permute-done.10 = bf16[6,32,1024]{2,1,0:T(8,128)(2,1)} collective-permute-done((bf16[6,32,1024]{2,1,0:T(8,128)(2,1)}, bf16[6,32,1024]{2,1,0:T(8,128)(2,1)}, u32[]{:S(2)}, u32[]{:S(2)}) %collective-permute-start.10) | collective-permute-done | bytes 393248 | tf_op jit(solution)/shard_map/ppermute | solution.py:284
  77.9 4.9 %collective-permute-done.14 = bf16[6,32,1024]{2,1,0:T(8,128)(2,1)} collective-permute-done((bf16[6,32,1024]{2,1,0:T(8,128)(2,1)}, bf16[6,32,1024]{2,1,0:T(8,128)(2,1)}, u32[]{:S(2)}, u32[]{:S(2)}) %collective-permute-start.14) | collective-permute-done | bytes 393248 | tf_op jit(solution)/shard_map/ppermute | solution.py:284
  82.8 3.0 %add_convert_fusion = (bf16[6,32,1024]{2,1,0:T(8,128)(2,1)S(1)}, f32[6,32,1024]{2,1,0:T(8,128)}) fusion(f32[6,32,1024]{2,1,0:T(8,128)S(1)} %copy-done.12, bf16[6,32,1024]{2,1,0:T(8,128)(2,1)} %collective-permute-done.14, bf16[6,32,1024]{2,1,0:T(8,128)(2,1)} %collective-permute-done.10, bf16[6,32,1024]{2,1,0:T(8,128)(2,1)} %collective-permute-done.13, ...), kind=kLoop, calls=%fused_computation.24 | loop fusion | flops 3145728 | bytes 4325380 | tf_op jit(solution)/shard_map/convert_element_type | solution.py:33
  86.4 3.2 %collective-permute-start.15 = (bf16[6,32,1024]{2,1,0:T(8,128)(2,1)S(1)}, bf16[6,32,1024]{2,1,0:T(8,128)(2,1)S(1)}, u32[]{:S(2)}, u32[]{:S(2)}) collective-permute-start(bf16[6,32,1024]{2,1,0:T(8,128)(2,1)S(1)} %get-tuple-element.42.refs_0_), channel_id=1, source_target_pairs={{0,24},{2,26},{4,28},{6,30},{8,0},{10,2},{12,4},{14,6},{16,8},{18,... | collective-permute-start | bytes 1179656 | tf_op jit(solution)/shard_map/ppermute | solution.py:284
  91.1 8.5 %collective-permute-done.16.refs_3_ = bf16[6,32,1024]{2,1,0:T(8,128)(2,1)S(1)} collective-permute-done((bf16[6,32,1024]{2,1,0:T(8,128)(2,1)S(1)}, bf16[6,32,1024]{2,1,0:T(8,128)(2,1)S(1)}, u32[]{:S(2)}, u32[]{:S(2)}) %collective-permute-start.16) | collective-permute-done | bytes 393248 | tf_op jit(solution)/shard_map/ppermute | solution.py:284
  101.1 4.2 %collective-permute-done.15.refs_1_ = bf16[6,32,1024]{2,1,0:T(8,128)(2,1)S(1)} collective-permute-done((bf16[6,32,1024]{2,1,0:T(8,128)(2,1)S(1)}, bf16[6,32,1024]{2,1,0:T(8,128)(2,1)S(1)}, u32[]{:S(2)}, u32[]{:S(2)}) %collective-permute-start.15) | collective-permute-done | bytes 393248 | tf_op jit(solution)/shard_map/ppermute | solution.py:284
  105.3 2.9 %collective-permute-start.19 = (bf16[6,32,1024]{2,1,0:T(8,128)(2,1)S(1)}, bf16[6,32,1024]{2,1,0:T(8,128)(2,1)}, u32[]{:S(2)}, u32[]{:S(2)}) collective-permute-start(bf16[6,32,1024]{2,1,0:T(8,128)(2,1)S(1)} %get-tuple-element.42.refs_0_), channel_id=1, source_target_pairs={{0,16},{2,18},{4,20},{6,22},{8,24},{10,26},{12,28},{14,30},{16,0},... | collective-permute-start | bytes 1179656 | tf_op jit(solution)/shard_map/ppermute | solution.py:284
  112.7 3.4 %collective-permute-done.22 = bf16[3,32,1024]{2,1,0:T(8,128)(2,1)S(1)} collective-permute-done((bf16[3,32,1024]{2,1,0:T(8,128)(2,1)S(1)}, bf16[3,32,1024]{2,1,0:T(8,128)(2,1)S(1)}, u32[]{:S(2)}, u32[]{:S(2)}) %collective-permute-start.22) | collective-permute-done | bytes 196640 | tf_op jit(solution)/shard_map/ppermute | solution.py:277
  118.5 6.3 %collective-permute-done.19.refs_2_ = bf16[6,32,1024]{2,1,0:T(8,128)(2,1)} collective-permute-done((bf16[6,32,1024]{2,1,0:T(8,128)(2,1)S(1)}, bf16[6,32,1024]{2,1,0:T(8,128)(2,1)}, u32[]{:S(2)}, u32[]{:S(2)}) %collective-permute-start.19) | collective-permute-done | bytes 393248 | tf_op jit(solution)/shard_map/ppermute | solution.py:284
  127.5 5.3 %collective-permute-done.29.refs_12_ = bf16[6,32,1024]{2,1,0:T(8,128)(2,1)} collective-permute-done((bf16[6,32,1024]{2,1,0:T(8,128)(2,1)}, bf16[6,32,1024]{2,1,0:T(8,128)(2,1)}, u32[]{:S(2)}, u32[]{:S(2)}) %collective-permute-start.29) | collective-permute-done | bytes 393248 | tf_op jit(solution)/shard_map/ppermute | solution.py:277
  143.5 6.1 %collective-permute-done.26.refs_9_ = bf16[6,32,1024]{2,1,0:T(8,128)(2,1)} collective-permute-done((bf16[6,32,1024]{2,1,0:T(8,128)(2,1)S(1)}, bf16[6,32,1024]{2,1,0:T(8,128)(2,1)}, u32[]{:S(2)}, u32[]{:S(2)}) %collective-permute-start.26) | collective-permute-done | bytes 393248 | tf_op jit(solution)/shard_map/ppermute | solution.py:277
  149.6 6.3 %collective-permute-done.30.refs_13_ = bf16[6,32,1024]{2,1,0:T(8,128)(2,1)} collective-permute-done((bf16[6,32,1024]{2,1,0:T(8,128)(2,1)S(1)}, bf16[6,32,1024]{2,1,0:T(8,128)(2,1)}, u32[]{:S(2)}, u32[]{:S(2)}) %collective-permute-start.30) | collective-permute-done | bytes 393248 | tf_op jit(solution)/shard_map/ppermute | solution.py:277
  155.9 3.9 %collective-permute-done.31.refs_14_ = bf16[6,32,1024]{2,1,0:T(8,128)(2,1)} collective-permute-done((bf16[6,32,1024]{2,1,0:T(8,128)(2,1)}, bf16[6,32,1024]{2,1,0:T(8,128)(2,1)}, u32[]{:S(2)}, u32[]{:S(2)}) %collective-permute-start.31) | collective-permute-done | bytes 393248 | tf_op jit(solution)/shard_map/ppermute | solution.py:280
  159.8 6.1 %shard_map.84 = (bf16[3,512,1024]{2,1,0:T(8,128)(2,1)}, bf16[3,512,512]{2,1,0:T(8,128)(2,1)}) custom-call(s32[3]{0:T(128)} %get-tuple-element.73.order_ref, bf16[6,32,1024]{2,1,0:T(8,128)(2,1)} %copy-done.5, bf16[6,32,1024]{2,1,0:T(8,128)(2,1)} %copy-done.9, bf16[6,32,1024]{2,1,0:T(8,128)(2,1)} %collective-permute-done.19.refs_2_, ...), custom_call_target="tpu_custom_call" | custom-call | flops 1610612736 | bytes 7864320 | tf_op jit(solution)/shard_map/pallas_call | solution.py:58
  166.0 3.0 %collective-permute-start.34 = (bf16[4,3,32,1024]{3,2,1,0:T(8,128)(2,1)S(1)}, bf16[4,3,32,1024]{3,2,1,0:T(8,128)(2,1)S(1)}, u32[]{:S(2)}, u32[]{:S(2)}) collective-permute-start(bf16[4,3,32,1024]{3,2,1,0:T(8,128)(2,1)S(1)} %slice.28), channel_id=1, source_target_pairs={{0,2},{2,0},{4,6},{6,4},{8,10},{10,8},{12,14},{14,12},{16,18},{18,... | collective-permute-start | bytes 2359304 | tf_op jit(solution)/shard_map/ppermute | solution.py:277
  169.0 5.9 %shard_map.83 = (bf16[3,512,1024]{2,1,0:T(8,128)(2,1)}, bf16[3,512,512]{2,1,0:T(8,128)(2,1)}) custom-call(s32[3]{0:T(128)} %get-tuple-element.74.order_ref, bf16[6,32,1024]{2,1,0:T(8,128)(2,1)} %copy-done.5, bf16[6,32,1024]{2,1,0:T(8,128)(2,1)} %copy-done.9, bf16[6,32,1024]{2,1,0:T(8,128)(2,1)} %collective-permute-done.19.refs_2_, ...), custom_call_target="tpu_custom_call" | custom-call | flops 1610612736 | bytes 7864320 | tf_op jit(solution)/shard_map/pallas_call | solution.py:58
  176.3 9.2 %shard_map.85 = (bf16[3,512,512]{2,1,0:T(8,128)(2,1)S(1)}, f32[3,8,128]{2,1,0:T(8,128)S(1)}) custom-call(bf16[3,512,512]{2,1,0:T(8,128)(2,1)S(1)} %copy-done.2, bf16[3,512,512]{2,1,0:T(8,128)(2,1)S(1)} %collective-permute-done.33.refs_1_), custom_call_target="tpu_custom_call" | custom-call | flops 7247757312 | bytes 4718592 | tf_op jit(solution)/shard_map/pallas_call | solution.py:133
  191.9 14.4 %shard_map.86 = (bf16[6,512,1024]{2,1,0:T(8,128)(2,1)}, f32[6,32,1024]{2,1,0:T(8,128)}, bf16[2,512,1024]{2,1,0:T(8,128)(2,1)}, f32[1,2]{1,0:T(1,128)}) custom-call(s32[16]{0:T(128)} %stack.125.places_ref, s32[16]{0:T(128)} %stack.142.spans_ref, s32[6]{0:T(128)} %broadcast_select_fusion.slots_ref, s32[6]{0:T(128)} %copy-done.14, ...), custom_call_target="tpu_custom_call" | custom-call | flops 3221225472 | bytes 28311552 | tf_op jit(solution)/shard_map/pallas_call | solution.py:228
  (107 shorter events, 57.1 us)
Async XLA Ops:
  7.2 58.6 %all-gather.5.cloned.1.call-start = ((), (), s32[]{:S(2)}) async-start(), calls=%async_computation | async-start | bytes 1966080 | tf_op jit(solution)/shard_map/all_gather | solution.py:306
  9.2 181.5 %all-gather.7.cloned.1.call-start = ((), (), s32[]{:S(2)}) async-start(), calls=%async_computation.1 | async-start | bytes 3932160 | tf_op jit(solution)/shard_map/all_gather | solution.py:320
  10.5 13.1 %collective-permute-start.3 = (bf16[6,32,1024]{2,1,0:T(8,128)(2,1)S(1)}, bf16[6,32,1024]{2,1,0:T(8,128)(2,1)}, u32[]{:S(2)}, u32[]{:S(2)}) collective-permute-start(bf16[6,32,1024]{2,1,0:T(8,128)(2,1)S(1)} %get-tuple-element.69), channel_id=1, source_target_pairs={{0,4},{2,6},{4,0},{6,2},{8,12},{10,14},{12,8},{14,10},{16,20},{18,... | collective-permute-start | bytes 1179656 | tf_op jit(solution)/shard_map/ppermute | solution.py:280
  17.7 16.4 %collective-permute-start.1 = (bf16[6,32,1024]{2,1,0:T(8,128)(2,1)}, bf16[6,32,1024]{2,1,0:T(8,128)(2,1)}, u32[]{:S(2)}, u32[]{:S(2)}) collective-permute-start(bf16[6,32,1024]{2,1,0:T(8,128)(2,1)} %get-tuple-element.63), channel_id=1, source_target_pairs={{0,2},{2,0},{4,6},{6,4},{8,10},{10,8},{12,14},{14,12},{16,18},{18,... | collective-permute-start | bytes 1179656 | tf_op jit(solution)/shard_map/ppermute | solution.py:277
  18.2 15.9 %collective-permute-start = (bf16[6,32,1024]{2,1,0:T(8,128)(2,1)S(1)}, bf16[6,32,1024]{2,1,0:T(8,128)(2,1)}, u32[]{:S(2)}, u32[]{:S(2)}) collective-permute-start(bf16[6,32,1024]{2,1,0:T(8,128)(2,1)S(1)} %get-tuple-element.64), channel_id=1, source_target_pairs={{0,4},{2,6},{4,0},{6,2},{8,12},{10,14},{12,8},{14,10},{16,20},{18,... | collective-permute-start | bytes 1179656 | tf_op jit(solution)/shard_map/ppermute | solution.py:280
  18.3 22.2 %collective-permute-start.9 = (bf16[6,32,1024]{2,1,0:T(8,128)(2,1)S(1)}, bf16[6,32,1024]{2,1,0:T(8,128)(2,1)}, u32[]{:S(2)}, u32[]{:S(2)}) collective-permute-start(bf16[6,32,1024]{2,1,0:T(8,128)(2,1)S(1)} %get-tuple-element.60), channel_id=1, source_target_pairs={{0,4},{2,6},{4,0},{6,2},{8,12},{10,14},{12,8},{14,10},{16,20},{18,... | collective-permute-start | bytes 1179656 | tf_op jit(solution)/shard_map/ppermute | solution.py:280
  28.3 20.6 %collective-permute-start.8 = (bf16[6,32,1024]{2,1,0:T(8,128)(2,1)}, bf16[6,32,1024]{2,1,0:T(8,128)(2,1)}, u32[]{:S(2)}, u32[]{:S(2)}) collective-permute-start(bf16[6,32,1024]{2,1,0:T(8,128)(2,1)} %get-tuple-element.67), channel_id=1, source_target_pairs={{0,4},{2,6},{4,0},{6,2},{8,12},{10,14},{12,8},{14,10},{16,20},{18,... | collective-permute-start | bytes 1179656 | tf_op jit(solution)/shard_map/ppermute | solution.py:280
  28.3 14.2 %collective-permute-start.6 = (bf16[6,32,1024]{2,1,0:T(8,128)(2,1)}, bf16[6,32,1024]{2,1,0:T(8,128)(2,1)}, u32[]{:S(2)}, u32[]{:S(2)}) collective-permute-start(bf16[6,32,1024]{2,1,0:T(8,128)(2,1)} %get-tuple-element.68), channel_id=1, source_target_pairs={{0,2},{2,0},{4,6},{6,4},{8,10},{10,8},{12,14},{14,12},{16,18},{18,... | collective-permute-start | bytes 1179656 | tf_op jit(solution)/shard_map/ppermute | solution.py:277
  36.1 14.7 %collective-permute-start.4 = (bf16[6,32,1024]{2,1,0:T(8,128)(2,1)}, bf16[6,32,1024]{2,1,0:T(8,128)(2,1)S(1)}, u32[]{:S(2)}, u32[]{:S(2)}) collective-permute-start(bf16[6,32,1024]{2,1,0:T(8,128)(2,1)} %fusion.11), channel_id=1, source_target_pairs={{0,2},{2,0},{4,6},{6,4},{8,10},{10,8},{12,14},{14,12},{16,18},{18,... | collective-permute-start | bytes 1179656 | tf_op jit(solution)/shard_map/ppermute | solution.py:277
  37.6 18.7 %collective-permute-start.5 = (bf16[6,32,1024]{2,1,0:T(8,128)(2,1)S(1)}, bf16[6,32,1024]{2,1,0:T(8,128)(2,1)S(1)}, u32[]{:S(2)}, u32[]{:S(2)}) collective-permute-start(bf16[6,32,1024]{2,1,0:T(8,128)(2,1)S(1)} %get-tuple-element.34), channel_id=1, source_target_pairs={{0,4},{2,6},{4,0},{6,2},{8,12},{10,14},{12,8},{14,10},{16,20},{18,... | collective-permute-start | bytes 1179656 | tf_op jit(solution)/shard_map/ppermute | solution.py:280
  42.5 16.7 %collective-permute-start.7 = (bf16[6,32,1024]{2,1,0:T(8,128)(2,1)S(1)}, bf16[6,32,1024]{2,1,0:T(8,128)(2,1)S(1)}, u32[]{:S(2)}, u32[]{:S(2)}) collective-permute-start(bf16[6,32,1024]{2,1,0:T(8,128)(2,1)S(1)} %get-tuple-element.35), channel_id=1, source_target_pairs={{0,2},{2,0},{4,6},{6,4},{8,10},{10,8},{12,14},{14,12},{16,18},{18,... | collective-permute-start | bytes 1179656 | tf_op jit(solution)/shard_map/ppermute | solution.py:277
  46.2 29.0 %collective-permute-start.10 = (bf16[6,32,1024]{2,1,0:T(8,128)(2,1)}, bf16[6,32,1024]{2,1,0:T(8,128)(2,1)}, u32[]{:S(2)}, u32[]{:S(2)}) collective-permute-start(bf16[6,32,1024]{2,1,0:T(8,128)(2,1)} %fusion.10), channel_id=1, source_target_pairs={{0,16},{2,18},{4,20},{6,22},{8,24},{10,26},{12,28},{14,30},{16,0},... | collective-permute-start | bytes 1179656 | tf_op jit(solution)/shard_map/ppermute | solution.py:284
  53.1 23.2 %collective-permute-start.13 = (bf16[6,32,1024]{2,1,0:T(8,128)(2,1)}, bf16[6,32,1024]{2,1,0:T(8,128)(2,1)}, u32[]{:S(2)}, u32[]{:S(2)}) collective-permute-start(bf16[6,32,1024]{2,1,0:T(8,128)(2,1)} %fusion.8), channel_id=1, source_target_pairs={{0,8},{2,10},{4,12},{6,14},{8,16},{10,18},{12,20},{14,22},{16,24},... | collective-permute-start | bytes 1179656 | tf_op jit(solution)/shard_map/ppermute | solution.py:284
  54.6 23.3 %collective-permute-start.11 = (bf16[6,32,1024]{2,1,0:T(8,128)(2,1)S(1)}, bf16[6,32,1024]{2,1,0:T(8,128)(2,1)}, u32[]{:S(2)}, u32[]{:S(2)}) collective-permute-start(bf16[6,32,1024]{2,1,0:T(8,128)(2,1)S(1)} %get-tuple-element.40), channel_id=1, source_target_pairs={{0,2},{2,0},{4,6},{6,4},{8,10},{10,8},{12,14},{14,12},{16,18},{18,... | collective-permute-start | bytes 1179656 | tf_op jit(solution)/shard_map/ppermute | solution.py:277
  61.6 16.3 %collective-permute-start.12 = (bf16[6,32,1024]{2,1,0:T(8,128)(2,1)}, bf16[6,32,1024]{2,1,0:T(8,128)(2,1)}, u32[]{:S(2)}, u32[]{:S(2)}) collective-permute-start(bf16[6,32,1024]{2,1,0:T(8,128)(2,1)} %get-tuple-element.65), channel_id=1, source_target_pairs={{0,4},{2,6},{4,0},{6,2},{8,12},{10,14},{12,8},{14,10},{16,20},{18,... | collective-permute-start | bytes 1179656 | tf_op jit(solution)/shard_map/ppermute | solution.py:280
  61.8 21.0 %collective-permute-start.14 = (bf16[6,32,1024]{2,1,0:T(8,128)(2,1)}, bf16[6,32,1024]{2,1,0:T(8,128)(2,1)}, u32[]{:S(2)}, u32[]{:S(2)}) collective-permute-start(bf16[6,32,1024]{2,1,0:T(8,128)(2,1)} %get-tuple-element.66), channel_id=1, source_target_pairs={{0,24},{2,26},{4,28},{6,30},{8,0},{10,2},{12,4},{14,6},{16,8},{18,... | collective-permute-start | bytes 1179656 | tf_op jit(solution)/shard_map/ppermute | solution.py:284
  75.2 30.0 %collective-permute-start.18 = (bf16[5,3,32,1024]{3,2,1,0:T(8,128)(2,1)}, bf16[5,3,32,1024]{3,2,1,0:T(8,128)(2,1)S(1)}, u32[]{:S(2)}, u32[]{:S(2)}) collective-permute-start(bf16[5,3,32,1024]{3,2,1,0:T(8,128)(2,1)} %pad_maximum_fusion), channel_id=1, source_target_pairs={{0,4},{2,6},{4,0},{6,2},{8,12},{10,14},{12,8},{14,10},{16,20},{18,... | collective-permute-start | bytes 2949128 | tf_op jit(solution)/shard_map/ppermute | solution.py:280
  76.3 29.0 %collective-permute-start.17 = (bf16[5,3,32,1024]{3,2,1,0:T(8,128)(2,1)}, bf16[5,3,32,1024]{3,2,1,0:T(8,128)(2,1)}, u32[]{:S(2)}, u32[]{:S(2)}) collective-permute-start(bf16[5,3,32,1024]{3,2,1,0:T(8,128)(2,1)} %pad_maximum_fusion), channel_id=1, source_target_pairs={{0,2},{2,0},{4,6},{6,4},{8,10},{10,8},{12,14},{14,12},{16,18},{18,... | collective-permute-start | bytes 2949128 | tf_op jit(solution)/shard_map/ppermute | solution.py:277
  85.8 13.8 %collective-permute-start.16 = (bf16[6,32,1024]{2,1,0:T(8,128)(2,1)S(1)}, bf16[6,32,1024]{2,1,0:T(8,128)(2,1)S(1)}, u32[]{:S(2)}, u32[]{:S(2)}) collective-permute-start(bf16[6,32,1024]{2,1,0:T(8,128)(2,1)S(1)} %get-tuple-element.42.refs_0_), channel_id=1, source_target_pairs={{0,8},{2,10},{4,12},{6,14},{8,16},{10,18},{12,20},{14,22},{16,24},... | collective-permute-start | bytes 1179656 | tf_op jit(solution)/shard_map/ppermute | solution.py:284
  86.4 18.9 %collective-permute-start.15 = (bf16[6,32,1024]{2,1,0:T(8,128)(2,1)S(1)}, bf16[6,32,1024]{2,1,0:T(8,128)(2,1)S(1)}, u32[]{:S(2)}, u32[]{:S(2)}) collective-permute-start(bf16[6,32,1024]{2,1,0:T(8,128)(2,1)S(1)} %get-tuple-element.42.refs_0_), channel_id=1, source_target_pairs={{0,24},{2,26},{4,28},{6,30},{8,0},{10,2},{12,4},{14,6},{16,8},{18,... | collective-permute-start | bytes 1179656 | tf_op jit(solution)/shard_map/ppermute | solution.py:284
  89.6 36.7 %collective-permute-start.25 = (bf16[6,32,1024]{2,1,0:T(8,128)(2,1)S(1)}, bf16[6,32,1024]{2,1,0:T(8,128)(2,1)}, u32[]{:S(2)}, u32[]{:S(2)}) collective-permute-start(bf16[6,32,1024]{2,1,0:T(8,128)(2,1)S(1)} %get-tuple-element.42.refs_0_), channel_id=1, source_target_pairs={{0,2},{2,0},{4,6},{6,4},{8,10},{10,8},{12,14},{14,12},{16,18},{18,... | collective-permute-start | bytes 1179656 | tf_op jit(solution)/shard_map/ppermute | solution.py:277
  105.3 19.6 %collective-permute-start.19 = (bf16[6,32,1024]{2,1,0:T(8,128)(2,1)S(1)}, bf16[6,32,1024]{2,1,0:T(8,128)(2,1)}, u32[]{:S(2)}, u32[]{:S(2)}) collective-permute-start(bf16[6,32,1024]{2,1,0:T(8,128)(2,1)S(1)} %get-tuple-element.42.refs_0_), channel_id=1, source_target_pairs={{0,16},{2,18},{4,20},{6,22},{8,24},{10,26},{12,28},{14,30},{16,0},... | collective-permute-start | bytes 1179656 | tf_op jit(solution)/shard_map/ppermute | solution.py:284
  109.7 24.3 %collective-permute-start.28 = (bf16[6,32,1024]{2,1,0:T(8,128)(2,1)S(1)}, bf16[6,32,1024]{2,1,0:T(8,128)(2,1)}, u32[]{:S(2)}, u32[]{:S(2)}) collective-permute-start(bf16[6,32,1024]{2,1,0:T(8,128)(2,1)S(1)} %collective-permute-done.16.refs_3_), channel_id=1, source_target_pairs={{0,2},{2,0},{4,6},{6,4},{8,10},{10,8},{12,14},{14,12},{16,18},{18,... | collective-permute-start | bytes 1179656 | tf_op jit(solution)/shard_map/ppermute | solution.py:277
  111.3 27.0 %collective-permute-start.24 = (bf16[6,32,1024]{2,1,0:T(8,128)(2,1)S(1)}, bf16[6,32,1024]{2,1,0:T(8,128)(2,1)}, u32[]{:S(2)}, u32[]{:S(2)}) collective-permute-start(bf16[6,32,1024]{2,1,0:T(8,128)(2,1)S(1)} %collective-permute-done.16.refs_3_), channel_id=1, source_target_pairs={{0,4},{2,6},{4,0},{6,2},{8,12},{10,14},{12,8},{14,10},{16,20},{18,... | collective-permute-start | bytes 1179656 | tf_op jit(solution)/shard_map/ppermute | solution.py:280
  116.1 16.6 %collective-permute-start.29 = (bf16[6,32,1024]{2,1,0:T(8,128)(2,1)}, bf16[6,32,1024]{2,1,0:T(8,128)(2,1)}, u32[]{:S(2)}, u32[]{:S(2)}) collective-permute-start(bf16[6,32,1024]{2,1,0:T(8,128)(2,1)} %collective-permute-done.20.refs_4_), channel_id=1, source_target_pairs={{0,2},{2,0},{4,6},{6,4},{8,10},{10,8},{12,14},{14,12},{16,18},{18,... | collective-permute-start | bytes 1179656 | tf_op jit(solution)/shard_map/ppermute | solution.py:277
  126.3 14.9 %collective-permute-start.27 = (bf16[6,32,1024]{2,1,0:T(8,128)(2,1)}, bf16[6,32,1024]{2,1,0:T(8,128)(2,1)}, u32[]{:S(2)}, u32[]{:S(2)}) collective-permute-start(bf16[6,32,1024]{2,1,0:T(8,128)(2,1)} %collective-permute-done.19.refs_2_), channel_id=1, source_target_pairs={{0,2},{2,0},{4,6},{6,4},{8,10},{10,8},{12,14},{14,12},{16,18},{18,... | collective-permute-start | bytes 1179656 | tf_op jit(solution)/shard_map/ppermute | solution.py:277
  132.8 16.9 %collective-permute-start.26 = (bf16[6,32,1024]{2,1,0:T(8,128)(2,1)S(1)}, bf16[6,32,1024]{2,1,0:T(8,128)(2,1)}, u32[]{:S(2)}, u32[]{:S(2)}) collective-permute-start(bf16[6,32,1024]{2,1,0:T(8,128)(2,1)S(1)} %collective-permute-done.15.refs_1_), channel_id=1, source_target_pairs={{0,2},{2,0},{4,6},{6,4},{8,10},{10,8},{12,14},{14,12},{16,18},{18,... | collective-permute-start | bytes 1179656 | tf_op jit(solution)/shard_map/ppermute | solution.py:277
  134.0 15.7 %collective-permute-start.32 = (bf16[6,32,1024]{2,1,0:T(8,128)(2,1)}, bf16[6,32,1024]{2,1,0:T(8,128)(2,1)}, u32[]{:S(2)}, u32[]{:S(2)}) collective-permute-start(bf16[6,32,1024]{2,1,0:T(8,128)(2,1)} %collective-permute-done.28.refs_11_), channel_id=1, source_target_pairs={{0,4},{2,6},{4,0},{6,2},{8,12},{10,14},{12,8},{14,10},{16,20},{18,... | collective-permute-start | bytes 1179656 | tf_op jit(solution)/shard_map/ppermute | solution.py:280
  136.4 19.5 %collective-permute-start.30 = (bf16[6,32,1024]{2,1,0:T(8,128)(2,1)S(1)}, bf16[6,32,1024]{2,1,0:T(8,128)(2,1)}, u32[]{:S(2)}, u32[]{:S(2)}) collective-permute-start(bf16[6,32,1024]{2,1,0:T(8,128)(2,1)S(1)} %collective-permute-done.21.refs_5_), channel_id=1, source_target_pairs={{0,2},{2,0},{4,6},{6,4},{8,10},{10,8},{12,14},{14,12},{16,18},{18,... | collective-permute-start | bytes 1179656 | tf_op jit(solution)/shard_map/ppermute | solution.py:277
  138.3 17.6 %collective-permute-start.23 = (bf16[6,32,1024]{2,1,0:T(8,128)(2,1)}, bf16[6,32,1024]{2,1,0:T(8,128)(2,1)}, u32[]{:S(2)}, u32[]{:S(2)}) collective-permute-start(bf16[6,32,1024]{2,1,0:T(8,128)(2,1)} %collective-permute-done.19.refs_2_), channel_id=1, source_target_pairs={{0,4},{2,6},{4,0},{6,2},{8,12},{10,14},{12,8},{14,10},{16,20},{18,... | collective-permute-start | bytes 1179656 | tf_op jit(solution)/shard_map/ppermute | solution.py:280
  141.2 18.5 %collective-permute-start.31 = (bf16[6,32,1024]{2,1,0:T(8,128)(2,1)}, bf16[6,32,1024]{2,1,0:T(8,128)(2,1)}, u32[]{:S(2)}, u32[]{:S(2)}) collective-permute-start(bf16[6,32,1024]{2,1,0:T(8,128)(2,1)} %collective-permute-done.27.refs_10_), channel_id=1, source_target_pairs={{0,4},{2,6},{4,0},{6,2},{8,12},{10,14},{12,8},{14,10},{16,20},{18,... | collective-permute-start | bytes 1179656 | tf_op jit(solution)/shard_map/ppermute | solution.py:280
  166.0 21.2 %collective-permute-start.34 = (bf16[4,3,32,1024]{3,2,1,0:T(8,128)(2,1)S(1)}, bf16[4,3,32,1024]{3,2,1,0:T(8,128)(2,1)S(1)}, u32[]{:S(2)}, u32[]{:S(2)}) collective-permute-start(bf16[4,3,32,1024]{3,2,1,0:T(8,128)(2,1)S(1)} %slice.28), channel_id=1, source_target_pairs={{0,2},{2,0},{4,6},{6,4},{8,10},{10,8},{12,14},{14,12},{16,18},{18,... | collective-permute-start | bytes 2359304 | tf_op jit(solution)/shard_map/ppermute | solution.py:277
  (23 other events, 581.4 us)
Sparse Core Ops, SparseCore 0:
  9.6 41.5 all-gather.4
  127.6 61.5 all-gather.6

commit v4 on v3

--- a/solution.py
+++ b/solution.py
@@ -388,13 +388,14 @@
     return added(term(me, 0, 0, 0), along_x0, along_y0, line1, line2, line3)
 
 
-def all_gather(grid, own, before_z2, before_x2):
-    x0, y0 = grid.over_x(own), grid.over_y(own)
+def all_gather(grid, own, before_x0, before_x2):
     z1, z3 = grid.over_z(own, LINE - 1), grid.over_z(own, 1)
+    z2 = grid.over_z(own, 2)
+    sent = after(own, *before_x0)
+    x0, y0 = grid.over_x(sent), grid.over_y(sent)
     far0 = grid.over_x(y0)
     x1, y1 = grid.over_x(z1), grid.over_y(z1)
     x3, y3 = grid.over_x(z3), grid.over_y(z3)
-    z2 = grid.over_z(after(own, z1, z3, *before_z2), 2)
     far3 = grid.over_y(x3)
     sent = after(z2, before_x2)
     x2, y2 = grid.over_x(sent), grid.over_y(sent)

time: 214 us -> 215 us (level)
  waiting for transfers between devices: 79.3 us -> 88.3 us
  starting transfers between devices: 53.5 us -> 47.2 us
    ppermute x15, waiting for transfers between devices: 37.3 us -> 41.2 us  [over_x(): return lax.ppermute(value, 'dp', self.x_pairs)]
    ppermute x13, waiting for transfers between devices: 10.1 us -> 13.8 us  [over_y(): return lax.ppermute(value, 'dp', self.y_pairs)]
    ppermute x15, starting transfers between devices: 22.3 us -> 19 us  [over_x(): return lax.ppermute(value, 'dp', self.x_pairs)]
    ppermute x6, starting transfers between devices: 14.8 us -> 12 us  [over_z(): return lax.ppermute(value, 'dp', pairs)]
    all_gather x1, waiting for transfers between devices: 0.02 us -> 2.42 us  [low_lines(): lax.all_gather(after(self.plane, *ties), 'dp', axis_index_groups=self.lines)]
  transfers between devices with their start and end apart: 39 -> 39, of which waited for: 23 -> 24; matrix products, arithmetic and copies ran while one was open for 12% -> 11% of each run, Pallas kernels for 10% -> 10%
where the time goes in v4:
time: 215 us; the launch traced here: 214 us
  waiting for transfers between devices  88.3 us (41%)
  starting transfers between devices  47.2 us (22%)
  Pallas kernels  35.6 us (17%)
  other arithmetic  19 us (9%)
  between operations  14.3 us (7%)
  local copies, waits for them, and re-layouts  9.33 us (4%)
    ppermute x15, waiting for transfers between devices, over_x(): return lax.ppermute(value, 'dp', self.x_pairs)  41.2 us
    ppermute x6, waiting for transfers between devices, over_z(): return lax.ppermute(value, 'dp', pairs)  30.2 us
    ppermute x15, starting transfers between devices, over_x(): return lax.ppermute(value, 'dp', self.x_pairs)  19 us
    convert_element_type x7, other arithmetic, half(): return value.astype(jnp.bfloat16)  16.2 us
    ppermute x13, starting transfers between devices, over_y(): return lax.ppermute(value, 'dp', self.y_pairs)  16.1 us
    pallas_call x1, Pallas kernels, applied(): pl.pallas_call(functools.partial(apply_kernel, len(sets), first_count, ma...  14.4 us
    ppermute x13, waiting for transfers between devices, over_y(): return lax.ppermute(value, 'dp', self.y_pairs)  13.8 us
    ppermute x6, starting transfers between devices, over_z(): return lax.ppermute(value, 'dp', pairs)  12 us
  transfers between devices with their start and end apart: 39, of which 24 were waited for; matrix products, arithmetic and copies ran while one was open for 11% of the time, Pallas kernels for 10%

profile of v4, /device:TPU:0, one launch (start us, length us, event | category | flops | bytes accessed | tf_op | source)
XLA Modules:
  0.0 213.7 jit_solution(8072126009765070765)
XLA Ops:
  10.5 3.0 %collective-permute-start.3 = (bf16[6,32,1024]{2,1,0:T(8,128)(2,1)S(1)}, bf16[6,32,1024]{2,1,0:T(8,128)(2,1)}, u32[]{:S(2)}, u32[]{:S(2)}) collective-permute-start(bf16[6,32,1024]{2,1,0:T(8,128)(2,1)S(1)} %get-tuple-element.69), channel_id=1, source_target_pairs={{0,4},{2,6},{4,0},{6,2},{8,12},{10,14},{12,8},{14,10},{16,20},{18,... | collective-permute-start | bytes 1179656 | tf_op jit(solution)/shard_map/ppermute | solution.py:280
  15.0 2.6 %dynamic-slice_bitcast_fusion = (bf16[6,32,1024]{2,1,0:T(8,128)(2,1)S(1)}, bf16[6,32,1024]{2,1,0:T(8,128)(2,1)S(1)}, bf16[6,32,1024]{2,1,0:T(8,128)(2,1)S(1)}, b...) fusion(bf16[1,6,512,1024]{3,2,1,0:T(8,128)(2,1)} %param.4, ...), kind=kLoop, calls=%fused_computation.26 | loop fusion | bytes 4718616 | tf_op jit(solution)/shard_map/dynamic_slice | solution.py:347
  20.2 3.4 %collective-permute-done.3 = bf16[6,32,1024]{2,1,0:T(8,128)(2,1)} collective-permute-done((bf16[6,32,1024]{2,1,0:T(8,128)(2,1)S(1)}, bf16[6,32,1024]{2,1,0:T(8,128)(2,1)}, u32[]{:S(2)}, u32[]{:S(2)}) %collective-permute-start.3) | collective-permute-done | bytes 393248 | tf_op jit(solution)/shard_map/ppermute | solution.py:280
  25.7 2.6 %fusion.12 = (bf16[6,32,1024]{2,1,0:T(8,128)(2,1)}, bf16[6,32,1024]{2,1,0:T(8,128)(2,1)}) fusion(bf16[6,32,1024]{2,1,0:T(8,128)(2,1)} %collective-permute-done.2, bf16[1,6,512,1024]{3,2,1,0:T(8,128)(2,1)} %param.4, s32[]{:T(128)S(6)} %select_n.67, bf16[6,32,1024]{2,1,0:T(8,128)(2,1)} %collective-permute-done.3, s32[]{:T(128)S(6)} %select_n.66), kind=kLoop, calls=%fused_computation.21 | loop fusion | flops 1572864 | bytes 2359304 | tf_op jit(solution)/shard_map/convert_element_type | solution.py:33
  30.3 3.8 %collective-permute-done.1 = bf16[6,32,1024]{2,1,0:T(8,128)(2,1)} collective-permute-done((bf16[6,32,1024]{2,1,0:T(8,128)(2,1)}, bf16[6,32,1024]{2,1,0:T(8,128)(2,1)}, u32[]{:S(2)}, u32[]{:S(2)}) %collective-permute-start.1) | collective-permute-done | bytes 393248 | tf_op jit(solution)/shard_map/ppermute | solution.py:277
  38.2 2.2 %collective-permute-done.9 = bf16[6,32,1024]{2,1,0:T(8,128)(2,1)} collective-permute-done((bf16[6,32,1024]{2,1,0:T(8,128)(2,1)S(1)}, bf16[6,32,1024]{2,1,0:T(8,128)(2,1)}, u32[]{:S(2)}, u32[]{:S(2)}) %collective-permute-start.9) | collective-permute-done | bytes 393248 | tf_op jit(solution)/shard_map/ppermute | solution.py:280
  44.0 2.2 %fusion.10 = bf16[6,32,1024]{2,1,0:T(8,128)(2,1)} fusion(bf16[6,32,1024]{2,1,0:T(8,128)(2,1)} %collective-permute-done.9, bf16[6,32,1024]{2,1,0:T(8,128)(2,1)} %collective-permute-done.6, bf16[1,6,512,1024]{3,2,1,0:T(8,128)(2,1)} %param.4, s32[]{:T(128)S(6)} %select_n.71), kind=kLoop, calls=%fused_computation.17 | loop fusion | flops 1179648 | bytes 1572868 | tf_op jit(solution)/shard_map/convert_element_type | solution.py:33
  46.2 2.6 %collective-permute-start.10 = (bf16[6,32,1024]{2,1,0:T(8,128)(2,1)}, bf16[6,32,1024]{2,1,0:T(8,128)(2,1)}, u32[]{:S(2)}, u32[]{:S(2)}) collective-permute-start(bf16[6,32,1024]{2,1,0:T(8,128)(2,1)} %fusion.10), channel_id=1, source_target_pairs={{0,16},{2,18},{4,20},{6,22},{8,24},{10,26},{12,28},{14,30},{16,0},... | collective-permute-start | bytes 1179656 | tf_op jit(solution)/shard_map/ppermute | solution.py:284
  50.9 2.2 %fusion.8 = bf16[6,32,1024]{2,1,0:T(8,128)(2,1)} fusion(bf16[6,32,1024]{2,1,0:T(8,128)(2,1)} %collective-permute-done.8, bf16[6,32,1024]{2,1,0:T(8,128)(2,1)} %collective-permute-done.1, bf16[1,6,512,1024]{3,2,1,0:T(8,128)(2,1)} %param.4, s32[]{:T(128)S(6)} %select_n.72), kind=kLoop, calls=%fused_computation.14 | loop fusion | flops 1179648 | bytes 1572868 | tf_op jit(solution)/shard_map/convert_element_type | solution.py:33
  56.4 2.9 %collective-permute-done.7 = bf16[6,32,1024]{2,1,0:T(8,128)(2,1)S(1)} collective-permute-done((bf16[6,32,1024]{2,1,0:T(8,128)(2,1)S(1)}, bf16[6,32,1024]{2,1,0:T(8,128)(2,1)S(1)}, u32[]{:S(2)}, u32[]{:S(2)}) %collective-permute-start.7) | collective-permute-done | bytes 393248 | tf_op jit(solution)/shard_map/ppermute | solution.py:277
  59.3 2.3 %fusion.4 = (bf16[6,32,1024]{2,1,0:T(8,128)(2,1)}, bf16[6,32,1024]{2,1,0:T(8,128)(2,1)}) fusion(bf16[6,32,1024]{2,1,0:T(8,128)(2,1)S(1)} %collective-permute-done.7, bf16[1,6,512,1024]{3,2,1,0:T(8,128)(2,1)} %param.4, s32[]{:T(128)S(6)} %select_n.74, bf16[6,32,1024]{2,1,0:T(8,128)(2,1)S(1)} %collective-permute-done.5, ...), kind=kLoop, calls=%fused_computation.8 | loop fusion | flops 1966080 | bytes 2752520 | tf_op jit(solution)/shard_map/convert_element_type | solution.py:33
  61.8 3.9 %collective-permute-start.14 = (bf16[6,32,1024]{2,1,0:T(8,128)(2,1)}, bf16[6,32,1024]{2,1,0:T(8,128)(2,1)}, u32[]{:S(2)}, u32[]{:S(2)}) collective-permute-start(bf16[6,32,1024]{2,1,0:T(8,128)(2,1)} %get-tuple-element.66), channel_id=1, source_target_pairs={{0,24},{2,26},{4,28},{6,30},{8,0},{10,2},{12,4},{14,6},{16,8},{18,... | collective-permute-start | bytes 1179656 | tf_op jit(solution)/shard_map/ppermute | solution.py:284
  68.1 7.1 %collective-permute-done.10 = bf16[6,32,1024]{2,1,0:T(8,128)(2,1)} collective-permute-done((bf16[6,32,1024]{2,1,0:T(8,128)(2,1)}, bf16[6,32,1024]{2,1,0:T(8,128)(2,1)}, u32[]{:S(2)}, u32[]{:S(2)}) %collective-permute-start.10) | collective-permute-done | bytes 393248 | tf_op jit(solution)/shard_map/ppermute | solution.py:284
  77.9 4.9 %collective-permute-done.14 = bf16[6,32,1024]{2,1,0:T(8,128)(2,1)} collective-permute-done((bf16[6,32,1024]{2,1,0:T(8,128)(2,1)}, bf16[6,32,1024]{2,1,0:T(8,128)(2,1)}, u32[]{:S(2)}, u32[]{:S(2)}) %collective-permute-start.14) | collective-permute-done | bytes 393248 | tf_op jit(solution)/shard_map/ppermute | solution.py:284
  82.8 3.0 %add_convert_fusion = (bf16[6,32,1024]{2,1,0:T(8,128)(2,1)S(1)}, f32[6,32,1024]{2,1,0:T(8,128)}) fusion(f32[6,32,1024]{2,1,0:T(8,128)S(1)} %copy-done.13, bf16[6,32,1024]{2,1,0:T(8,128)(2,1)} %collective-permute-done.14, bf16[6,32,1024]{2,1,0:T(8,128)(2,1)} %collective-permute-done.10, bf16[6,32,1024]{2,1,0:T(8,128)(2,1)} %collective-permute-done.13, ...), kind=kLoop, calls=%fused_computation.24 | loop fusion | flops 3145728 | bytes 4325380 | tf_op jit(solution)/shard_map/convert_element_type | solution.py:33
  86.4 3.2 %collective-permute-start.15 = (bf16[6,32,1024]{2,1,0:T(8,128)(2,1)S(1)}, bf16[6,32,1024]{2,1,0:T(8,128)(2,1)S(1)}, u32[]{:S(2)}, u32[]{:S(2)}) collective-permute-start(bf16[6,32,1024]{2,1,0:T(8,128)(2,1)S(1)} %get-tuple-element.42.refs_0_), channel_id=1, source_target_pairs={{0,24},{2,26},{4,28},{6,30},{8,0},{10,2},{12,4},{14,6},{16,8},{18,... | collective-permute-start | bytes 1179656 | tf_op jit(solution)/shard_map/ppermute | solution.py:284
  89.7 9.9 %collective-permute-done.17.refs_3_ = bf16[6,32,1024]{2,1,0:T(8,128)(2,1)S(1)} collective-permute-done((bf16[6,32,1024]{2,1,0:T(8,128)(2,1)S(1)}, bf16[6,32,1024]{2,1,0:T(8,128)(2,1)S(1)}, u32[]{:S(2)}, u32[]{:S(2)}) %collective-permute-start.17) | collective-permute-done | bytes 393248 | tf_op jit(solution)/shard_map/ppermute | solution.py:284
  102.6 2.7 %collective-permute-done.15.refs_1_ = bf16[6,32,1024]{2,1,0:T(8,128)(2,1)S(1)} collective-permute-done((bf16[6,32,1024]{2,1,0:T(8,128)(2,1)S(1)}, bf16[6,32,1024]{2,1,0:T(8,128)(2,1)S(1)}, u32[]{:S(2)}, u32[]{:S(2)}) %collective-permute-start.15) | collective-permute-done | bytes 393248 | tf_op jit(solution)/shard_map/ppermute | solution.py:284
  105.3 2.5 %collective-permute-start.22 = (bf16[3,32,1024]{2,1,0:T(8,128)(2,1)S(1)}, bf16[3,32,1024]{2,1,0:T(8,128)(2,1)S(1)}, u32[]{:S(2)}, u32[]{:S(2)}) collective-permute-start(bf16[3,32,1024]{2,1,0:T(8,128)(2,1)S(1)} %get-tuple-element.72), channel_id=1, source_target_pairs={{0,2},{2,0},{4,6},{6,4},{8,10},{10,8},{12,14},{14,12},{16,18},{18,... | collective-permute-start | bytes 589832 | tf_op jit(solution)/shard_map/ppermute | solution.py:277
  107.9 3.5 %collective-permute-done.28.refs_11_ = bf16[6,32,1024]{2,1,0:T(8,128)(2,1)} collective-permute-done((bf16[6,32,1024]{2,1,0:T(8,128)(2,1)S(1)}, bf16[6,32,1024]{2,1,0:T(8,128)(2,1)}, u32[]{:S(2)}, u32[]{:S(2)}) %collective-permute-start.28) | collective-permute-done | bytes 393248 | tf_op jit(solution)/shard_map/ppermute | solution.py:277
  112.8 2.7 %collective-permute-done.22 = bf16[3,32,1024]{2,1,0:T(8,128)(2,1)S(1)} collective-permute-done((bf16[3,32,1024]{2,1,0:T(8,128)(2,1)S(1)}, bf16[3,32,1024]{2,1,0:T(8,128)(2,1)S(1)}, u32[]{:S(2)}, u32[]{:S(2)}) %collective-permute-start.22) | collective-permute-done | bytes 196640 | tf_op jit(solution)/shard_map/ppermute | solution.py:277
  117.9 5.5 %collective-permute-done.16.refs_2_ = bf16[6,32,1024]{2,1,0:T(8,128)(2,1)} collective-permute-done((bf16[6,32,1024]{2,1,0:T(8,128)(2,1)S(1)}, bf16[6,32,1024]{2,1,0:T(8,128)(2,1)}, u32[]{:S(2)}, u32[]{:S(2)}) %collective-permute-start.16) | collective-permute-done | bytes 393248 | tf_op jit(solution)/shard_map/ppermute | solution.py:284
  130.3 6.7 %collective-permute-done.20.refs_4_ = bf16[6,32,1024]{2,1,0:T(8,128)(2,1)S(1)} collective-permute-done((bf16[6,32,1024]{2,1,0:T(8,128)(2,1)S(1)}, bf16[6,32,1024]{2,1,0:T(8,128)(2,1)S(1)}, u32[]{:S(2)}, u32[]{:S(2)}) %collective-permute-start.20) | collective-permute-done | bytes 393248 | tf_op jit(solution)/shard_map/ppermute | solution.py:280
  141.3 4.3 %collective-permute-done.30.refs_13_ = bf16[6,32,1024]{2,1,0:T(8,128)(2,1)} collective-permute-done((bf16[6,32,1024]{2,1,0:T(8,128)(2,1)}, bf16[6,32,1024]{2,1,0:T(8,128)(2,1)}, u32[]{:S(2)}, u32[]{:S(2)}) %collective-permute-start.30) | collective-permute-done | bytes 393248 | tf_op jit(solution)/shard_map/ppermute | solution.py:277
  145.6 8.4 %collective-permute-done.25.refs_8_ = bf16[6,32,1024]{2,1,0:T(8,128)(2,1)} collective-permute-done((bf16[6,32,1024]{2,1,0:T(8,128)(2,1)S(1)}, bf16[6,32,1024]{2,1,0:T(8,128)(2,1)}, u32[]{:S(2)}, u32[]{:S(2)}) %collective-permute-start.25) | collective-permute-done | bytes 393248 | tf_op jit(solution)/shard_map/ppermute | solution.py:277
  154.0 6.3 %collective-permute-done.29.refs_12_ = bf16[6,32,1024]{2,1,0:T(8,128)(2,1)} collective-permute-done((bf16[6,32,1024]{2,1,0:T(8,128)(2,1)S(1)}, bf16[6,32,1024]{2,1,0:T(8,128)(2,1)}, u32[]{:S(2)}, u32[]{:S(2)}) %collective-permute-start.29) | collective-permute-done | bytes 393248 | tf_op jit(solution)/shard_map/ppermute | solution.py:277
  160.4 6.1 %shard_map.84 = (bf16[3,512,1024]{2,1,0:T(8,128)(2,1)}, bf16[3,512,512]{2,1,0:T(8,128)(2,1)}) custom-call(s32[3]{0:T(128)} %get-tuple-element.73.order_ref, bf16[6,32,1024]{2,1,0:T(8,128)(2,1)} %copy-done.5, bf16[6,32,1024]{2,1,0:T(8,128)(2,1)} %copy-done.9, bf16[6,32,1024]{2,1,0:T(8,128)(2,1)} %collective-permute-done.16.refs_2_, ...), custom_call_target="tpu_custom_call" | custom-call | flops 1610612736 | bytes 7864320 | tf_op jit(solution)/shard_map/pallas_call | solution.py:58
  167.0 5.9 %shard_map.83 = (bf16[3,512,1024]{2,1,0:T(8,128)(2,1)}, bf16[3,512,512]{2,1,0:T(8,128)(2,1)}) custom-call(s32[3]{0:T(128)} %get-tuple-element.74.order_ref, bf16[6,32,1024]{2,1,0:T(8,128)(2,1)} %copy-done.5, bf16[6,32,1024]{2,1,0:T(8,128)(2,1)} %copy-done.9, bf16[6,32,1024]{2,1,0:T(8,128)(2,1)} %collective-permute-done.16.refs_2_, ...), custom_call_target="tpu_custom_call" | custom-call | flops 1610612736 | bytes 7864320 | tf_op jit(solution)/shard_map/pallas_call | solution.py:58
  174.3 9.2 %shard_map.85 = (bf16[3,512,512]{2,1,0:T(8,128)(2,1)S(1)}, f32[3,8,128]{2,1,0:T(8,128)S(1)}) custom-call(bf16[3,512,512]{2,1,0:T(8,128)(2,1)S(1)} %copy-done.2, bf16[3,512,512]{2,1,0:T(8,128)(2,1)S(1)} %collective-permute-done.33.refs_1_), custom_call_target="tpu_custom_call" | custom-call | flops 7247757312 | bytes 4718592 | tf_op jit(solution)/shard_map/pallas_call | solution.py:133
  183.6 3.1 %collective-permute-done.34.refs_10_ = bf16[4,3,32,1024]{3,2,1,0:T(8,128)(2,1)S(1)} collective-permute-done((bf16[4,3,32,1024]{3,2,1,0:T(8,128)(2,1)S(1)}, bf16[4,3,32,1024]{3,2,1,0:T(8,128)(2,1)S(1)}, u32[]{:S(2)}, u32[]{:S(2)}) %collective-permute-start.34) | collective-permute-done | bytes 786464 | tf_op jit(solution)/shard_map/ppermute | solution.py:277
  190.1 2.4 %all-gather.7.cloned.1.call-done.refs_6_ = bf16[16,3,32,1024]{3,2,1,0:T(8,128)(2,1)} async-done(((bf16[4,3,32,1024]{3,2,1,0:T(8,128)(2,1)}), bf16[16,3,32,1024]{3,2,1,0:T(8,128)(2,1)}) %all-gather.7.cloned.1.call-update) | async-done | bytes 3145744 | tf_op jit(solution)/shard_map/all_gather | solution.py:320
  192.5 14.4 %shard_map.86 = (bf16[6,512,1024]{2,1,0:T(8,128)(2,1)}, f32[6,32,1024]{2,1,0:T(8,128)}, bf16[2,512,1024]{2,1,0:T(8,128)(2,1)}, f32[1,2]{1,0:T(1,128)}) custom-call(s32[16]{0:T(128)} %stack.125.places_ref, s32[16]{0:T(128)} %stack.142.spans_ref, s32[6]{0:T(128)} %broadcast_select_fusion.slots_ref, s32[6]{0:T(128)} %copy-done.15, ...), custom_call_target="tpu_custom_call" | custom-call | flops 3221225472 | bytes 28311552 | tf_op jit(solution)/shard_map/pallas_call | solution.py:228
  (109 shorter events, 53.7 us)
Async XLA Ops:
  7.2 58.6 %all-gather.5.cloned.1.call-start = ((), (), s32[]{:S(2)}) async-start(), calls=%async_computation | async-start | bytes 1966080 | tf_op jit(solution)/shard_map/all_gather | solution.py:306
  9.2 183.3 %all-gather.7.cloned.1.call-start = ((), (), s32[]{:S(2)}) async-start(), calls=%async_computation.1 | async-start | bytes 3932160 | tf_op jit(solution)/shard_map/all_gather | solution.py:320
  17.7 16.4 %collective-permute-start.1 = (bf16[6,32,1024]{2,1,0:T(8,128)(2,1)}, bf16[6,32,1024]{2,1,0:T(8,128)(2,1)}, u32[]{:S(2)}, u32[]{:S(2)}) collective-permute-start(bf16[6,32,1024]{2,1,0:T(8,128)(2,1)} %get-tuple-element.63), channel_id=1, source_target_pairs={{0,2},{2,0},{4,6},{6,4},{8,10},{10,8},{12,14},{14,12},{16,18},{18,... | collective-permute-start | bytes 1179656 | tf_op jit(solution)/shard_map/ppermute | solution.py:277
  18.2 15.9 %collective-permute-start = (bf16[6,32,1024]{2,1,0:T(8,128)(2,1)S(1)}, bf16[6,32,1024]{2,1,0:T(8,128)(2,1)}, u32[]{:S(2)}, u32[]{:S(2)}) collective-permute-start(bf16[6,32,1024]{2,1,0:T(8,128)(2,1)S(1)} %get-tuple-element.64), channel_id=1, source_target_pairs={{0,4},{2,6},{4,0},{6,2},{8,12},{10,14},{12,8},{14,10},{16,20},{18,... | collective-permute-start | bytes 1179656 | tf_op jit(solution)/shard_map/ppermute | solution.py:280
  18.3 22.2 %collective-permute-start.9 = (bf16[6,32,1024]{2,1,0:T(8,128)(2,1)S(1)}, bf16[6,32,1024]{2,1,0:T(8,128)(2,1)}, u32[]{:S(2)}, u32[]{:S(2)}) collective-permute-start(bf16[6,32,1024]{2,1,0:T(8,128)(2,1)S(1)} %get-tuple-element.60), channel_id=1, source_target_pairs={{0,4},{2,6},{4,0},{6,2},{8,12},{10,14},{12,8},{14,10},{16,20},{18,... | collective-permute-start | bytes 1179656 | tf_op jit(solution)/shard_map/ppermute | solution.py:280
  28.3 20.6 %collective-permute-start.8 = (bf16[6,32,1024]{2,1,0:T(8,128)(2,1)}, bf16[6,32,1024]{2,1,0:T(8,128)(2,1)}, u32[]{:S(2)}, u32[]{:S(2)}) collective-permute-start(bf16[6,32,1024]{2,1,0:T(8,128)(2,1)} %get-tuple-element.67), channel_id=1, source_target_pairs={{0,4},{2,6},{4,0},{6,2},{8,12},{10,14},{12,8},{14,10},{16,20},{18,... | collective-permute-start | bytes 1179656 | tf_op jit(solution)/shard_map/ppermute | solution.py:280
  28.4 14.2 %collective-permute-start.6 = (bf16[6,32,1024]{2,1,0:T(8,128)(2,1)}, bf16[6,32,1024]{2,1,0:T(8,128)(2,1)}, u32[]{:S(2)}, u32[]{:S(2)}) collective-permute-start(bf16[6,32,1024]{2,1,0:T(8,128)(2,1)} %get-tuple-element.68), channel_id=1, source_target_pairs={{0,2},{2,0},{4,6},{6,4},{8,10},{10,8},{12,14},{14,12},{16,18},{18,... | collective-permute-start | bytes 1179656 | tf_op jit(solution)/shard_map/ppermute | solution.py:277
  36.1 14.7 %collective-permute-start.4 = (bf16[6,32,1024]{2,1,0:T(8,128)(2,1)}, bf16[6,32,1024]{2,1,0:T(8,128)(2,1)S(1)}, u32[]{:S(2)}, u32[]{:S(2)}) collective-permute-start(bf16[6,32,1024]{2,1,0:T(8,128)(2,1)} %fusion.11), channel_id=1, source_target_pairs={{0,2},{2,0},{4,6},{6,4},{8,10},{10,8},{12,14},{14,12},{16,18},{18,... | collective-permute-start | bytes 1179656 | tf_op jit(solution)/shard_map/ppermute | solution.py:277
  37.6 18.7 %collective-permute-start.5 = (bf16[6,32,1024]{2,1,0:T(8,128)(2,1)S(1)}, bf16[6,32,1024]{2,1,0:T(8,128)(2,1)S(1)}, u32[]{:S(2)}, u32[]{:S(2)}) collective-permute-start(bf16[6,32,1024]{2,1,0:T(8,128)(2,1)S(1)} %get-tuple-element.34), channel_id=1, source_target_pairs={{0,4},{2,6},{4,0},{6,2},{8,12},{10,14},{12,8},{14,10},{16,20},{18,... | collective-permute-start | bytes 1179656 | tf_op jit(solution)/shard_map/ppermute | solution.py:280
  42.5 16.7 %collective-permute-start.7 = (bf16[6,32,1024]{2,1,0:T(8,128)(2,1)S(1)}, bf16[6,32,1024]{2,1,0:T(8,128)(2,1)S(1)}, u32[]{:S(2)}, u32[]{:S(2)}) collective-permute-start(bf16[6,32,1024]{2,1,0:T(8,128)(2,1)S(1)} %get-tuple-element.35), channel_id=1, source_target_pairs={{0,2},{2,0},{4,6},{6,4},{8,10},{10,8},{12,14},{14,12},{16,18},{18,... | collective-permute-start | bytes 1179656 | tf_op jit(solution)/shard_map/ppermute | solution.py:277
  46.2 29.0 %collective-permute-start.10 = (bf16[6,32,1024]{2,1,0:T(8,128)(2,1)}, bf16[6,32,1024]{2,1,0:T(8,128)(2,1)}, u32[]{:S(2)}, u32[]{:S(2)}) collective-permute-start(bf16[6,32,1024]{2,1,0:T(8,128)(2,1)} %fusion.10), channel_id=1, source_target_pairs={{0,16},{2,18},{4,20},{6,22},{8,24},{10,26},{12,28},{14,30},{16,0},... | collective-permute-start | bytes 1179656 | tf_op jit(solution)/shard_map/ppermute | solution.py:284
  53.0 23.3 %collective-permute-start.13 = (bf16[6,32,1024]{2,1,0:T(8,128)(2,1)}, bf16[6,32,1024]{2,1,0:T(8,128)(2,1)}, u32[]{:S(2)}, u32[]{:S(2)}) collective-permute-start(bf16[6,32,1024]{2,1,0:T(8,128)(2,1)} %fusion.8), channel_id=1, source_target_pairs={{0,8},{2,10},{4,12},{6,14},{8,16},{10,18},{12,20},{14,22},{16,24},... | collective-permute-start | bytes 1179656 | tf_op jit(solution)/shard_map/ppermute | solution.py:284
  54.6 23.3 %collective-permute-start.11 = (bf16[6,32,1024]{2,1,0:T(8,128)(2,1)S(1)}, bf16[6,32,1024]{2,1,0:T(8,128)(2,1)}, u32[]{:S(2)}, u32[]{:S(2)}) collective-permute-start(bf16[6,32,1024]{2,1,0:T(8,128)(2,1)S(1)} %get-tuple-element.40), channel_id=1, source_target_pairs={{0,2},{2,0},{4,6},{6,4},{8,10},{10,8},{12,14},{14,12},{16,18},{18,... | collective-permute-start | bytes 1179656 | tf_op jit(solution)/shard_map/ppermute | solution.py:277
  61.6 16.3 %collective-permute-start.12 = (bf16[6,32,1024]{2,1,0:T(8,128)(2,1)}, bf16[6,32,1024]{2,1,0:T(8,128)(2,1)}, u32[]{:S(2)}, u32[]{:S(2)}) collective-permute-start(bf16[6,32,1024]{2,1,0:T(8,128)(2,1)} %get-tuple-element.65), channel_id=1, source_target_pairs={{0,4},{2,6},{4,0},{6,2},{8,12},{10,14},{12,8},{14,10},{16,20},{18,... | collective-permute-start | bytes 1179656 | tf_op jit(solution)/shard_map/ppermute | solution.py:280
  61.8 21.0 %collective-permute-start.14 = (bf16[6,32,1024]{2,1,0:T(8,128)(2,1)}, bf16[6,32,1024]{2,1,0:T(8,128)(2,1)}, u32[]{:S(2)}, u32[]{:S(2)}) collective-permute-start(bf16[6,32,1024]{2,1,0:T(8,128)(2,1)} %get-tuple-element.66), channel_id=1, source_target_pairs={{0,24},{2,26},{4,28},{6,30},{8,0},{10,2},{12,4},{14,6},{16,8},{18,... | collective-permute-start | bytes 1179656 | tf_op jit(solution)/shard_map/ppermute | solution.py:284
  75.2 25.9 %collective-permute-start.19 = (bf16[5,3,32,1024]{3,2,1,0:T(8,128)(2,1)}, bf16[5,3,32,1024]{3,2,1,0:T(8,128)(2,1)S(1)}, u32[]{:S(2)}, u32[]{:S(2)}) collective-permute-start(bf16[5,3,32,1024]{3,2,1,0:T(8,128)(2,1)} %pad_maximum_fusion), channel_id=1, source_target_pairs={{0,4},{2,6},{4,0},{6,2},{8,12},{10,14},{12,8},{14,10},{16,20},{18,... | collective-permute-start | bytes 2949128 | tf_op jit(solution)/shard_map/ppermute | solution.py:280
  76.3 31.5 %collective-permute-start.18 = (bf16[5,3,32,1024]{3,2,1,0:T(8,128)(2,1)}, bf16[5,3,32,1024]{3,2,1,0:T(8,128)(2,1)S(1)}, u32[]{:S(2)}, u32[]{:S(2)}) collective-permute-start(bf16[5,3,32,1024]{3,2,1,0:T(8,128)(2,1)} %pad_maximum_fusion), channel_id=1, source_target_pairs={{0,2},{2,0},{4,6},{6,4},{8,10},{10,8},{12,14},{14,12},{16,18},{18,... | collective-permute-start | bytes 2949128 | tf_op jit(solution)/shard_map/ppermute | solution.py:277
  85.8 13.8 %collective-permute-start.17 = (bf16[6,32,1024]{2,1,0:T(8,128)(2,1)S(1)}, bf16[6,32,1024]{2,1,0:T(8,128)(2,1)S(1)}, u32[]{:S(2)}, u32[]{:S(2)}) collective-permute-start(bf16[6,32,1024]{2,1,0:T(8,128)(2,1)S(1)} %get-tuple-element.42.refs_0_), channel_id=1, source_target_pairs={{0,8},{2,10},{4,12},{6,14},{8,16},{10,18},{12,20},{14,22},{16,24},... | collective-permute-start | bytes 1179656 | tf_op jit(solution)/shard_map/ppermute | solution.py:284
  86.4 18.9 %collective-permute-start.15 = (bf16[6,32,1024]{2,1,0:T(8,128)(2,1)S(1)}, bf16[6,32,1024]{2,1,0:T(8,128)(2,1)S(1)}, u32[]{:S(2)}, u32[]{:S(2)}) collective-permute-start(bf16[6,32,1024]{2,1,0:T(8,128)(2,1)S(1)} %get-tuple-element.42.refs_0_), channel_id=1, source_target_pairs={{0,24},{2,26},{4,28},{6,30},{8,0},{10,2},{12,4},{14,6},{16,8},{18,... | collective-permute-start | bytes 1179656 | tf_op jit(solution)/shard_map/ppermute | solution.py:284
  89.6 33.7 %collective-permute-start.16 = (bf16[6,32,1024]{2,1,0:T(8,128)(2,1)S(1)}, bf16[6,32,1024]{2,1,0:T(8,128)(2,1)}, u32[]{:S(2)}, u32[]{:S(2)}) collective-permute-start(bf16[6,32,1024]{2,1,0:T(8,128)(2,1)S(1)} %get-tuple-element.42.refs_0_), channel_id=1, source_target_pairs={{0,16},{2,18},{4,20},{6,22},{8,24},{10,26},{12,28},{14,30},{16,0},... | collective-permute-start | bytes 1179656 | tf_op jit(solution)/shard_map/ppermute | solution.py:284
  101.1 23.7 %collective-permute-start.24 = (bf16[6,32,1024]{2,1,0:T(8,128)(2,1)S(1)}, bf16[6,32,1024]{2,1,0:T(8,128)(2,1)}, u32[]{:S(2)}, u32[]{:S(2)}) collective-permute-start(bf16[6,32,1024]{2,1,0:T(8,128)(2,1)S(1)} %collective-permute-done.17.refs_3_), channel_id=1, source_target_pairs={{0,4},{2,6},{4,0},{6,2},{8,12},{10,14},{12,8},{14,10},{16,20},{18,... | collective-permute-start | bytes 1179656 | tf_op jit(solution)/shard_map/ppermute | solution.py:280
  107.8 19.1 %collective-permute-start.26 = (bf16[6,32,1024]{2,1,0:T(8,128)(2,1)S(1)}, bf16[6,32,1024]{2,1,0:T(8,128)(2,1)}, u32[]{:S(2)}, u32[]{:S(2)}) collective-permute-start(bf16[6,32,1024]{2,1,0:T(8,128)(2,1)S(1)} %collective-permute-done.15.refs_1_), channel_id=1, source_target_pairs={{0,2},{2,0},{4,6},{6,4},{8,10},{10,8},{12,14},{14,12},{16,18},{18,... | collective-permute-start | bytes 1179656 | tf_op jit(solution)/shard_map/ppermute | solution.py:277
  111.3 14.1 %collective-permute-start.21 = (bf16[6,32,1024]{2,1,0:T(8,128)(2,1)S(1)}, bf16[6,32,1024]{2,1,0:T(8,128)(2,1)}, u32[]{:S(2)}, u32[]{:S(2)}) collective-permute-start(bf16[6,32,1024]{2,1,0:T(8,128)(2,1)S(1)} %collective-permute-done.15.refs_1_), channel_id=1, source_target_pairs={{0,4},{2,6},{4,0},{6,2},{8,12},{10,14},{12,8},{14,10},{16,20},{18,... | collective-permute-start | bytes 1179656 | tf_op jit(solution)/shard_map/ppermute | solution.py:280
  115.4 13.2 %collective-permute-start.32 = (bf16[6,32,1024]{2,1,0:T(8,128)(2,1)}, bf16[6,32,1024]{2,1,0:T(8,128)(2,1)}, u32[]{:S(2)}, u32[]{:S(2)}) collective-permute-start(bf16[6,32,1024]{2,1,0:T(8,128)(2,1)} %collective-permute-done.28.refs_11_), channel_id=1, source_target_pairs={{0,4},{2,6},{4,0},{6,2},{8,12},{10,14},{12,8},{14,10},{16,20},{18,... | collective-permute-start | bytes 1179656 | tf_op jit(solution)/shard_map/ppermute | solution.py:280
  123.4 13.6 %collective-permute-start.20 = (bf16[6,32,1024]{2,1,0:T(8,128)(2,1)S(1)}, bf16[6,32,1024]{2,1,0:T(8,128)(2,1)S(1)}, u32[]{:S(2)}, u32[]{:S(2)}) collective-permute-start(bf16[6,32,1024]{2,1,0:T(8,128)(2,1)S(1)} %get-tuple-element.42.refs_0_), channel_id=1, source_target_pairs={{0,4},{2,6},{4,0},{6,2},{8,12},{10,14},{12,8},{14,10},{16,20},{18,... | collective-permute-start | bytes 1179656 | tf_op jit(solution)/shard_map/ppermute | solution.py:280
  124.8 14.1 %collective-permute-start.27 = (bf16[6,32,1024]{2,1,0:T(8,128)(2,1)}, bf16[6,32,1024]{2,1,0:T(8,128)(2,1)}, u32[]{:S(2)}, u32[]{:S(2)}) collective-permute-start(bf16[6,32,1024]{2,1,0:T(8,128)(2,1)} %collective-permute-done.16.refs_2_), channel_id=1, source_target_pairs={{0,2},{2,0},{4,6},{6,4},{8,10},{10,8},{12,14},{14,12},{16,18},{18,... | collective-permute-start | bytes 1179656 | tf_op jit(solution)/shard_map/ppermute | solution.py:277
  125.4 20.1 %collective-permute-start.30 = (bf16[6,32,1024]{2,1,0:T(8,128)(2,1)}, bf16[6,32,1024]{2,1,0:T(8,128)(2,1)}, u32[]{:S(2)}, u32[]{:S(2)}) collective-permute-start(bf16[6,32,1024]{2,1,0:T(8,128)(2,1)} %collective-permute-done.21.refs_5_), channel_id=1, source_target_pairs={{0,2},{2,0},{4,6},{6,4},{8,10},{10,8},{12,14},{14,12},{16,18},{18,... | collective-permute-start | bytes 1179656 | tf_op jit(solution)/shard_map/ppermute | solution.py:277
  126.9 27.1 %collective-permute-start.25 = (bf16[6,32,1024]{2,1,0:T(8,128)(2,1)S(1)}, bf16[6,32,1024]{2,1,0:T(8,128)(2,1)}, u32[]{:S(2)}, u32[]{:S(2)}) collective-permute-start(bf16[6,32,1024]{2,1,0:T(8,128)(2,1)S(1)} %get-tuple-element.42.refs_0_), channel_id=1, source_target_pairs={{0,2},{2,0},{4,6},{6,4},{8,10},{10,8},{12,14},{14,12},{16,18},{18,... | collective-permute-start | bytes 1179656 | tf_op jit(solution)/shard_map/ppermute | solution.py:277
  128.7 25.3 %collective-permute-start.23 = (bf16[6,32,1024]{2,1,0:T(8,128)(2,1)}, bf16[6,32,1024]{2,1,0:T(8,128)(2,1)}, u32[]{:S(2)}, u32[]{:S(2)}) collective-permute-start(bf16[6,32,1024]{2,1,0:T(8,128)(2,1)} %collective-permute-done.16.refs_2_), channel_id=1, source_target_pairs={{0,4},{2,6},{4,0},{6,2},{8,12},{10,14},{12,8},{14,10},{16,20},{18,... | collective-permute-start | bytes 1179656 | tf_op jit(solution)/shard_map/ppermute | solution.py:280
  137.0 23.3 %collective-permute-start.29 = (bf16[6,32,1024]{2,1,0:T(8,128)(2,1)S(1)}, bf16[6,32,1024]{2,1,0:T(8,128)(2,1)}, u32[]{:S(2)}, u32[]{:S(2)}) collective-permute-start(bf16[6,32,1024]{2,1,0:T(8,128)(2,1)S(1)} %collective-permute-done.20.refs_4_), channel_id=1, source_target_pairs={{0,2},{2,0},{4,6},{6,4},{8,10},{10,8},{12,14},{14,12},{16,18},{18,... | collective-permute-start | bytes 1179656 | tf_op jit(solution)/shard_map/ppermute | solution.py:277
  138.9 21.5 %collective-permute-start.31 = (bf16[6,32,1024]{2,1,0:T(8,128)(2,1)}, bf16[6,32,1024]{2,1,0:T(8,128)(2,1)}, u32[]{:S(2)}, u32[]{:S(2)}) collective-permute-start(bf16[6,32,1024]{2,1,0:T(8,128)(2,1)} %collective-permute-done.27.refs_10_), channel_id=1, source_target_pairs={{0,4},{2,6},{4,0},{6,2},{8,12},{10,14},{12,8},{14,10},{16,20},{18,... | collective-permute-start | bytes 1179656 | tf_op jit(solution)/shard_map/ppermute | solution.py:280
  166.6 20.0 %collective-permute-start.34 = (bf16[4,3,32,1024]{3,2,1,0:T(8,128)(2,1)S(1)}, bf16[4,3,32,1024]{3,2,1,0:T(8,128)(2,1)S(1)}, u32[]{:S(2)}, u32[]{:S(2)}) collective-permute-start(bf16[4,3,32,1024]{3,2,1,0:T(8,128)(2,1)S(1)} %slice.28), channel_id=1, source_target_pairs={{0,2},{2,0},{4,6},{6,4},{8,10},{10,8},{12,14},{14,12},{16,18},{18,... | collective-permute-start | bytes 2359304 | tf_op jit(solution)/shard_map/ppermute | solution.py:277
  (24 other events, 603.2 us)
Sparse Core Ops, SparseCore 0:
  9.6 41.4 all-gather.4
  125.6 66.9 all-gather.6

commit v5 on v3

--- a/solution.py
+++ b/solution.py
@@ -357,35 +357,42 @@
     far3 = grid.over_y(raw_far3)
     along_y2 = grid.over_y(raw_y2)
 
-    me = after(grid.me, far1, far2, raw_y3)
-    sent_x2 = half(added(term(me, 1, 0, 2), far2))
-    sent_y1 = half(added(term(me, 0, 1, 1), far1))
+    ahead_at = [(1, 0, 2), (0, 1, 1), (1, 0, 3), (0, 0, 2), (0, 0, 1), (0, 0, 3), (0, 1, 0), (0, 0, 0)]
+    me = after(grid.me, raw_y3)
+    ahead = dict(zip(ahead_at, lax.optimization_barrier([term(me, *at) for at in ahead_at])))
+
+    def ready(ties, *at):
+        return after(ahead[at], *ties)
+
+    ties = [far1, far2]
+    sent_x2 = half(added(ready(ties, 1, 0, 2), far2))
+    sent_y1 = half(added(ready(ties, 0, 1, 1), far1))
     along_x2 = grid.over_x(sent_x2)
     along_y1 = grid.over_y(sent_y1)
 
-    me = after(grid.me, far3, along_x1, sent_x2, sent_y1)
-    sent_x3 = half(added(term(me, 1, 0, 3), far3))
+    ties = [far3, along_x1, sent_x2, sent_y1]
+    sent_x3 = half(added(ready(ties, 1, 0, 3), far3))
     along_x3 = grid.over_x(sent_x3)
     along_y3 = grid.over_y(after(raw_y3, far3, along_x1))
 
-    me = after(grid.me, along_y2, along_x2, sent_x3)
-    near2 = half(added(term(me, 0, 0, 2), along_x2, along_y2))
+    ties = [along_y2, along_x2, sent_x3]
+    near2 = half(added(ready(ties, 0, 0, 2), along_x2, along_y2))
     line2 = grid.over_z(near2, 2)
     far0 = grid.over_x(after(raw_far0, along_x2))
 
-    me = after(grid.me, along_x1, along_y1, along_x3, near2)
-    near1 = half(added(term(me, 0, 0, 1), along_x1, along_y1))
+    ties = [along_x1, along_y1, along_x3, near2, sent_x3]
+    near1 = half(added(ready(ties, 0, 0, 1), along_x1, along_y1))
     line1 = grid.over_z(near1, 1)
-    along_x0 = grid.over_x(after(raw_x0, along_x3))
-
-    me = after(grid.me, along_x3, along_y3, far0, near1)
-    near3 = half(added(term(me, 0, 0, 3), along_x3, along_y3))
-    sent_y0 = half(added(term(me, 0, 1, 0), far0))
+    along_x0 = grid.over_x(after(raw_x0, near1))
+
+    ties = [along_x3, along_y3, far0, near1]
+    near3 = half(added(ready(ties, 0, 0, 3), along_x3, along_y3))
+    sent_y0 = half(added(ready(ties, 0, 1, 0), far0))
     line3 = grid.over_z(near3, 3)
     master_gather.near(near3, sent_y0)
     along_y0 = grid.over_y(sent_y0)
-    me = after(grid.me, near3, sent_y0, line2)
-    return added(term(me, 0, 0, 0), along_x0, along_y0, line1, line2, line3)
+    ties = [near3, sent_y0, line2]
+    return added(ready(ties, 0, 0, 0), along_x0, along_y0, line1, line2, line3)
 
 
 def all_gather(grid, own, before_z2, before_x2):

time: 214 us -> 216 us (level)
  other arithmetic: 19.1 us -> 9.81 us
  waiting for transfers between devices: 79.3 us -> 88.2 us
    ppermute x13, waiting for transfers between devices: 10.1 us -> 18.7 us  [over_y(): return lax.ppermute(value, 'dp', self.y_pairs)]
    all_gather x1, waiting for transfers between devices: 0.01 us -> 8.45 us  [__init__(): self.line = lax.all_gather(self.own, 'dp', axis_index_groups=self.lines)]
    convert_element_type x7 -> x9, other arithmetic: 16.3 us -> 8.06 us  [half(): return value.astype(jnp.bfloat16)]
    ppermute x15, waiting for transfers between devices: 37.3 us -> 32.9 us  [over_x(): return lax.ppermute(value, 'dp', self.x_pairs)]
    ppermute x6, waiting for transfers between devices: 31.1 us -> 27.4 us  [over_z(): return lax.ppermute(value, 'dp', pairs)]
    dynamic_slice x2 -> x3, local copies, waits for them, and re-layouts: 3.87 us -> 6.78 us  [term(): return lax.dynamic_slice_in_dim(terms, start, row_count, axis=1)]
    ppermute x6, starting transfers between devices: 14.8 us -> 12.3 us  [over_z(): return lax.ppermute(value, 'dp', pairs)]
  transfers between devices with their start and end apart: 39 -> 39, of which waited for: 23 -> 19; matrix products, arithmetic and copies ran while one was open for 12% -> 9% of each run, Pallas kernels for 10% -> 10%
where the time goes in v5:
time: 216 us; the launch traced here: 215 us
  waiting for transfers between devices  88.2 us (41%)
  starting transfers between devices  54 us (25%)
  Pallas kernels  35.5 us (16%)
  between operations  14.4 us (7%)
  local copies, waits for them, and re-layouts  13.3 us (6%)
  other arithmetic  9.81 us (5%)
    ppermute x15, waiting for transfers between devices, over_x(): return lax.ppermute(value, 'dp', self.x_pairs)  32.9 us
    ppermute x6, waiting for transfers between devices, over_z(): return lax.ppermute(value, 'dp', pairs)  27.4 us
    ppermute x15, starting transfers between devices, over_x(): return lax.ppermute(value, 'dp', self.x_pairs)  24.1 us
    ppermute x13, waiting for transfers between devices, over_y(): return lax.ppermute(value, 'dp', self.y_pairs)  18.7 us
    ppermute x13, starting transfers between devices, over_y(): return lax.ppermute(value, 'dp', self.y_pairs)  17.4 us
    pallas_call x1, Pallas kernels, applied(): pl.pallas_call(functools.partial(apply_kernel, len(sets), first_count, ma...  14.3 us
    ppermute x6, starting transfers between devices, over_z(): return lax.ppermute(value, 'dp', pairs)  12.3 us
    pallas_call x2, Pallas kernels, grams(): pl.pallas_call(gram_kernel, grid_spec=pltpu.PrefetchScalarGridSpec(num_sc...  12 us
  transfers between devices with their start and end apart: 39, of which 19 were waited for; matrix products, arithmetic and copies ran while one was open for 9% of the time, Pallas kernels for 10%

profile of v5, /device:TPU:0, one launch (start us, length us, event | category | flops | bytes accessed | tf_op | source)
XLA Modules:
  0.0 215.2 jit_solution(11451424774945786096)
XLA Ops:
  8.4 3.0 %collective-permute-start.3 = (bf16[6,32,1024]{2,1,0:T(8,128)(2,1)S(1)}, bf16[6,32,1024]{2,1,0:T(8,128)(2,1)S(1)}, u32[]{:S(2)}, u32[]{:S(2)}) collective-permute-start(bf16[6,32,1024]{2,1,0:T(8,128)(2,1)S(1)} %get-tuple-element.94), channel_id=1, source_target_pairs={{0,4},{2,6},{4,0},{6,2},{8,12},{10,14},{12,8},{14,10},{16,20},{18,... | collective-permute-start | bytes 1179656 | tf_op jit(solution)/shard_map/ppermute | solution.py:280
  16.8 3.8 %dynamic-slice_bitcast_fusion = (bf16[6,32,1024]{2,1,0:T(8,128)(2,1)}, bf16[6,32,1024]{2,1,0:T(8,128)(2,1)S(1)}, bf16[6,32,1024]{2,1,0:T(8,128)(2,1)S(1)}, bf16[...) fusion(bf16[1,6,512,1024]{3,2,1,0:T(8,128)(2,1)} %param.4, ...), kind=kLoop, calls=%fused_computation.12 | loop fusion | bytes 10223668 | tf_op jit(solution)/shard_map/dynamic_slice | solution.py:347
  25.6 7.1 %collective-permute-done.1 = bf16[6,32,1024]{2,1,0:T(8,128)(2,1)S(1)} collective-permute-done((bf16[6,32,1024]{2,1,0:T(8,128)(2,1)S(1)}, bf16[6,32,1024]{2,1,0:T(8,128)(2,1)S(1)}, u32[]{:S(2)}, u32[]{:S(2)}) %collective-permute-start.1) | collective-permute-done | bytes 393248 | tf_op jit(solution)/shard_map/ppermute | solution.py:277
  35.5 5.6 %collective-permute-done.6 = bf16[6,32,1024]{2,1,0:T(8,128)(2,1)S(1)} collective-permute-done((bf16[6,32,1024]{2,1,0:T(8,128)(2,1)S(1)}, bf16[6,32,1024]{2,1,0:T(8,128)(2,1)S(1)}, u32[]{:S(2)}, u32[]{:S(2)}) %collective-permute-start.6) | collective-permute-done | bytes 393248 | tf_op jit(solution)/shard_map/ppermute | solution.py:277
  41.8 2.7 %collective-permute-start.10 = (bf16[6,32,1024]{2,1,0:T(8,128)(2,1)S(1)}, bf16[6,32,1024]{2,1,0:T(8,128)(2,1)S(1)}, u32[]{:S(2)}, u32[]{:S(2)}) collective-permute-start(bf16[6,32,1024]{2,1,0:T(8,128)(2,1)S(1)} %add_convert_fusion.4), channel_id=1, source_target_pairs={{0,16},{2,18},{4,20},{6,22},{8,24},{10,26},{12,28},{14,30},{16,0},... | collective-permute-start | bytes 1179656 | tf_op jit(solution)/shard_map/ppermute | solution.py:284
  44.5 5.6 %collective-permute-done.8 = bf16[6,32,1024]{2,1,0:T(8,128)(2,1)S(1)} collective-permute-done((bf16[6,32,1024]{2,1,0:T(8,128)(2,1)S(1)}, bf16[6,32,1024]{2,1,0:T(8,128)(2,1)S(1)}, u32[]{:S(2)}, u32[]{:S(2)}) %collective-permute-start.8) | collective-permute-done | bytes 393248 | tf_op jit(solution)/shard_map/ppermute | solution.py:280
  54.1 2.4 %collective-permute-done.5 = bf16[6,32,1024]{2,1,0:T(8,128)(2,1)S(1)} collective-permute-done((bf16[6,32,1024]{2,1,0:T(8,128)(2,1)}, bf16[6,32,1024]{2,1,0:T(8,128)(2,1)S(1)}, u32[]{:S(2)}, u32[]{:S(2)}) %collective-permute-start.5) | collective-permute-done | bytes 393248 | tf_op jit(solution)/shard_map/ppermute | solution.py:280
  58.9 3.6 %collective-permute-start.14 = (bf16[6,32,1024]{2,1,0:T(8,128)(2,1)}, bf16[6,32,1024]{2,1,0:T(8,128)(2,1)}, u32[]{:S(2)}, u32[]{:S(2)}) collective-permute-start(bf16[6,32,1024]{2,1,0:T(8,128)(2,1)} %add_convert_fusion.2), channel_id=1, source_target_pairs={{0,24},{2,26},{4,28},{6,30},{8,0},{10,2},{12,4},{14,6},{16,8},{18,... | collective-permute-start | bytes 1179656 | tf_op jit(solution)/shard_map/ppermute | solution.py:284
  63.9 8.4 %all-gather.5.cloned.1.call-done = bf16[24,32,1024]{2,1,0:T(8,128)(2,1)} async-done(((bf16[6,32,1024]{2,1,0:T(8,128)(2,1)}), bf16[24,32,1024]{2,1,0:T(8,128)(2,1)}) %all-gather.5.cloned.1.call-update) | async-done | bytes 1572880 | tf_op jit(solution)/shard_map/all_gather | solution.py:306
  73.7 2.0 collective-permute-start.18
  78.5 4.8 %collective-permute-done.14 = bf16[6,32,1024]{2,1,0:T(8,128)(2,1)} collective-permute-done((bf16[6,32,1024]{2,1,0:T(8,128)(2,1)}, bf16[6,32,1024]{2,1,0:T(8,128)(2,1)}, u32[]{:S(2)}, u32[]{:S(2)}) %collective-permute-start.14) | collective-permute-done | bytes 393248 | tf_op jit(solution)/shard_map/ppermute | solution.py:284
  83.3 2.8 %add_convert_fusion = (bf16[6,32,1024]{2,1,0:T(8,128)(2,1)S(1)}, f32[6,32,1024]{2,1,0:T(8,128)}) fusion(bf16[6,32,1024]{2,1,0:T(8,128)(2,1)} %collective-permute-done.14, bf16[6,32,1024]{2,1,0:T(8,128)(2,1)S(1)} %collective-permute-done.10, bf16[6,32,1024]{2,1,0:T(8,128)(2,1)} %collective-permute-done.13, bf16[6,32,1024]{2,1,0:T(8,128)(2,1)} %collective-permute-done.12, ...), kind=kLoop, calls=%fused_computation.2 | loop fusion | flops 3145728 | bytes 4325376 | tf_op jit(solution)/shard_map/convert_element_type | solution.py:33
  86.0 2.3 %collective-permute-start.16 = (bf16[6,32,1024]{2,1,0:T(8,128)(2,1)S(1)}, bf16[6,32,1024]{2,1,0:T(8,128)(2,1)S(1)}, u32[]{:S(2)}, u32[]{:S(2)}) collective-permute-start(bf16[6,32,1024]{2,1,0:T(8,128)(2,1)S(1)} %get-tuple-element.64.refs_0_), channel_id=1, source_target_pairs={{0,8},{2,10},{4,12},{6,14},{8,16},{10,18},{12,20},{14,22},{16,24},... | collective-permute-start | bytes 1179656 | tf_op jit(solution)/shard_map/ppermute | solution.py:284
  91.6 8.3 %collective-permute-done.16.refs_3_ = bf16[6,32,1024]{2,1,0:T(8,128)(2,1)S(1)} collective-permute-done((bf16[6,32,1024]{2,1,0:T(8,128)(2,1)S(1)}, bf16[6,32,1024]{2,1,0:T(8,128)(2,1)S(1)}, u32[]{:S(2)}, u32[]{:S(2)}) %collective-permute-start.16) | collective-permute-done | bytes 393248 | tf_op jit(solution)/shard_map/ppermute | solution.py:284
  101.3 4.2 %collective-permute-done.15.refs_1_ = bf16[6,32,1024]{2,1,0:T(8,128)(2,1)S(1)} collective-permute-done((bf16[6,32,1024]{2,1,0:T(8,128)(2,1)S(1)}, bf16[6,32,1024]{2,1,0:T(8,128)(2,1)S(1)}, u32[]{:S(2)}, u32[]{:S(2)}) %collective-permute-start.15) | collective-permute-done | bytes 393248 | tf_op jit(solution)/shard_map/ppermute | solution.py:284
  106.3 2.3 %collective-permute-start.22 = (bf16[3,32,1024]{2,1,0:T(8,128)(2,1)S(1)}, bf16[3,32,1024]{2,1,0:T(8,128)(2,1)S(1)}, u32[]{:S(2)}, u32[]{:S(2)}) collective-permute-start(bf16[3,32,1024]{2,1,0:T(8,128)(2,1)S(1)} %get-tuple-element.97), channel_id=1, source_target_pairs={{0,2},{2,0},{4,6},{6,4},{8,10},{10,8},{12,14},{14,12},{16,18},{18,... | collective-permute-start | bytes 589832 | tf_op jit(solution)/shard_map/ppermute | solution.py:277
  108.6 2.0 collective-permute-start.24
  110.6 3.7 %collective-permute-done.22 = bf16[3,32,1024]{2,1,0:T(8,128)(2,1)S(1)} collective-permute-done((bf16[3,32,1024]{2,1,0:T(8,128)(2,1)S(1)}, bf16[3,32,1024]{2,1,0:T(8,128)(2,1)S(1)}, u32[]{:S(2)}, u32[]{:S(2)}) %collective-permute-start.22) | collective-permute-done | bytes 196640 | tf_op jit(solution)/shard_map/ppermute | solution.py:277
  114.3 2.0 collective-permute-start.29
  117.3 8.7 %collective-permute-done.19.refs_2_ = bf16[6,32,1024]{2,1,0:T(8,128)(2,1)} collective-permute-done((bf16[6,32,1024]{2,1,0:T(8,128)(2,1)S(1)}, bf16[6,32,1024]{2,1,0:T(8,128)(2,1)}, u32[]{:S(2)}, u32[]{:S(2)}) %collective-permute-start.19) | collective-permute-done | bytes 393248 | tf_op jit(solution)/shard_map/ppermute | solution.py:284
  127.4 2.8 %collective-permute-start.27 = (bf16[6,32,1024]{2,1,0:T(8,128)(2,1)}, bf16[6,32,1024]{2,1,0:T(8,128)(2,1)}, u32[]{:S(2)}, u32[]{:S(2)}) collective-permute-start(bf16[6,32,1024]{2,1,0:T(8,128)(2,1)} %collective-permute-done.19.refs_2_), channel_id=1, source_target_pairs={{0,2},{2,0},{4,6},{6,4},{8,10},{10,8},{12,14},{14,12},{16,18},{18,... | collective-permute-start | bytes 1179656 | tf_op jit(solution)/shard_map/ppermute | solution.py:277
  131.7 2.3 %collective-permute-start.32 = (bf16[6,32,1024]{2,1,0:T(8,128)(2,1)}, bf16[6,32,1024]{2,1,0:T(8,128)(2,1)}, u32[]{:S(2)}, u32[]{:S(2)}) collective-permute-start(bf16[6,32,1024]{2,1,0:T(8,128)(2,1)} %collective-permute-done.28.refs_11_), channel_id=1, source_target_pairs={{0,4},{2,6},{4,0},{6,2},{8,12},{10,14},{12,8},{14,10},{16,20},{18,... | collective-permute-start | bytes 1179656 | tf_op jit(solution)/shard_map/ppermute | solution.py:280
  134.0 4.1 %collective-permute-done.21.refs_5_ = bf16[6,32,1024]{2,1,0:T(8,128)(2,1)} collective-permute-done((bf16[6,32,1024]{2,1,0:T(8,128)(2,1)S(1)}, bf16[6,32,1024]{2,1,0:T(8,128)(2,1)}, u32[]{:S(2)}, u32[]{:S(2)}) %collective-permute-start.21) | collective-permute-done | bytes 393248 | tf_op jit(solution)/shard_map/ppermute | solution.py:280
  138.1 2.2 %collective-permute-start.30 = (bf16[6,32,1024]{2,1,0:T(8,128)(2,1)}, bf16[6,32,1024]{2,1,0:T(8,128)(2,1)}, u32[]{:S(2)}, u32[]{:S(2)}) collective-permute-start(bf16[6,32,1024]{2,1,0:T(8,128)(2,1)} %collective-permute-done.21.refs_5_), channel_id=1, source_target_pairs={{0,2},{2,0},{4,6},{6,4},{8,10},{10,8},{12,14},{14,12},{16,18},{18,... | collective-permute-start | bytes 1179656 | tf_op jit(solution)/shard_map/ppermute | solution.py:277
  143.0 5.9 %collective-permute-done.26.refs_9_ = bf16[6,32,1024]{2,1,0:T(8,128)(2,1)} collective-permute-done((bf16[6,32,1024]{2,1,0:T(8,128)(2,1)S(1)}, bf16[6,32,1024]{2,1,0:T(8,128)(2,1)}, u32[]{:S(2)}, u32[]{:S(2)}) %collective-permute-start.26) | collective-permute-done | bytes 393248 | tf_op jit(solution)/shard_map/ppermute | solution.py:277
  148.9 7.5 %collective-permute-done.30.refs_13_ = bf16[6,32,1024]{2,1,0:T(8,128)(2,1)} collective-permute-done((bf16[6,32,1024]{2,1,0:T(8,128)(2,1)}, bf16[6,32,1024]{2,1,0:T(8,128)(2,1)}, u32[]{:S(2)}, u32[]{:S(2)}) %collective-permute-start.30) | collective-permute-done | bytes 393248 | tf_op jit(solution)/shard_map/ppermute | solution.py:277
  156.4 6.1 %collective-permute-done.31.refs_14_ = bf16[6,32,1024]{2,1,0:T(8,128)(2,1)} collective-permute-done((bf16[6,32,1024]{2,1,0:T(8,128)(2,1)}, bf16[6,32,1024]{2,1,0:T(8,128)(2,1)}, u32[]{:S(2)}, u32[]{:S(2)}) %collective-permute-start.31) | collective-permute-done | bytes 393248 | tf_op jit(solution)/shard_map/ppermute | solution.py:280
  162.5 6.1 %shard_map.84 = (bf16[3,512,1024]{2,1,0:T(8,128)(2,1)}, bf16[3,512,512]{2,1,0:T(8,128)(2,1)}) custom-call(s32[3]{0:T(128)} %get-tuple-element.98.order_ref, bf16[6,32,1024]{2,1,0:T(8,128)(2,1)} %copy-done.5, bf16[6,32,1024]{2,1,0:T(8,128)(2,1)} %copy-done.9, bf16[6,32,1024]{2,1,0:T(8,128)(2,1)} %collective-permute-done.19.refs_2_, ...), custom_call_target="tpu_custom_call" | custom-call | flops 1610612736 | bytes 7864320 | tf_op jit(solution)/shard_map/pallas_call | solution.py:58
  168.7 2.5 %collective-permute-start.34 = (bf16[4,3,32,1024]{3,2,1,0:T(8,128)(2,1)S(1)}, bf16[4,3,32,1024]{3,2,1,0:T(8,128)(2,1)S(1)}, u32[]{:S(2)}, u32[]{:S(2)}) collective-permute-start(bf16[4,3,32,1024]{3,2,1,0:T(8,128)(2,1)S(1)} %slice.28), channel_id=1, source_target_pairs={{0,2},{2,0},{4,6},{6,4},{8,10},{10,8},{12,14},{14,12},{16,18},{18,... | collective-permute-start | bytes 2359304 | tf_op jit(solution)/shard_map/ppermute | solution.py:277
  171.2 5.9 %shard_map.83 = (bf16[3,512,1024]{2,1,0:T(8,128)(2,1)}, bf16[3,512,512]{2,1,0:T(8,128)(2,1)}) custom-call(s32[3]{0:T(128)} %get-tuple-element.99.order_ref, bf16[6,32,1024]{2,1,0:T(8,128)(2,1)} %copy-done.5, bf16[6,32,1024]{2,1,0:T(8,128)(2,1)} %copy-done.9, bf16[6,32,1024]{2,1,0:T(8,128)(2,1)} %collective-permute-done.19.refs_2_, ...), custom_call_target="tpu_custom_call" | custom-call | flops 1610612736 | bytes 7864320 | tf_op jit(solution)/shard_map/pallas_call | solution.py:58
  178.5 9.2 %shard_map.85 = (bf16[3,512,512]{2,1,0:T(8,128)(2,1)S(1)}, f32[3,8,128]{2,1,0:T(8,128)S(1)}) custom-call(bf16[3,512,512]{2,1,0:T(8,128)(2,1)S(1)} %copy-done.2, bf16[3,512,512]{2,1,0:T(8,128)(2,1)S(1)} %collective-permute-done.33.refs_1_), custom_call_target="tpu_custom_call" | custom-call | flops 7247757312 | bytes 4718592 | tf_op jit(solution)/shard_map/pallas_call | solution.py:133
  194.1 14.3 %shard_map.86 = (bf16[6,512,1024]{2,1,0:T(8,128)(2,1)}, f32[6,32,1024]{2,1,0:T(8,128)}, bf16[2,512,1024]{2,1,0:T(8,128)(2,1)}, f32[1,2]{1,0:T(1,128)}) custom-call(s32[16]{0:T(128)} %stack.125.places_ref, s32[16]{0:T(128)} %stack.142.spans_ref, s32[6]{0:T(128)} %broadcast_select_fusion.slots_ref, s32[6]{0:T(128)} %copy-done.16, ...), custom_call_target="tpu_custom_call" | custom-call | flops 3221225472 | bytes 28311552 | tf_op jit(solution)/shard_map/pallas_call | solution.py:228
  (114 shorter events, 46.6 us)
Async XLA Ops:
  7.2 65.2 %all-gather.5.cloned.1.call-start = ((), (), s32[]{:S(2)}) async-start(), calls=%async_computation | async-start | bytes 1966080 | tf_op jit(solution)/shard_map/all_gather | solution.py:306
  8.4 14.7 %collective-permute-start.3 = (bf16[6,32,1024]{2,1,0:T(8,128)(2,1)S(1)}, bf16[6,32,1024]{2,1,0:T(8,128)(2,1)S(1)}, u32[]{:S(2)}, u32[]{:S(2)}) collective-permute-start(bf16[6,32,1024]{2,1,0:T(8,128)(2,1)S(1)} %get-tuple-element.94), channel_id=1, source_target_pairs={{0,4},{2,6},{4,0},{6,2},{8,12},{10,14},{12,8},{14,10},{16,20},{18,... | collective-permute-start | bytes 1179656 | tf_op jit(solution)/shard_map/ppermute | solution.py:280
  14.9 177.9 %all-gather.7.cloned.1.call-start = ((), (), s32[]{:S(2)}) async-start(), calls=%async_computation.1 | async-start | bytes 3932160 | tf_op jit(solution)/shard_map/all_gather | solution.py:320
  20.6 12.1 %collective-permute-start.1 = (bf16[6,32,1024]{2,1,0:T(8,128)(2,1)S(1)}, bf16[6,32,1024]{2,1,0:T(8,128)(2,1)S(1)}, u32[]{:S(2)}, u32[]{:S(2)}) collective-permute-start(bf16[6,32,1024]{2,1,0:T(8,128)(2,1)S(1)} %get-tuple-element.83), channel_id=1, source_target_pairs={{0,2},{2,0},{4,6},{6,4},{8,10},{10,8},{12,14},{14,12},{16,18},{18,... | collective-permute-start | bytes 1179656 | tf_op jit(solution)/shard_map/ppermute | solution.py:277
  21.2 20.4 %collective-permute-start.9 = (bf16[6,32,1024]{2,1,0:T(8,128)(2,1)S(1)}, bf16[6,32,1024]{2,1,0:T(8,128)(2,1)S(1)}, u32[]{:S(2)}, u32[]{:S(2)}) collective-permute-start(bf16[6,32,1024]{2,1,0:T(8,128)(2,1)S(1)} %get-tuple-element.93), channel_id=1, source_target_pairs={{0,4},{2,6},{4,0},{6,2},{8,12},{10,14},{12,8},{14,10},{16,20},{18,... | collective-permute-start | bytes 1179656 | tf_op jit(solution)/shard_map/ppermute | solution.py:280
  23.3 26.7 %collective-permute-start.8 = (bf16[6,32,1024]{2,1,0:T(8,128)(2,1)S(1)}, bf16[6,32,1024]{2,1,0:T(8,128)(2,1)S(1)}, u32[]{:S(2)}, u32[]{:S(2)}) collective-permute-start(bf16[6,32,1024]{2,1,0:T(8,128)(2,1)S(1)} %add_convert_fusion.6), channel_id=1, source_target_pairs={{0,4},{2,6},{4,0},{6,2},{8,12},{10,14},{12,8},{14,10},{16,20},{18,... | collective-permute-start | bytes 1179656 | tf_op jit(solution)/shard_map/ppermute | solution.py:280
  23.6 17.5 %collective-permute-start.6 = (bf16[6,32,1024]{2,1,0:T(8,128)(2,1)S(1)}, bf16[6,32,1024]{2,1,0:T(8,128)(2,1)S(1)}, u32[]{:S(2)}, u32[]{:S(2)}) collective-permute-start(bf16[6,32,1024]{2,1,0:T(8,128)(2,1)S(1)} %add_convert_fusion.7), channel_id=1, source_target_pairs={{0,2},{2,0},{4,6},{6,4},{8,10},{10,8},{12,14},{14,12},{16,18},{18,... | collective-permute-start | bytes 1179656 | tf_op jit(solution)/shard_map/ppermute | solution.py:277
  33.3 16.7 %collective-permute-start.4 = (bf16[6,32,1024]{2,1,0:T(8,128)(2,1)S(1)}, bf16[6,32,1024]{2,1,0:T(8,128)(2,1)S(1)}, u32[]{:S(2)}, u32[]{:S(2)}) collective-permute-start(bf16[6,32,1024]{2,1,0:T(8,128)(2,1)S(1)} %add_convert_fusion.5), channel_id=1, source_target_pairs={{0,2},{2,0},{4,6},{6,4},{8,10},{10,8},{12,14},{14,12},{16,18},{18,... | collective-permute-start | bytes 1179656 | tf_op jit(solution)/shard_map/ppermute | solution.py:277
  34.9 21.5 %collective-permute-start.5 = (bf16[6,32,1024]{2,1,0:T(8,128)(2,1)}, bf16[6,32,1024]{2,1,0:T(8,128)(2,1)S(1)}, u32[]{:S(2)}, u32[]{:S(2)}) collective-permute-start(bf16[6,32,1024]{2,1,0:T(8,128)(2,1)} %dynamic-slice_bitcast_fusion.13), channel_id=1, source_target_pairs={{0,4},{2,6},{4,0},{6,2},{8,12},{10,14},{12,8},{14,10},{16,20},{18,... | collective-permute-start | bytes 1179656 | tf_op jit(solution)/shard_map/ppermute | solution.py:280
  41.1 16.9 %collective-permute-start.7 = (bf16[6,32,1024]{2,1,0:T(8,128)(2,1)S(1)}, bf16[6,32,1024]{2,1,0:T(8,128)(2,1)S(1)}, u32[]{:S(2)}, u32[]{:S(2)}) collective-permute-start(bf16[6,32,1024]{2,1,0:T(8,128)(2,1)S(1)} %get-tuple-element.53), channel_id=1, source_target_pairs={{0,2},{2,0},{4,6},{6,4},{8,10},{10,8},{12,14},{14,12},{16,18},{18,... | collective-permute-start | bytes 1179656 | tf_op jit(solution)/shard_map/ppermute | solution.py:277
  41.8 35.2 %collective-permute-start.10 = (bf16[6,32,1024]{2,1,0:T(8,128)(2,1)S(1)}, bf16[6,32,1024]{2,1,0:T(8,128)(2,1)S(1)}, u32[]{:S(2)}, u32[]{:S(2)}) collective-permute-start(bf16[6,32,1024]{2,1,0:T(8,128)(2,1)S(1)} %add_convert_fusion.4), channel_id=1, source_target_pairs={{0,16},{2,18},{4,20},{6,22},{8,24},{10,26},{12,28},{14,30},{16,0},... | collective-permute-start | bytes 1179656 | tf_op jit(solution)/shard_map/ppermute | solution.py:284
  51.0 27.5 %collective-permute-start.13 = (bf16[6,32,1024]{2,1,0:T(8,128)(2,1)}, bf16[6,32,1024]{2,1,0:T(8,128)(2,1)}, u32[]{:S(2)}, u32[]{:S(2)}) collective-permute-start(bf16[6,32,1024]{2,1,0:T(8,128)(2,1)} %add_convert_fusion.3), channel_id=1, source_target_pairs={{0,8},{2,10},{4,12},{6,14},{8,16},{10,18},{12,20},{14,22},{16,24},... | collective-permute-start | bytes 1179656 | tf_op jit(solution)/shard_map/ppermute | solution.py:284
  52.6 21.1 %collective-permute-start.11 = (bf16[6,32,1024]{2,1,0:T(8,128)(2,1)}, bf16[6,32,1024]{2,1,0:T(8,128)(2,1)}, u32[]{:S(2)}, u32[]{:S(2)}) collective-permute-start(bf16[6,32,1024]{2,1,0:T(8,128)(2,1)} %get-tuple-element.62), channel_id=1, source_target_pairs={{0,2},{2,0},{4,6},{6,4},{8,10},{10,8},{12,14},{14,12},{16,18},{18,... | collective-permute-start | bytes 1179656 | tf_op jit(solution)/shard_map/ppermute | solution.py:277
  58.9 24.4 %collective-permute-start.14 = (bf16[6,32,1024]{2,1,0:T(8,128)(2,1)}, bf16[6,32,1024]{2,1,0:T(8,128)(2,1)}, u32[]{:S(2)}, u32[]{:S(2)}) collective-permute-start(bf16[6,32,1024]{2,1,0:T(8,128)(2,1)} %add_convert_fusion.2), channel_id=1, source_target_pairs={{0,24},{2,26},{4,28},{6,30},{8,0},{10,2},{12,4},{14,6},{16,8},{18,... | collective-permute-start | bytes 1179656 | tf_op jit(solution)/shard_map/ppermute | solution.py:284
  63.4 19.9 %collective-permute-start.12 = (bf16[6,32,1024]{2,1,0:T(8,128)(2,1)}, bf16[6,32,1024]{2,1,0:T(8,128)(2,1)}, u32[]{:S(2)}, u32[]{:S(2)}) collective-permute-start(bf16[6,32,1024]{2,1,0:T(8,128)(2,1)} %add_convert_fusion.1), channel_id=1, source_target_pairs={{0,4},{2,6},{4,0},{6,2},{8,12},{10,14},{12,8},{14,10},{16,20},{18,... | collective-permute-start | bytes 1179656 | tf_op jit(solution)/shard_map/ppermute | solution.py:280
  73.7 31.9 %collective-permute-start.18 = (bf16[5,3,32,1024]{3,2,1,0:T(8,128)(2,1)S(1)}, bf16[5,3,32,1024]{3,2,1,0:T(8,128)(2,1)S(1)}, u32[]{:S(2)}, u32[]{:S(2)}) collective-permute-start(bf16[5,3,32,1024]{3,2,1,0:T(8,128)(2,1)S(1)} %pad_maximum_fusion), channel_id=1, source_target_pairs={{0,4},{2,6},{4,0},{6,2},{8,12},{10,14},{12,8},{14,10},{16,20},{18,... | collective-permute-start | bytes 2949128 | tf_op jit(solution)/shard_map/ppermute | solution.py:280
  77.0 28.6 %collective-permute-start.17 = (bf16[5,3,32,1024]{3,2,1,0:T(8,128)(2,1)S(1)}, bf16[5,3,32,1024]{3,2,1,0:T(8,128)(2,1)S(1)}, u32[]{:S(2)}, u32[]{:S(2)}) collective-permute-start(bf16[5,3,32,1024]{3,2,1,0:T(8,128)(2,1)S(1)} %pad_maximum_fusion), channel_id=1, source_target_pairs={{0,2},{2,0},{4,6},{6,4},{8,10},{10,8},{12,14},{14,12},{16,18},{18,... | collective-permute-start | bytes 2949128 | tf_op jit(solution)/shard_map/ppermute | solution.py:277
  86.0 13.9 %collective-permute-start.16 = (bf16[6,32,1024]{2,1,0:T(8,128)(2,1)S(1)}, bf16[6,32,1024]{2,1,0:T(8,128)(2,1)S(1)}, u32[]{:S(2)}, u32[]{:S(2)}) collective-permute-start(bf16[6,32,1024]{2,1,0:T(8,128)(2,1)S(1)} %get-tuple-element.64.refs_0_), channel_id=1, source_target_pairs={{0,8},{2,10},{4,12},{6,14},{8,16},{10,18},{12,20},{14,22},{16,24},... | collective-permute-start | bytes 1179656 | tf_op jit(solution)/shard_map/ppermute | solution.py:284
  88.3 17.2 %collective-permute-start.15 = (bf16[6,32,1024]{2,1,0:T(8,128)(2,1)S(1)}, bf16[6,32,1024]{2,1,0:T(8,128)(2,1)S(1)}, u32[]{:S(2)}, u32[]{:S(2)}) collective-permute-start(bf16[6,32,1024]{2,1,0:T(8,128)(2,1)S(1)} %get-tuple-element.64.refs_0_), channel_id=1, source_target_pairs={{0,24},{2,26},{4,28},{6,30},{8,0},{10,2},{12,4},{14,6},{16,8},{18,... | collective-permute-start | bytes 1179656 | tf_op jit(solution)/shard_map/ppermute | solution.py:284
  89.9 37.5 %collective-permute-start.25 = (bf16[6,32,1024]{2,1,0:T(8,128)(2,1)S(1)}, bf16[6,32,1024]{2,1,0:T(8,128)(2,1)S(1)}, u32[]{:S(2)}, u32[]{:S(2)}) collective-permute-start(bf16[6,32,1024]{2,1,0:T(8,128)(2,1)S(1)} %get-tuple-element.64.refs_0_), channel_id=1, source_target_pairs={{0,2},{2,0},{4,6},{6,4},{8,10},{10,8},{12,14},{14,12},{16,18},{18,... | collective-permute-start | bytes 1179656 | tf_op jit(solution)/shard_map/ppermute | solution.py:277
  105.6 20.5 %collective-permute-start.19 = (bf16[6,32,1024]{2,1,0:T(8,128)(2,1)S(1)}, bf16[6,32,1024]{2,1,0:T(8,128)(2,1)}, u32[]{:S(2)}, u32[]{:S(2)}) collective-permute-start(bf16[6,32,1024]{2,1,0:T(8,128)(2,1)S(1)} %get-tuple-element.64.refs_0_), channel_id=1, source_target_pairs={{0,16},{2,18},{4,20},{6,22},{8,24},{10,26},{12,28},{14,30},{16,0},... | collective-permute-start | bytes 1179656 | tf_op jit(solution)/shard_map/ppermute | solution.py:284
  108.5 23.2 %collective-permute-start.28 = (bf16[6,32,1024]{2,1,0:T(8,128)(2,1)S(1)}, bf16[6,32,1024]{2,1,0:T(8,128)(2,1)}, u32[]{:S(2)}, u32[]{:S(2)}) collective-permute-start(bf16[6,32,1024]{2,1,0:T(8,128)(2,1)S(1)} %collective-permute-done.16.refs_3_), channel_id=1, source_target_pairs={{0,2},{2,0},{4,6},{6,4},{8,10},{10,8},{12,14},{14,12},{16,18},{18,... | collective-permute-start | bytes 1179656 | tf_op jit(solution)/shard_map/ppermute | solution.py:277
  108.6 31.7 %collective-permute-start.24 = (bf16[6,32,1024]{2,1,0:T(8,128)(2,1)S(1)}, bf16[6,32,1024]{2,1,0:T(8,128)(2,1)}, u32[]{:S(2)}, u32[]{:S(2)}) collective-permute-start(bf16[6,32,1024]{2,1,0:T(8,128)(2,1)S(1)} %collective-permute-done.16.refs_3_), channel_id=1, source_target_pairs={{0,4},{2,6},{4,0},{6,2},{8,12},{10,14},{12,8},{14,10},{16,20},{18,... | collective-permute-start | bytes 1179656 | tf_op jit(solution)/shard_map/ppermute | solution.py:280
  114.3 15.9 %collective-permute-start.29 = (bf16[6,32,1024]{2,1,0:T(8,128)(2,1)S(1)}, bf16[6,32,1024]{2,1,0:T(8,128)(2,1)}, u32[]{:S(2)}, u32[]{:S(2)}) collective-permute-start(bf16[6,32,1024]{2,1,0:T(8,128)(2,1)S(1)} %collective-permute-done.20.refs_4_), channel_id=1, source_target_pairs={{0,2},{2,0},{4,6},{6,4},{8,10},{10,8},{12,14},{14,12},{16,18},{18,... | collective-permute-start | bytes 1179656 | tf_op jit(solution)/shard_map/ppermute | solution.py:277
  126.1 12.1 %collective-permute-start.21 = (bf16[6,32,1024]{2,1,0:T(8,128)(2,1)S(1)}, bf16[6,32,1024]{2,1,0:T(8,128)(2,1)}, u32[]{:S(2)}, u32[]{:S(2)}) collective-permute-start(bf16[6,32,1024]{2,1,0:T(8,128)(2,1)S(1)} %collective-permute-done.15.refs_1_), channel_id=1, source_target_pairs={{0,4},{2,6},{4,0},{6,2},{8,12},{10,14},{12,8},{14,10},{16,20},{18,... | collective-permute-start | bytes 1179656 | tf_op jit(solution)/shard_map/ppermute | solution.py:280
  127.4 14.9 %collective-permute-start.27 = (bf16[6,32,1024]{2,1,0:T(8,128)(2,1)}, bf16[6,32,1024]{2,1,0:T(8,128)(2,1)}, u32[]{:S(2)}, u32[]{:S(2)}) collective-permute-start(bf16[6,32,1024]{2,1,0:T(8,128)(2,1)} %collective-permute-done.19.refs_2_), channel_id=1, source_target_pairs={{0,2},{2,0},{4,6},{6,4},{8,10},{10,8},{12,14},{14,12},{16,18},{18,... | collective-permute-start | bytes 1179656 | tf_op jit(solution)/shard_map/ppermute | solution.py:277
  130.3 18.7 %collective-permute-start.26 = (bf16[6,32,1024]{2,1,0:T(8,128)(2,1)S(1)}, bf16[6,32,1024]{2,1,0:T(8,128)(2,1)}, u32[]{:S(2)}, u32[]{:S(2)}) collective-permute-start(bf16[6,32,1024]{2,1,0:T(8,128)(2,1)S(1)} %collective-permute-done.15.refs_1_), channel_id=1, source_target_pairs={{0,2},{2,0},{4,6},{6,4},{8,10},{10,8},{12,14},{14,12},{16,18},{18,... | collective-permute-start | bytes 1179656 | tf_op jit(solution)/shard_map/ppermute | solution.py:277
  131.7 17.2 %collective-permute-start.32 = (bf16[6,32,1024]{2,1,0:T(8,128)(2,1)}, bf16[6,32,1024]{2,1,0:T(8,128)(2,1)}, u32[]{:S(2)}, u32[]{:S(2)}) collective-permute-start(bf16[6,32,1024]{2,1,0:T(8,128)(2,1)} %collective-permute-done.28.refs_11_), channel_id=1, source_target_pairs={{0,4},{2,6},{4,0},{6,2},{8,12},{10,14},{12,8},{14,10},{16,20},{18,... | collective-permute-start | bytes 1179656 | tf_op jit(solution)/shard_map/ppermute | solution.py:280
  138.1 18.2 %collective-permute-start.30 = (bf16[6,32,1024]{2,1,0:T(8,128)(2,1)}, bf16[6,32,1024]{2,1,0:T(8,128)(2,1)}, u32[]{:S(2)}, u32[]{:S(2)}) collective-permute-start(bf16[6,32,1024]{2,1,0:T(8,128)(2,1)} %collective-permute-done.21.refs_5_), channel_id=1, source_target_pairs={{0,2},{2,0},{4,6},{6,4},{8,10},{10,8},{12,14},{14,12},{16,18},{18,... | collective-permute-start | bytes 1179656 | tf_op jit(solution)/shard_map/ppermute | solution.py:277
  140.3 16.1 %collective-permute-start.23 = (bf16[6,32,1024]{2,1,0:T(8,128)(2,1)}, bf16[6,32,1024]{2,1,0:T(8,128)(2,1)}, u32[]{:S(2)}, u32[]{:S(2)}) collective-permute-start(bf16[6,32,1024]{2,1,0:T(8,128)(2,1)} %collective-permute-done.19.refs_2_), channel_id=1, source_target_pairs={{0,4},{2,6},{4,0},{6,2},{8,12},{10,14},{12,8},{14,10},{16,20},{18,... | collective-permute-start | bytes 1179656 | tf_op jit(solution)/shard_map/ppermute | solution.py:280
  142.3 20.1 %collective-permute-start.31 = (bf16[6,32,1024]{2,1,0:T(8,128)(2,1)}, bf16[6,32,1024]{2,1,0:T(8,128)(2,1)}, u32[]{:S(2)}, u32[]{:S(2)}) collective-permute-start(bf16[6,32,1024]{2,1,0:T(8,128)(2,1)} %collective-permute-done.27.refs_10_), channel_id=1, source_target_pairs={{0,4},{2,6},{4,0},{6,2},{8,12},{10,14},{12,8},{14,10},{16,20},{18,... | collective-permute-start | bytes 1179656 | tf_op jit(solution)/shard_map/ppermute | solution.py:280
  168.7 20.7 %collective-permute-start.34 = (bf16[4,3,32,1024]{3,2,1,0:T(8,128)(2,1)S(1)}, bf16[4,3,32,1024]{3,2,1,0:T(8,128)(2,1)S(1)}, u32[]{:S(2)}, u32[]{:S(2)}) collective-permute-start(bf16[4,3,32,1024]{3,2,1,0:T(8,128)(2,1)S(1)} %slice.28), channel_id=1, source_target_pairs={{0,2},{2,0},{4,6},{6,4},{8,10},{10,8},{12,14},{14,12},{16,18},{18,... | collective-permute-start | bytes 2359304 | tf_op jit(solution)/shard_map/ppermute | solution.py:277
  (25 other events, 516.9 us)
Sparse Core Ops, SparseCore 0:
  15.0 57.2 all-gather.4
  130.4 60.4 all-gather.6

commit v6 on v5

--- a/solution.py
+++ b/solution.py
@@ -346,6 +346,8 @@
         start = place(me, dx, dy, dz) * row_count
         return lax.dynamic_slice_in_dim(terms, start, row_count, axis=1)
 
+    own = after(master_gather.own, grid.me)
+    terms = after(terms, own)
     me = grid.me
     raw_far1, raw_far2 = term(me, 1, 1, 1), term(me, 1, 1, 2)
     me = after(grid.me, raw_far1, raw_far2, master_gather.own)

time: 216 us -> 215 us (level)
  starting transfers between devices: 54 us -> 42.8 us
  waiting for transfers between devices: 88.2 us -> 98.3 us
    ppermute x15, waiting for transfers between devices: 32.9 us -> 44 us  [over_x(): return lax.ppermute(value, 'dp', self.x_pairs)]
    ppermute x15, starting transfers between devices: 24.1 us -> 18.1 us  [over_x(): return lax.ppermute(value, 'dp', self.x_pairs)]
    ppermute x13, starting transfers between devices: 17.4 us -> 12.3 us  [over_y(): return lax.ppermute(value, 'dp', self.y_pairs)]
    all_gather x1, waiting for transfers between devices: 8.45 us -> 4.15 us  [__init__(): self.line = lax.all_gather(self.own, 'dp', axis_index_groups=self.lines)]
  transfers between devices with their start and end apart: 39 -> 39, of which waited for: 19 -> 21; matrix products, arithmetic and copies ran while one was open for 9% -> 9% of each run, Pallas kernels for 10% -> 10%
where the time goes in v6:
time: 215 us; the launch traced here: 214 us
  waiting for transfers between devices  98.3 us (46%)
  starting transfers between devices  42.8 us (20%)
  Pallas kernels  35.5 us (17%)
  between operations  14.4 us (7%)
  local copies, waits for them, and re-layouts  13.3 us (6%)
  other arithmetic  9.81 us (5%)
    ppermute x15, waiting for transfers between devices, over_x(): return lax.ppermute(value, 'dp', self.x_pairs)  44 us
    ppermute x6, waiting for transfers between devices, over_z(): return lax.ppermute(value, 'dp', pairs)  28.4 us
    ppermute x13, waiting for transfers between devices, over_y(): return lax.ppermute(value, 'dp', self.y_pairs)  20.8 us
    ppermute x15, starting transfers between devices, over_x(): return lax.ppermute(value, 'dp', self.x_pairs)  18.1 us
    pallas_call x1, Pallas kernels, applied(): pl.pallas_call(functools.partial(apply_kernel, len(sets), first_count, ma...  14.3 us
    ppermute x6, starting transfers between devices, over_z(): return lax.ppermute(value, 'dp', pairs)  12.3 us
    ppermute x13, starting transfers between devices, over_y(): return lax.ppermute(value, 'dp', self.y_pairs)  12.3 us
    pallas_call x2, Pallas kernels, grams(): pl.pallas_call(gram_kernel, grid_spec=pltpu.PrefetchScalarGridSpec(num_sc...  12 us
  transfers between devices with their start and end apart: 39, of which 21 were waited for; matrix products, arithmetic and copies ran while one was open for 9% of the time, Pallas kernels for 10%

profile of v6, /device:TPU:0, one launch (start us, length us, event | category | flops | bytes accessed | tf_op | source)
XLA Modules:
  0.0 214.1 jit_solution(12431571546425308296)
XLA Ops:
  8.4 3.0 %collective-permute-start.3 = (bf16[6,32,1024]{2,1,0:T(8,128)(2,1)S(1)}, bf16[6,32,1024]{2,1,0:T(8,128)(2,1)S(1)}, u32[]{:S(2)}, u32[]{:S(2)}) collective-permute-start(bf16[6,32,1024]{2,1,0:T(8,128)(2,1)S(1)} %get-tuple-element.94), channel_id=1, source_target_pairs={{0,4},{2,6},{4,0},{6,2},{8,12},{10,14},{12,8},{14,10},{16,20},{18,... | collective-permute-start | bytes 1179656 | tf_op jit(solution)/shard_map/ppermute | solution.py:280
  16.8 3.8 %constant_dynamic-slice_fusion = (bf16[6,32,1024]{2,1,0:T(8,128)(2,1)}, bf16[6,32,1024]{2,1,0:T(8,128)(2,1)S(1)}, bf16[6,32,1024]{2,1,0:T(8,128)(2,1)S(1)}, bf16...) fusion(bf16[6,512,1024]{2,1,0:T(8,128)(2,1)} %bitcast.42, ...), kind=kLoop, calls=%fused_computation.15 | loop fusion | bytes 10223668 | tf_op jit(solution)/shard_map/dynamic_slice | solution.py:347
  23.6 2.0 collective-permute-start.6
  25.6 7.6 %collective-permute-done.1 = bf16[6,32,1024]{2,1,0:T(8,128)(2,1)S(1)} collective-permute-done((bf16[6,32,1024]{2,1,0:T(8,128)(2,1)S(1)}, bf16[6,32,1024]{2,1,0:T(8,128)(2,1)S(1)}, u32[]{:S(2)}, u32[]{:S(2)}) %collective-permute-start.1) | collective-permute-done | bytes 393248 | tf_op jit(solution)/shard_map/ppermute | solution.py:277
  33.2 7.9 %collective-permute-done = bf16[6,32,1024]{2,1,0:T(8,128)(2,1)S(1)} collective-permute-done((bf16[6,32,1024]{2,1,0:T(8,128)(2,1)S(1)}, bf16[6,32,1024]{2,1,0:T(8,128)(2,1)S(1)}, u32[]{:S(2)}, u32[]{:S(2)}) %collective-permute-start) | collective-permute-done | bytes 393248 | tf_op jit(solution)/shard_map/ppermute | solution.py:280
  44.1 2.7 %collective-permute-start.10 = (bf16[6,32,1024]{2,1,0:T(8,128)(2,1)S(1)}, bf16[6,32,1024]{2,1,0:T(8,128)(2,1)S(1)}, u32[]{:S(2)}, u32[]{:S(2)}) collective-permute-start(bf16[6,32,1024]{2,1,0:T(8,128)(2,1)S(1)} %add_convert_fusion.4), channel_id=1, source_target_pairs={{0,16},{2,18},{4,20},{6,22},{8,24},{10,26},{12,28},{14,30},{16,0},... | collective-permute-start | bytes 1179656 | tf_op jit(solution)/shard_map/ppermute | solution.py:284
  46.8 2.7 %collective-permute-done.8 = bf16[6,32,1024]{2,1,0:T(8,128)(2,1)S(1)} collective-permute-done((bf16[6,32,1024]{2,1,0:T(8,128)(2,1)S(1)}, bf16[6,32,1024]{2,1,0:T(8,128)(2,1)S(1)}, u32[]{:S(2)}, u32[]{:S(2)}) %collective-permute-start.8) | collective-permute-done | bytes 393248 | tf_op jit(solution)/shard_map/ppermute | solution.py:280
  49.5 3.8 %collective-permute-done.4 = bf16[6,32,1024]{2,1,0:T(8,128)(2,1)S(1)} collective-permute-done((bf16[6,32,1024]{2,1,0:T(8,128)(2,1)S(1)}, bf16[6,32,1024]{2,1,0:T(8,128)(2,1)S(1)}, u32[]{:S(2)}, u32[]{:S(2)}) %collective-permute-start.4) | collective-permute-done | bytes 393248 | tf_op jit(solution)/shard_map/ppermute | solution.py:277
  56.4 5.2 %collective-permute-done.7 = bf16[6,32,1024]{2,1,0:T(8,128)(2,1)S(1)} collective-permute-done((bf16[6,32,1024]{2,1,0:T(8,128)(2,1)S(1)}, bf16[6,32,1024]{2,1,0:T(8,128)(2,1)S(1)}, u32[]{:S(2)}, u32[]{:S(2)}) %collective-permute-start.7) | collective-permute-done | bytes 393248 | tf_op jit(solution)/shard_map/ppermute | solution.py:277
  62.6 3.6 %collective-permute-start.14 = (bf16[6,32,1024]{2,1,0:T(8,128)(2,1)}, bf16[6,32,1024]{2,1,0:T(8,128)(2,1)}, u32[]{:S(2)}, u32[]{:S(2)}) collective-permute-start(bf16[6,32,1024]{2,1,0:T(8,128)(2,1)} %add_convert_fusion.2), channel_id=1, source_target_pairs={{0,24},{2,26},{4,28},{6,30},{8,0},{10,2},{12,4},{14,6},{16,8},{18,... | collective-permute-start | bytes 1179656 | tf_op jit(solution)/shard_map/ppermute | solution.py:284
  67.6 4.2 %all-gather.5.cloned.1.call-done = bf16[24,32,1024]{2,1,0:T(8,128)(2,1)} async-done(((bf16[6,32,1024]{2,1,0:T(8,128)(2,1)}), bf16[24,32,1024]{2,1,0:T(8,128)(2,1)}) %all-gather.5.cloned.1.call-update) | async-done | bytes 1572880 | tf_op jit(solution)/shard_map/all_gather | solution.py:306
  73.1 4.0 %collective-permute-done.10 = bf16[6,32,1024]{2,1,0:T(8,128)(2,1)S(1)} collective-permute-done((bf16[6,32,1024]{2,1,0:T(8,128)(2,1)S(1)}, bf16[6,32,1024]{2,1,0:T(8,128)(2,1)S(1)}, u32[]{:S(2)}, u32[]{:S(2)}) %collective-permute-start.10) | collective-permute-done | bytes 393248 | tf_op jit(solution)/shard_map/ppermute | solution.py:284
  80.0 3.0 %collective-permute-done.14 = bf16[6,32,1024]{2,1,0:T(8,128)(2,1)} collective-permute-done((bf16[6,32,1024]{2,1,0:T(8,128)(2,1)}, bf16[6,32,1024]{2,1,0:T(8,128)(2,1)}, u32[]{:S(2)}, u32[]{:S(2)}) %collective-permute-start.14) | collective-permute-done | bytes 393248 | tf_op jit(solution)/shard_map/ppermute | solution.py:284
  83.1 2.8 %add_convert_fusion = (bf16[6,32,1024]{2,1,0:T(8,128)(2,1)S(1)}, f32[6,32,1024]{2,1,0:T(8,128)}) fusion(bf16[6,32,1024]{2,1,0:T(8,128)(2,1)} %collective-permute-done.14, bf16[6,32,1024]{2,1,0:T(8,128)(2,1)S(1)} %collective-permute-done.10, bf16[6,32,1024]{2,1,0:T(8,128)(2,1)} %collective-permute-done.13, bf16[6,32,1024]{2,1,0:T(8,128)(2,1)} %collective-permute-done.12, ...), kind=kLoop, calls=%fused_computation.2 | loop fusion | flops 3145728 | bytes 4325376 | tf_op jit(solution)/shard_map/convert_element_type | solution.py:33
  85.8 2.5 %collective-permute-start.16 = (bf16[6,32,1024]{2,1,0:T(8,128)(2,1)S(1)}, bf16[6,32,1024]{2,1,0:T(8,128)(2,1)S(1)}, u32[]{:S(2)}, u32[]{:S(2)}) collective-permute-start(bf16[6,32,1024]{2,1,0:T(8,128)(2,1)S(1)} %get-tuple-element.64.refs_0_), channel_id=1, source_target_pairs={{0,8},{2,10},{4,12},{6,14},{8,16},{10,18},{12,20},{14,22},{16,24},... | collective-permute-start | bytes 1179656 | tf_op jit(solution)/shard_map/ppermute | solution.py:284
  90.5 9.2 %collective-permute-done.16.refs_3_ = bf16[6,32,1024]{2,1,0:T(8,128)(2,1)S(1)} collective-permute-done((bf16[6,32,1024]{2,1,0:T(8,128)(2,1)S(1)}, bf16[6,32,1024]{2,1,0:T(8,128)(2,1)S(1)}, u32[]{:S(2)}, u32[]{:S(2)}) %collective-permute-start.16) | collective-permute-done | bytes 393248 | tf_op jit(solution)/shard_map/ppermute | solution.py:284
  100.3 4.8 %collective-permute-done.15.refs_1_ = bf16[6,32,1024]{2,1,0:T(8,128)(2,1)S(1)} collective-permute-done((bf16[6,32,1024]{2,1,0:T(8,128)(2,1)S(1)}, bf16[6,32,1024]{2,1,0:T(8,128)(2,1)S(1)}, u32[]{:S(2)}, u32[]{:S(2)}) %collective-permute-start.15) | collective-permute-done | bytes 393248 | tf_op jit(solution)/shard_map/ppermute | solution.py:284
  109.6 5.3 %collective-permute-done.22 = bf16[3,32,1024]{2,1,0:T(8,128)(2,1)S(1)} collective-permute-done((bf16[3,32,1024]{2,1,0:T(8,128)(2,1)S(1)}, bf16[3,32,1024]{2,1,0:T(8,128)(2,1)S(1)}, u32[]{:S(2)}, u32[]{:S(2)}) %collective-permute-start.22) | collective-permute-done | bytes 196640 | tf_op jit(solution)/shard_map/ppermute | solution.py:277
  114.9 2.4 %collective-permute-start.29 = (bf16[6,32,1024]{2,1,0:T(8,128)(2,1)S(1)}, bf16[6,32,1024]{2,1,0:T(8,128)(2,1)}, u32[]{:S(2)}, u32[]{:S(2)}) collective-permute-start(bf16[6,32,1024]{2,1,0:T(8,128)(2,1)S(1)} %collective-permute-done.20.refs_4_), channel_id=1, source_target_pairs={{0,2},{2,0},{4,6},{6,4},{8,10},{10,8},{12,14},{14,12},{16,18},{18,... | collective-permute-start | bytes 1179656 | tf_op jit(solution)/shard_map/ppermute | solution.py:277
  118.3 7.3 %collective-permute-done.19.refs_2_ = bf16[6,32,1024]{2,1,0:T(8,128)(2,1)} collective-permute-done((bf16[6,32,1024]{2,1,0:T(8,128)(2,1)S(1)}, bf16[6,32,1024]{2,1,0:T(8,128)(2,1)}, u32[]{:S(2)}, u32[]{:S(2)}) %collective-permute-start.19) | collective-permute-done | bytes 393248 | tf_op jit(solution)/shard_map/ppermute | solution.py:284
  125.6 2.3 %collective-permute-start.27 = (bf16[6,32,1024]{2,1,0:T(8,128)(2,1)}, bf16[6,32,1024]{2,1,0:T(8,128)(2,1)}, u32[]{:S(2)}, u32[]{:S(2)}) collective-permute-start(bf16[6,32,1024]{2,1,0:T(8,128)(2,1)} %collective-permute-done.19.refs_2_), channel_id=1, source_target_pairs={{0,2},{2,0},{4,6},{6,4},{8,10},{10,8},{12,14},{14,12},{16,18},{18,... | collective-permute-start | bytes 1179656 | tf_op jit(solution)/shard_map/ppermute | solution.py:277
  128.0 3.8 %collective-permute-done.29.refs_12_ = bf16[6,32,1024]{2,1,0:T(8,128)(2,1)} collective-permute-done((bf16[6,32,1024]{2,1,0:T(8,128)(2,1)S(1)}, bf16[6,32,1024]{2,1,0:T(8,128)(2,1)}, u32[]{:S(2)}, u32[]{:S(2)}) %collective-permute-start.29) | collective-permute-done | bytes 393248 | tf_op jit(solution)/shard_map/ppermute | solution.py:277
  134.0 3.7 %collective-permute-done.21.refs_5_ = bf16[6,32,1024]{2,1,0:T(8,128)(2,1)} collective-permute-done((bf16[6,32,1024]{2,1,0:T(8,128)(2,1)S(1)}, bf16[6,32,1024]{2,1,0:T(8,128)(2,1)}, u32[]{:S(2)}, u32[]{:S(2)}) %collective-permute-start.21) | collective-permute-done | bytes 393248 | tf_op jit(solution)/shard_map/ppermute | solution.py:280
  138.1 2.0 collective-permute-start.23
  140.8 7.8 %collective-permute-done.26.refs_9_ = bf16[6,32,1024]{2,1,0:T(8,128)(2,1)} collective-permute-done((bf16[6,32,1024]{2,1,0:T(8,128)(2,1)S(1)}, bf16[6,32,1024]{2,1,0:T(8,128)(2,1)}, u32[]{:S(2)}, u32[]{:S(2)}) %collective-permute-start.26) | collective-permute-done | bytes 393248 | tf_op jit(solution)/shard_map/ppermute | solution.py:277
  148.7 7.1 %collective-permute-done.30.refs_13_ = bf16[6,32,1024]{2,1,0:T(8,128)(2,1)} collective-permute-done((bf16[6,32,1024]{2,1,0:T(8,128)(2,1)}, bf16[6,32,1024]{2,1,0:T(8,128)(2,1)}, u32[]{:S(2)}, u32[]{:S(2)}) %collective-permute-start.30) | collective-permute-done | bytes 393248 | tf_op jit(solution)/shard_map/ppermute | solution.py:277
  155.7 6.3 %collective-permute-done.31.refs_14_ = bf16[6,32,1024]{2,1,0:T(8,128)(2,1)} collective-permute-done((bf16[6,32,1024]{2,1,0:T(8,128)(2,1)}, bf16[6,32,1024]{2,1,0:T(8,128)(2,1)}, u32[]{:S(2)}, u32[]{:S(2)}) %collective-permute-start.31) | collective-permute-done | bytes 393248 | tf_op jit(solution)/shard_map/ppermute | solution.py:280
  162.0 6.1 %shard_map.84 = (bf16[3,512,1024]{2,1,0:T(8,128)(2,1)}, bf16[3,512,512]{2,1,0:T(8,128)(2,1)}) custom-call(s32[3]{0:T(128)} %get-tuple-element.98.order_ref, bf16[6,32,1024]{2,1,0:T(8,128)(2,1)} %copy-done.5, bf16[6,32,1024]{2,1,0:T(8,128)(2,1)} %copy-done.9, bf16[6,32,1024]{2,1,0:T(8,128)(2,1)} %collective-permute-done.19.refs_2_, ...), custom_call_target="tpu_custom_call" | custom-call | flops 1610612736 | bytes 7864320 | tf_op jit(solution)/shard_map/pallas_call | solution.py:58
  168.5 5.9 %shard_map.83 = (bf16[3,512,1024]{2,1,0:T(8,128)(2,1)}, bf16[3,512,512]{2,1,0:T(8,128)(2,1)}) custom-call(s32[3]{0:T(128)} %get-tuple-element.99.order_ref, bf16[6,32,1024]{2,1,0:T(8,128)(2,1)} %copy-done.5, bf16[6,32,1024]{2,1,0:T(8,128)(2,1)} %copy-done.9, bf16[6,32,1024]{2,1,0:T(8,128)(2,1)} %collective-permute-done.19.refs_2_, ...), custom_call_target="tpu_custom_call" | custom-call | flops 1610612736 | bytes 7864320 | tf_op jit(solution)/shard_map/pallas_call | solution.py:58
  175.8 9.2 %shard_map.85 = (bf16[3,512,512]{2,1,0:T(8,128)(2,1)S(1)}, f32[3,8,128]{2,1,0:T(8,128)S(1)}) custom-call(bf16[3,512,512]{2,1,0:T(8,128)(2,1)S(1)} %copy-done.2, bf16[3,512,512]{2,1,0:T(8,128)(2,1)S(1)} %collective-permute-done.33.refs_1_), custom_call_target="tpu_custom_call" | custom-call | flops 7247757312 | bytes 4718592 | tf_op jit(solution)/shard_map/pallas_call | solution.py:133
  185.0 3.3 %collective-permute-done.34.refs_10_ = bf16[4,3,32,1024]{3,2,1,0:T(8,128)(2,1)S(1)} collective-permute-done((bf16[4,3,32,1024]{3,2,1,0:T(8,128)(2,1)S(1)}, bf16[4,3,32,1024]{3,2,1,0:T(8,128)(2,1)S(1)}, u32[]{:S(2)}, u32[]{:S(2)}) %collective-permute-start.34) | collective-permute-done | bytes 786464 | tf_op jit(solution)/shard_map/ppermute | solution.py:277
  193.0 14.3 %shard_map.86 = (bf16[6,512,1024]{2,1,0:T(8,128)(2,1)}, f32[6,32,1024]{2,1,0:T(8,128)}, bf16[2,512,1024]{2,1,0:T(8,128)(2,1)}, f32[1,2]{1,0:T(1,128)}) custom-call(s32[16]{0:T(128)} %stack.125.places_ref, s32[16]{0:T(128)} %stack.142.spans_ref, s32[6]{0:T(128)} %broadcast_select_fusion.slots_ref, s32[6]{0:T(128)} %copy-done.16, ...), custom_call_target="tpu_custom_call" | custom-call | flops 3221225472 | bytes 28311552 | tf_op jit(solution)/shard_map/pallas_call | solution.py:228
  (114 shorter events, 39.9 us)
Async XLA Ops:
  7.2 64.6 %all-gather.5.cloned.1.call-start = ((), (), s32[]{:S(2)}) async-start(), calls=%async_computation | async-start | bytes 1966080 | tf_op jit(solution)/shard_map/all_gather | solution.py:306
  8.4 14.7 %collective-permute-start.3 = (bf16[6,32,1024]{2,1,0:T(8,128)(2,1)S(1)}, bf16[6,32,1024]{2,1,0:T(8,128)(2,1)S(1)}, u32[]{:S(2)}, u32[]{:S(2)}) collective-permute-start(bf16[6,32,1024]{2,1,0:T(8,128)(2,1)S(1)} %get-tuple-element.94), channel_id=1, source_target_pairs={{0,4},{2,6},{4,0},{6,2},{8,12},{10,14},{12,8},{14,10},{16,20},{18,... | collective-permute-start | bytes 1179656 | tf_op jit(solution)/shard_map/ppermute | solution.py:280
  14.9 176.8 %all-gather.7.cloned.1.call-start = ((), (), s32[]{:S(2)}) async-start(), calls=%async_computation.1 | async-start | bytes 3932160 | tf_op jit(solution)/shard_map/all_gather | solution.py:320
  20.6 23.3 %collective-permute-start.9 = (bf16[6,32,1024]{2,1,0:T(8,128)(2,1)S(1)}, bf16[6,32,1024]{2,1,0:T(8,128)(2,1)S(1)}, u32[]{:S(2)}, u32[]{:S(2)}) collective-permute-start(bf16[6,32,1024]{2,1,0:T(8,128)(2,1)S(1)} %get-tuple-element.82), channel_id=1, source_target_pairs={{0,4},{2,6},{4,0},{6,2},{8,12},{10,14},{12,8},{14,10},{16,20},{18,... | collective-permute-start | bytes 1179656 | tf_op jit(solution)/shard_map/ppermute | solution.py:280
  21.2 19.9 %collective-permute-start = (bf16[6,32,1024]{2,1,0:T(8,128)(2,1)S(1)}, bf16[6,32,1024]{2,1,0:T(8,128)(2,1)S(1)}, u32[]{:S(2)}, u32[]{:S(2)}) collective-permute-start(bf16[6,32,1024]{2,1,0:T(8,128)(2,1)S(1)} %get-tuple-element.85), channel_id=1, source_target_pairs={{0,4},{2,6},{4,0},{6,2},{8,12},{10,14},{12,8},{14,10},{16,20},{18,... | collective-permute-start | bytes 1179656 | tf_op jit(solution)/shard_map/ppermute | solution.py:280
  23.3 26.2 %collective-permute-start.8 = (bf16[6,32,1024]{2,1,0:T(8,128)(2,1)S(1)}, bf16[6,32,1024]{2,1,0:T(8,128)(2,1)S(1)}, u32[]{:S(2)}, u32[]{:S(2)}) collective-permute-start(bf16[6,32,1024]{2,1,0:T(8,128)(2,1)S(1)} %add_convert_fusion.6), channel_id=1, source_target_pairs={{0,4},{2,6},{4,0},{6,2},{8,12},{10,14},{12,8},{14,10},{16,20},{18,... | collective-permute-start | bytes 1179656 | tf_op jit(solution)/shard_map/ppermute | solution.py:280
  23.6 18.4 %collective-permute-start.6 = (bf16[6,32,1024]{2,1,0:T(8,128)(2,1)S(1)}, bf16[6,32,1024]{2,1,0:T(8,128)(2,1)S(1)}, u32[]{:S(2)}, u32[]{:S(2)}) collective-permute-start(bf16[6,32,1024]{2,1,0:T(8,128)(2,1)S(1)} %add_convert_fusion.7), channel_id=1, source_target_pairs={{0,2},{2,0},{4,6},{6,4},{8,10},{10,8},{12,14},{14,12},{16,18},{18,... | collective-permute-start | bytes 1179656 | tf_op jit(solution)/shard_map/ppermute | solution.py:277
  41.2 12.1 %collective-permute-start.4 = (bf16[6,32,1024]{2,1,0:T(8,128)(2,1)S(1)}, bf16[6,32,1024]{2,1,0:T(8,128)(2,1)S(1)}, u32[]{:S(2)}, u32[]{:S(2)}) collective-permute-start(bf16[6,32,1024]{2,1,0:T(8,128)(2,1)S(1)} %add_convert_fusion.5), channel_id=1, source_target_pairs={{0,2},{2,0},{4,6},{6,4},{8,10},{10,8},{12,14},{14,12},{16,18},{18,... | collective-permute-start | bytes 1179656 | tf_op jit(solution)/shard_map/ppermute | solution.py:277
  41.8 14.6 %collective-permute-start.5 = (bf16[6,32,1024]{2,1,0:T(8,128)(2,1)}, bf16[6,32,1024]{2,1,0:T(8,128)(2,1)S(1)}, u32[]{:S(2)}, u32[]{:S(2)}) collective-permute-start(bf16[6,32,1024]{2,1,0:T(8,128)(2,1)} %constant_dynamic-slice_fusion.13), channel_id=1, source_target_pairs={{0,4},{2,6},{4,0},{6,2},{8,12},{10,14},{12,8},{14,10},{16,20},{18,... | collective-permute-start | bytes 1179656 | tf_op jit(solution)/shard_map/ppermute | solution.py:280
  42.0 19.7 %collective-permute-start.7 = (bf16[6,32,1024]{2,1,0:T(8,128)(2,1)S(1)}, bf16[6,32,1024]{2,1,0:T(8,128)(2,1)S(1)}, u32[]{:S(2)}, u32[]{:S(2)}) collective-permute-start(bf16[6,32,1024]{2,1,0:T(8,128)(2,1)S(1)} %get-tuple-element.53), channel_id=1, source_target_pairs={{0,2},{2,0},{4,6},{6,4},{8,10},{10,8},{12,14},{14,12},{16,18},{18,... | collective-permute-start | bytes 1179656 | tf_op jit(solution)/shard_map/ppermute | solution.py:277
  44.1 33.0 %collective-permute-start.10 = (bf16[6,32,1024]{2,1,0:T(8,128)(2,1)S(1)}, bf16[6,32,1024]{2,1,0:T(8,128)(2,1)S(1)}, u32[]{:S(2)}, u32[]{:S(2)}) collective-permute-start(bf16[6,32,1024]{2,1,0:T(8,128)(2,1)S(1)} %add_convert_fusion.4), channel_id=1, source_target_pairs={{0,16},{2,18},{4,20},{6,22},{8,24},{10,26},{12,28},{14,30},{16,0},... | collective-permute-start | bytes 1179656 | tf_op jit(solution)/shard_map/ppermute | solution.py:284
  54.3 25.7 %collective-permute-start.13 = (bf16[6,32,1024]{2,1,0:T(8,128)(2,1)}, bf16[6,32,1024]{2,1,0:T(8,128)(2,1)}, u32[]{:S(2)}, u32[]{:S(2)}) collective-permute-start(bf16[6,32,1024]{2,1,0:T(8,128)(2,1)} %add_convert_fusion.3), channel_id=1, source_target_pairs={{0,8},{2,10},{4,12},{6,14},{8,16},{10,18},{12,20},{14,22},{16,24},... | collective-permute-start | bytes 1179656 | tf_op jit(solution)/shard_map/ppermute | solution.py:284
  55.9 22.7 %collective-permute-start.11 = (bf16[6,32,1024]{2,1,0:T(8,128)(2,1)}, bf16[6,32,1024]{2,1,0:T(8,128)(2,1)}, u32[]{:S(2)}, u32[]{:S(2)}) collective-permute-start(bf16[6,32,1024]{2,1,0:T(8,128)(2,1)} %get-tuple-element.62), channel_id=1, source_target_pairs={{0,2},{2,0},{4,6},{6,4},{8,10},{10,8},{12,14},{14,12},{16,18},{18,... | collective-permute-start | bytes 1179656 | tf_op jit(solution)/shard_map/ppermute | solution.py:277
  62.6 20.5 %collective-permute-start.14 = (bf16[6,32,1024]{2,1,0:T(8,128)(2,1)}, bf16[6,32,1024]{2,1,0:T(8,128)(2,1)}, u32[]{:S(2)}, u32[]{:S(2)}) collective-permute-start(bf16[6,32,1024]{2,1,0:T(8,128)(2,1)} %add_convert_fusion.2), channel_id=1, source_target_pairs={{0,24},{2,26},{4,28},{6,30},{8,0},{10,2},{12,4},{14,6},{16,8},{18,... | collective-permute-start | bytes 1179656 | tf_op jit(solution)/shard_map/ppermute | solution.py:284
  67.1 16.0 %collective-permute-start.12 = (bf16[6,32,1024]{2,1,0:T(8,128)(2,1)}, bf16[6,32,1024]{2,1,0:T(8,128)(2,1)}, u32[]{:S(2)}, u32[]{:S(2)}) collective-permute-start(bf16[6,32,1024]{2,1,0:T(8,128)(2,1)} %add_convert_fusion.1), channel_id=1, source_target_pairs={{0,4},{2,6},{4,0},{6,2},{8,12},{10,14},{12,8},{14,10},{16,20},{18,... | collective-permute-start | bytes 1179656 | tf_op jit(solution)/shard_map/ppermute | solution.py:280
  77.1 28.0 %collective-permute-start.18 = (bf16[5,3,32,1024]{3,2,1,0:T(8,128)(2,1)S(1)}, bf16[5,3,32,1024]{3,2,1,0:T(8,128)(2,1)S(1)}, u32[]{:S(2)}, u32[]{:S(2)}) collective-permute-start(bf16[5,3,32,1024]{3,2,1,0:T(8,128)(2,1)S(1)} %pad_maximum_fusion), channel_id=1, source_target_pairs={{0,4},{2,6},{4,0},{6,2},{8,12},{10,14},{12,8},{14,10},{16,20},{18,... | collective-permute-start | bytes 2949128 | tf_op jit(solution)/shard_map/ppermute | solution.py:280
  78.6 26.5 %collective-permute-start.17 = (bf16[5,3,32,1024]{3,2,1,0:T(8,128)(2,1)S(1)}, bf16[5,3,32,1024]{3,2,1,0:T(8,128)(2,1)S(1)}, u32[]{:S(2)}, u32[]{:S(2)}) collective-permute-start(bf16[5,3,32,1024]{3,2,1,0:T(8,128)(2,1)S(1)} %pad_maximum_fusion), channel_id=1, source_target_pairs={{0,2},{2,0},{4,6},{6,4},{8,10},{10,8},{12,14},{14,12},{16,18},{18,... | collective-permute-start | bytes 2949128 | tf_op jit(solution)/shard_map/ppermute | solution.py:277
  85.8 13.9 %collective-permute-start.16 = (bf16[6,32,1024]{2,1,0:T(8,128)(2,1)S(1)}, bf16[6,32,1024]{2,1,0:T(8,128)(2,1)S(1)}, u32[]{:S(2)}, u32[]{:S(2)}) collective-permute-start(bf16[6,32,1024]{2,1,0:T(8,128)(2,1)S(1)} %get-tuple-element.64.refs_0_), channel_id=1, source_target_pairs={{0,8},{2,10},{4,12},{6,14},{8,16},{10,18},{12,20},{14,22},{16,24},... | collective-permute-start | bytes 1179656 | tf_op jit(solution)/shard_map/ppermute | solution.py:284
  88.4 16.7 %collective-permute-start.15 = (bf16[6,32,1024]{2,1,0:T(8,128)(2,1)S(1)}, bf16[6,32,1024]{2,1,0:T(8,128)(2,1)S(1)}, u32[]{:S(2)}, u32[]{:S(2)}) collective-permute-start(bf16[6,32,1024]{2,1,0:T(8,128)(2,1)S(1)} %get-tuple-element.64.refs_0_), channel_id=1, source_target_pairs={{0,24},{2,26},{4,28},{6,30},{8,0},{10,2},{12,4},{14,6},{16,8},{18,... | collective-permute-start | bytes 1179656 | tf_op jit(solution)/shard_map/ppermute | solution.py:284
  89.6 36.0 %collective-permute-start.25 = (bf16[6,32,1024]{2,1,0:T(8,128)(2,1)S(1)}, bf16[6,32,1024]{2,1,0:T(8,128)(2,1)S(1)}, u32[]{:S(2)}, u32[]{:S(2)}) collective-permute-start(bf16[6,32,1024]{2,1,0:T(8,128)(2,1)S(1)} %get-tuple-element.64.refs_0_), channel_id=1, source_target_pairs={{0,2},{2,0},{4,6},{6,4},{8,10},{10,8},{12,14},{14,12},{16,18},{18,... | collective-permute-start | bytes 1179656 | tf_op jit(solution)/shard_map/ppermute | solution.py:277
  105.1 20.5 %collective-permute-start.19 = (bf16[6,32,1024]{2,1,0:T(8,128)(2,1)S(1)}, bf16[6,32,1024]{2,1,0:T(8,128)(2,1)}, u32[]{:S(2)}, u32[]{:S(2)}) collective-permute-start(bf16[6,32,1024]{2,1,0:T(8,128)(2,1)S(1)} %get-tuple-element.64.refs_0_), channel_id=1, source_target_pairs={{0,16},{2,18},{4,20},{6,22},{8,24},{10,26},{12,28},{14,30},{16,0},... | collective-permute-start | bytes 1179656 | tf_op jit(solution)/shard_map/ppermute | solution.py:284
  107.3 26.2 %collective-permute-start.28 = (bf16[6,32,1024]{2,1,0:T(8,128)(2,1)S(1)}, bf16[6,32,1024]{2,1,0:T(8,128)(2,1)}, u32[]{:S(2)}, u32[]{:S(2)}) collective-permute-start(bf16[6,32,1024]{2,1,0:T(8,128)(2,1)S(1)} %collective-permute-done.16.refs_3_), channel_id=1, source_target_pairs={{0,2},{2,0},{4,6},{6,4},{8,10},{10,8},{12,14},{14,12},{16,18},{18,... | collective-permute-start | bytes 1179656 | tf_op jit(solution)/shard_map/ppermute | solution.py:277
  108.1 30.0 %collective-permute-start.24 = (bf16[6,32,1024]{2,1,0:T(8,128)(2,1)S(1)}, bf16[6,32,1024]{2,1,0:T(8,128)(2,1)}, u32[]{:S(2)}, u32[]{:S(2)}) collective-permute-start(bf16[6,32,1024]{2,1,0:T(8,128)(2,1)S(1)} %collective-permute-done.16.refs_3_), channel_id=1, source_target_pairs={{0,4},{2,6},{4,0},{6,2},{8,12},{10,14},{12,8},{14,10},{16,20},{18,... | collective-permute-start | bytes 1179656 | tf_op jit(solution)/shard_map/ppermute | solution.py:280
  114.9 17.0 %collective-permute-start.29 = (bf16[6,32,1024]{2,1,0:T(8,128)(2,1)S(1)}, bf16[6,32,1024]{2,1,0:T(8,128)(2,1)}, u32[]{:S(2)}, u32[]{:S(2)}) collective-permute-start(bf16[6,32,1024]{2,1,0:T(8,128)(2,1)S(1)} %collective-permute-done.20.refs_4_), channel_id=1, source_target_pairs={{0,2},{2,0},{4,6},{6,4},{8,10},{10,8},{12,14},{14,12},{16,18},{18,... | collective-permute-start | bytes 1179656 | tf_op jit(solution)/shard_map/ppermute | solution.py:277
  125.6 12.1 %collective-permute-start.21 = (bf16[6,32,1024]{2,1,0:T(8,128)(2,1)S(1)}, bf16[6,32,1024]{2,1,0:T(8,128)(2,1)}, u32[]{:S(2)}, u32[]{:S(2)}) collective-permute-start(bf16[6,32,1024]{2,1,0:T(8,128)(2,1)S(1)} %collective-permute-done.15.refs_1_), channel_id=1, source_target_pairs={{0,4},{2,6},{4,0},{6,2},{8,12},{10,14},{12,8},{14,10},{16,20},{18,... | collective-permute-start | bytes 1179656 | tf_op jit(solution)/shard_map/ppermute | solution.py:280
  125.6 14.6 %collective-permute-start.27 = (bf16[6,32,1024]{2,1,0:T(8,128)(2,1)}, bf16[6,32,1024]{2,1,0:T(8,128)(2,1)}, u32[]{:S(2)}, u32[]{:S(2)}) collective-permute-start(bf16[6,32,1024]{2,1,0:T(8,128)(2,1)} %collective-permute-done.19.refs_2_), channel_id=1, source_target_pairs={{0,2},{2,0},{4,6},{6,4},{8,10},{10,8},{12,14},{14,12},{16,18},{18,... | collective-permute-start | bytes 1179656 | tf_op jit(solution)/shard_map/ppermute | solution.py:277
  131.8 16.9 %collective-permute-start.26 = (bf16[6,32,1024]{2,1,0:T(8,128)(2,1)S(1)}, bf16[6,32,1024]{2,1,0:T(8,128)(2,1)}, u32[]{:S(2)}, u32[]{:S(2)}) collective-permute-start(bf16[6,32,1024]{2,1,0:T(8,128)(2,1)S(1)} %collective-permute-done.15.refs_1_), channel_id=1, source_target_pairs={{0,2},{2,0},{4,6},{6,4},{8,10},{10,8},{12,14},{14,12},{16,18},{18,... | collective-permute-start | bytes 1179656 | tf_op jit(solution)/shard_map/ppermute | solution.py:277
  133.6 15.1 %collective-permute-start.32 = (bf16[6,32,1024]{2,1,0:T(8,128)(2,1)}, bf16[6,32,1024]{2,1,0:T(8,128)(2,1)}, u32[]{:S(2)}, u32[]{:S(2)}) collective-permute-start(bf16[6,32,1024]{2,1,0:T(8,128)(2,1)} %collective-permute-done.28.refs_11_), channel_id=1, source_target_pairs={{0,4},{2,6},{4,0},{6,2},{8,12},{10,14},{12,8},{14,10},{16,20},{18,... | collective-permute-start | bytes 1179656 | tf_op jit(solution)/shard_map/ppermute | solution.py:280
  137.7 18.0 %collective-permute-start.30 = (bf16[6,32,1024]{2,1,0:T(8,128)(2,1)}, bf16[6,32,1024]{2,1,0:T(8,128)(2,1)}, u32[]{:S(2)}, u32[]{:S(2)}) collective-permute-start(bf16[6,32,1024]{2,1,0:T(8,128)(2,1)} %collective-permute-done.21.refs_5_), channel_id=1, source_target_pairs={{0,2},{2,0},{4,6},{6,4},{8,10},{10,8},{12,14},{14,12},{16,18},{18,... | collective-permute-start | bytes 1179656 | tf_op jit(solution)/shard_map/ppermute | solution.py:277
  138.1 17.6 %collective-permute-start.23 = (bf16[6,32,1024]{2,1,0:T(8,128)(2,1)}, bf16[6,32,1024]{2,1,0:T(8,128)(2,1)}, u32[]{:S(2)}, u32[]{:S(2)}) collective-permute-start(bf16[6,32,1024]{2,1,0:T(8,128)(2,1)} %collective-permute-done.19.refs_2_), channel_id=1, source_target_pairs={{0,4},{2,6},{4,0},{6,2},{8,12},{10,14},{12,8},{14,10},{16,20},{18,... | collective-permute-start | bytes 1179656 | tf_op jit(solution)/shard_map/ppermute | solution.py:280
  140.2 21.8 %collective-permute-start.31 = (bf16[6,32,1024]{2,1,0:T(8,128)(2,1)}, bf16[6,32,1024]{2,1,0:T(8,128)(2,1)}, u32[]{:S(2)}, u32[]{:S(2)}) collective-permute-start(bf16[6,32,1024]{2,1,0:T(8,128)(2,1)} %collective-permute-done.27.refs_10_), channel_id=1, source_target_pairs={{0,4},{2,6},{4,0},{6,2},{8,12},{10,14},{12,8},{14,10},{16,20},{18,... | collective-permute-start | bytes 1179656 | tf_op jit(solution)/shard_map/ppermute | solution.py:280
  168.3 20.0 %collective-permute-start.34 = (bf16[4,3,32,1024]{3,2,1,0:T(8,128)(2,1)S(1)}, bf16[4,3,32,1024]{3,2,1,0:T(8,128)(2,1)S(1)}, u32[]{:S(2)}, u32[]{:S(2)}) collective-permute-start(bf16[4,3,32,1024]{3,2,1,0:T(8,128)(2,1)S(1)} %slice.28), channel_id=1, source_target_pairs={{0,2},{2,0},{4,6},{6,4},{8,10},{10,8},{12,14},{14,12},{16,18},{18,... | collective-permute-start | bytes 2359304 | tf_op jit(solution)/shard_map/ppermute | solution.py:277
  (25 other events, 526.1 us)
Sparse Core Ops, SparseCore 0:
  15.0 56.6 all-gather.4
  128.1 61.0 all-gather.6
